TPU v7x, 32 devices: a whole 2x2x4 slice. The times are simulated.
32 devices in a mesh: dp: 8 (over y, x, core), fsdp: 4 (over z).
Axes of the slice: x: 2, y: 2, z: 4, core: 2. Of those that a mesh axis runs over, the one named last changes fastest.
Arguments:
- tokens: bfloat16 [64, 160, 1280], P(('dp', 'fsdp')), may hold values from -6 to 6
- cotangent: bfloat16 [64, 160, 1280], P(('dp', 'fsdp')), may hold values from -15 to 15
- segment_ids: int32 [64, 160], P(('dp', 'fsdp')), may hold values from 0 to 3, never falling along the last dimension, each value on 1 to 80 neighbouring positions
- w_query: float32 [1280, 1024], P(('dp', 'fsdp')), may hold values from -0.15625 to 0.15625
- w_key: float32 [1280, 256], P(('dp', 'fsdp')), may hold values from -0.15625 to 0.15625
- w_value: float32 [1280, 256], P(('dp', 'fsdp')), may hold values from -0.15625 to 0.15625
- w_out: float32 [1024, 1280], P(('dp', 'fsdp')), may hold values from -0.5 to 0.5
- w_gate: float32 [1280, 3072], P(('dp', 'fsdp')), may hold values from -0.15625 to 0.15625
- w_up: float32 [1280, 3072], P(('dp', 'fsdp')), may hold values from -0.15625 to 0.15625
- w_down: float32 [3072, 1280], P(('dp', 'fsdp')), may hold values from -0.109375 to 0.109375
- m_query: float32 [1280, 1024], P(('dp', 'fsdp')), may hold values from -0.00024414062 to 0.00024414062
- m_key: float32 [1280, 256], P(('dp', 'fsdp')), may hold values from -0.00048828125 to 0.00048828125
- m_value: float32 [1280, 256], P(('dp', 'fsdp')), may hold values from -0.00048828125 to 0.00048828125
- m_out: float32 [1024, 1280], P(('dp', 'fsdp')), may hold values from -9.1552734e-05 to 9.1552734e-05
- m_gate: float32 [1280, 3072], P(('dp', 'fsdp')), may hold values from -0.00010681152 to 0.00010681152
- m_up: float32 [1280, 3072], P(('dp', 'fsdp')), may hold values from -0.00010681152 to 0.00010681152
- m_down: float32 [3072, 1280], P(('dp', 'fsdp')), may hold values from -0.00015258789 to 0.00015258789
- v_query: float32 [1280, 1024], P(('dp', 'fsdp')), may hold values from 7.3703874e-09 to 2.9412345e-08
- v_key: float32 [1280, 256], P(('dp', 'fsdp')), may hold values from 2.6298096e-08 to 1.05192385e-07
- v_value: float32 [1280, 256], P(('dp', 'fsdp')), may hold values from 3.287262e-08 to 1.3149048e-07
- v_out: float32 [1024, 1280], P(('dp', 'fsdp')), may hold values from 9.91369e-10 to 3.9620156e-09
- v_gate: float32 [1280, 3072], P(('dp', 'fsdp')), may hold values from 1.179954e-09 to 4.7232764e-09
- v_up: float32 [1280, 3072], P(('dp', 'fsdp')), may hold values from 1.179954e-09 to 4.7232764e-09
- v_down: float32 [3072, 1280], P(('dp', 'fsdp')), may hold values from 3.2699607e-09 to 1.3097144e-08
- gains: float32 [2688], replicated, may hold values from 0.4 to 2.6
- gain_first: float32 [2688], replicated, may hold values from -0.00048828125 to 0.00048828125
- gain_second: float32 [2688], replicated, may hold values from 3.6332896e-08 to 1.4533158e-07
Outputs:
- output: bfloat16 [64, 160, 1280], P(('dp', 'fsdp'))
- input_grad: bfloat16 [64, 160, 1280], P(('dp', 'fsdp'))
- grad_query: float32 [1280, 1024], P(('dp', 'fsdp'))
- grad_key: float32 [1280, 256], P(('dp', 'fsdp'))
- grad_value: float32 [1280, 256], P(('dp', 'fsdp'))
- grad_out: float32 [1024, 1280], P(('dp', 'fsdp'))
- grad_gate: float32 [1280, 3072], P(('dp', 'fsdp'))
- grad_up: float32 [1280, 3072], P(('dp', 'fsdp'))
- grad_down: float32 [3072, 1280], P(('dp', 'fsdp'))
- grad_gains: float32 [2688], replicated
- grad_norm: float32 [], replicated
- new_query: float32 [1280, 1024], P(('dp', 'fsdp'))
- new_key: float32 [1280, 256], P(('dp', 'fsdp'))
- new_value: float32 [1280, 256], P(('dp', 'fsdp'))
- new_out: float32 [1024, 1280], P(('dp', 'fsdp'))
- new_gate: float32 [1280, 3072], P(('dp', 'fsdp'))
- new_up: float32 [1280, 3072], P(('dp', 'fsdp'))
- new_down: float32 [3072, 1280], P(('dp', 'fsdp'))
- new_gains: float32 [2688], replicated
- copy_query: bfloat16 [1280, 1024], P(('dp', 'fsdp'))
- copy_key: bfloat16 [1280, 256], P(('dp', 'fsdp'))
- copy_value: bfloat16 [1280, 256], P(('dp', 'fsdp'))
- copy_out: bfloat16 [1024, 1280], P(('dp', 'fsdp'))
- copy_gate: bfloat16 [1280, 3072], P(('dp', 'fsdp'))
- copy_up: bfloat16 [1280, 3072], P(('dp', 'fsdp'))
- copy_down: bfloat16 [3072, 1280], P(('dp', 'fsdp'))
- second_query: float32 [1280, 1024], P(('dp', 'fsdp'))
- second_key: float32 [1280, 256], P(('dp', 'fsdp'))
- second_value: float32 [1280, 256], P(('dp', 'fsdp'))
- second_out: float32 [1024, 1280], P(('dp', 'fsdp'))
- second_gate: float32 [1280, 3072], P(('dp', 'fsdp'))
- second_up: float32 [1280, 3072], P(('dp', 'fsdp'))
- second_down: float32 [3072, 1280], P(('dp', 'fsdp'))
- second_gains: float32 [2688], replicated
Inputs may be any that keep to these rules, and one draw needn't show every extreme that they name: `segment_ids`: along each row the ids never fall, so that each document is one run of positions.
All inputs are finite; a program needn't handle non-finite values.
Results may differ from a plain program's by a relative error of at most 0.014.
Values may be sent and summed in bfloat16 or wider, within the bound.
A program may use at most 256 MiB of HBM per device.

v0:
```python
import jax
import jax.numpy as jnp
from jax import lax
from jax.sharding import PartitionSpec as P

D = 1280
HQ = 16
KV = 4
HD = 64
STEP = 10


norm_eps = 1e-05
rope_base = 10000.0
beta_one = 0.9
beta_two = 0.95
adam_eps = 1e-08
decay_rate = 0.1
clip_limit = 1.0
gain_rate = 0.4
masked_score = -1e30


def rms_scale(values, gain):
    return values * lax.rsqrt(jnp.mean(values * values, -1, keepdims=True) + norm_eps) * gain


def rotary_tables(length, size):
    half = size // 2
    frequency = rope_base ** (-jnp.arange(half, dtype=jnp.float32) * 2.0 / size)
    angles = jnp.arange(length, dtype=jnp.float32)[:, None] * frequency[None, :]
    return (jnp.cos(angles), jnp.sin(angles))


def rotate(vectors, cosine, sine):
    half = vectors.shape[-1] // 2
    first = vectors[..., :half]
    second = vectors[..., half:]
    cosine = cosine[:, None, :]
    sine = sine[:, None, :]
    return jnp.concatenate([first * cosine - second * sine, second * cosine + first * sine], -1)


def head_norm(raw, gain, cosine, sine):
    size = gain.shape[0]
    shaped = raw.reshape(raw.shape[:-1] + (raw.shape[-1] // size, size))
    return rotate(rms_scale(shaped, gain), cosine, sine)


def swiglu(gate, upper):
    return jax.nn.silu(gate) * upper


def forward_product(left, right):
    return jnp.dot(left, right, preferred_element_type=jnp.float32)


def weight_product(left, right):
    return lax.dot_general(
        left, right, (((0,), (0,)), ((), ())), preferred_element_type=jnp.float32
    )


def back_product(left, right):
    return lax.dot_general(
        left, right, (((1,), (1,)), ((), ())), preferred_element_type=jnp.float32
    )


def adam_update(master, first, second, grad, rate, decay):
    first_new = beta_one * first + (1.0 - beta_one) * grad
    second_new = beta_two * second + (1.0 - beta_two) * grad * grad
    first_hat = first_new / (1.0 - beta_one**STEP)
    second_hat = second_new / (1.0 - beta_two**STEP)
    master_new = master - rate * (first_hat / (jnp.sqrt(second_hat) + adam_eps) + decay * master)
    return (master_new, second_new)


def add_terms(held, fresh):
    if held is None:
        return fresh
    return tuple((left + right for left, right in zip(held, fresh)))


def shards(
    tokens,
    cotangent,
    segment_ids,
    w_query,
    w_key,
    w_value,
    w_out,
    w_gate,
    w_up,
    w_down,
    m_query,
    m_key,
    m_value,
    m_out,
    m_gate,
    m_up,
    m_down,
    v_query,
    v_key,
    v_value,
    v_out,
    v_gate,
    v_up,
    v_down,
    gains,
    gain_first,
    gain_second,
):
    masters = (w_query, w_key, w_value, w_out, w_gate, w_up, w_down)
    firsts = (m_query, m_key, m_value, m_out, m_gate, m_up, m_down)
    seconds = (v_query, v_key, v_value, v_out, v_gate, v_up, v_down)
    rounded = tuple((weight.astype(jnp.bfloat16) for weight in masters))
    length = tokens.shape[1]
    cosine, sine = rotary_tables(length, HD)
    scale = HD ** (-0.5)
    group_size = HQ // KV
    gain_attn = gains[:D]
    gain_ffn = gains[D : 2 * D]
    gain_query = gains[2 * D : 2 * D + HD]
    gain_key = gains[2 * D + HD :]
    positions = jnp.arange(length)
    causal = positions[None, :] <= positions[:, None]
    last_micro = tokens.shape[0] - 1

    def query_piece(raw, gain):
        return head_norm(raw, gain, cosine, sine)

    outputs = []
    input_grads = []
    down_held = None
    inner_held = None
    attention_held = None
    gain_accum = jnp.zeros(gains.shape, jnp.float32)
    for micro in range(tokens.shape[0]):
        inputs = tokens[micro].astype(jnp.float32)
        back_in = cotangent[micro]
        row_ids = segment_ids[micro]
        allowed = causal & (row_ids[:, None] == row_ids[None, :])
        query_w, key_w, value_w, out_w = (
            lax.all_gather(rounded[0], ("dp", "fsdp"), axis=0, tiled=True),
            lax.all_gather(rounded[1], ("dp", "fsdp"), axis=0, tiled=True),
            lax.all_gather(rounded[2], ("dp", "fsdp"), axis=0, tiled=True),
            lax.all_gather(rounded[3], ("dp", "fsdp"), axis=0, tiled=True),
        )
        normed = rms_scale(inputs, gain_attn).astype(jnp.bfloat16)
        query_raw = forward_product(normed, query_w)
        key_raw = forward_product(normed, key_w)
        values = forward_product(normed, value_w).astype(jnp.bfloat16).reshape(length, KV, HD)
        queries = (
            query_piece(query_raw, gain_query)
            .astype(jnp.bfloat16)
            .reshape(length, KV, group_size, HD)
        )
        keys = query_piece(key_raw, gain_key).astype(jnp.bfloat16)
        scores = (
            jnp.einsum("lkrd,mkd->krlm", queries, keys, preferred_element_type=jnp.float32) * scale
        )
        scores = jnp.where(allowed, scores, masked_score)
        top = jnp.max(scores, -1, keepdims=True)
        log_total = top + jnp.log(jnp.sum(jnp.exp(scores - top), -1, keepdims=True))
        attention = jnp.exp(scores - log_total).astype(jnp.bfloat16)
        mixed = jnp.einsum("krlm,mkd->lkrd", attention, values, preferred_element_type=jnp.float32)
        mixed = mixed.reshape(length, HQ * HD).astype(jnp.bfloat16)
        hidden_in = inputs + forward_product(mixed, out_w)
        gate_w, up_w = (
            lax.all_gather(rounded[4], ("dp", "fsdp"), axis=0, tiled=True),
            lax.all_gather(rounded[5], ("dp", "fsdp"), axis=0, tiled=True),
        )
        ffn_in = rms_scale(hidden_in, gain_ffn).astype(jnp.bfloat16)
        gate = forward_product(ffn_in, gate_w)
        upper = forward_product(ffn_in, up_w)
        hidden = swiglu(gate, upper).astype(jnp.bfloat16)
        down_w = lax.all_gather(rounded[6], ("dp", "fsdp"), axis=0, tiled=True)
        outputs.append((hidden_in + forward_product(hidden, down_w)).astype(jnp.bfloat16))
        down_w = lax.all_gather(rounded[6], ("dp", "fsdp"), axis=0, tiled=True)
        grad_down_w = weight_product(hidden, back_in)
        down_held = grad_down_w if down_held is None else down_held + grad_down_w
        if micro == last_micro:
            down_held = lax.psum_scatter(down_held, ("dp", "fsdp"), scatter_dimension=0, tiled=True)
        grad_hidden = back_product(back_in, down_w)
        swiglu_out, swiglu_pull = jax.vjp(swiglu, gate, upper)
        grad_gate, grad_upper = swiglu_pull(grad_hidden)
        grad_gate = grad_gate.astype(jnp.bfloat16)
        grad_upper = grad_upper.astype(jnp.bfloat16)
        gate_w, up_w = (
            lax.all_gather(rounded[4], ("dp", "fsdp"), axis=0, tiled=True),
            lax.all_gather(rounded[5], ("dp", "fsdp"), axis=0, tiled=True),
        )
        inner_terms = (weight_product(ffn_in, grad_gate), weight_product(ffn_in, grad_upper))
        inner_held = add_terms(inner_held, inner_terms)
        if micro == last_micro:
            inner_held = (
                lax.psum_scatter(inner_held[0], ("dp", "fsdp"), scatter_dimension=0, tiled=True),
                lax.psum_scatter(inner_held[1], ("dp", "fsdp"), scatter_dimension=0, tiled=True),
            )
        grad_ffn_in = back_product(grad_gate, gate_w) + back_product(grad_upper, up_w)
        ffn_out, ffn_pull = jax.vjp(rms_scale, hidden_in, gain_ffn)
        grad_hidden_in, grad_gain_ffn = ffn_pull(grad_ffn_in)
        grad_hidden_in = grad_hidden_in + back_in.astype(jnp.float32)
        grad_branch = grad_hidden_in.astype(jnp.bfloat16)
        query_w, key_w, value_w, out_w = (
            lax.all_gather(rounded[0], ("dp", "fsdp"), axis=0, tiled=True),
            lax.all_gather(rounded[1], ("dp", "fsdp"), axis=0, tiled=True),
            lax.all_gather(rounded[2], ("dp", "fsdp"), axis=0, tiled=True),
            lax.all_gather(rounded[3], ("dp", "fsdp"), axis=0, tiled=True),
        )
        grad_out_w = weight_product(mixed, grad_branch)
        grad_mixed = (
            back_product(grad_branch, out_w)
            .astype(jnp.bfloat16)
            .reshape(length, KV, group_size, HD)
        )
        scores = (
            jnp.einsum("lkrd,mkd->krlm", queries, keys, preferred_element_type=jnp.float32) * scale
        )
        scores = jnp.where(allowed, scores, masked_score)
        attention_full = jnp.exp(scores - log_total)
        attention = attention_full.astype(jnp.bfloat16)
        grad_attention = jnp.einsum(
            "lkrd,mkd->krlm", grad_mixed, values, preferred_element_type=jnp.float32
        )
        grad_scores = attention_full * (
            grad_attention - jnp.sum(attention_full * grad_attention, -1, keepdims=True)
        )
        grad_scores = grad_scores.astype(jnp.bfloat16)
        grad_values = jnp.einsum(
            "krlm,lkrd->mkd", attention, grad_mixed, preferred_element_type=jnp.float32
        )
        grad_values = grad_values.reshape(length, KV * HD).astype(jnp.bfloat16)
        grad_queries = (
            jnp.einsum("krlm,mkd->lkrd", grad_scores, keys, preferred_element_type=jnp.float32)
            * scale
        )
        grad_keys = (
            jnp.einsum("krlm,lkrd->mkd", grad_scores, queries, preferred_element_type=jnp.float32)
            * scale
        )
        query_out, query_pull = jax.vjp(query_piece, query_raw, gain_query)
        grad_query_raw, grad_gain_query = query_pull(grad_queries.reshape(length, HQ, HD))
        key_out, key_pull = jax.vjp(query_piece, key_raw, gain_key)
        grad_key_raw, grad_gain_key = key_pull(grad_keys)
        grad_query_raw = grad_query_raw.astype(jnp.bfloat16)
        grad_key_raw = grad_key_raw.astype(jnp.bfloat16)
        attention_terms = (
            weight_product(normed, grad_query_raw),
            weight_product(normed, grad_key_raw),
            weight_product(normed, grad_values),
            grad_out_w,
        )
        attention_held = add_terms(attention_held, attention_terms)
        if micro == last_micro:
            attention_held = (
                lax.psum_scatter(
                    attention_held[0], ("dp", "fsdp"), scatter_dimension=0, tiled=True
                ),
                lax.psum_scatter(
                    attention_held[1], ("dp", "fsdp"), scatter_dimension=0, tiled=True
                ),
                lax.psum_scatter(
                    attention_held[2], ("dp", "fsdp"), scatter_dimension=0, tiled=True
                ),
                lax.psum_scatter(
                    attention_held[3], ("dp", "fsdp"), scatter_dimension=0, tiled=True
                ),
            )
        grad_normed = (
            back_product(grad_query_raw, query_w)
            + back_product(grad_key_raw, key_w)
            + back_product(grad_values, value_w)
        )
        attn_out, attn_pull = jax.vjp(rms_scale, inputs, gain_attn)
        grad_inputs, grad_gain_attn = attn_pull(grad_normed)
        input_grads.append((grad_inputs + grad_hidden_in).astype(jnp.bfloat16))
        gain_accum = gain_accum + jnp.concatenate(
            [grad_gain_attn, grad_gain_ffn, grad_gain_query, grad_gain_key]
        )
    reduced = attention_held + inner_held + (down_held,)
    local_squares = sum((jnp.sum(share * share) for share in reduced))
    gain_total = lax.psum(gain_accum, ("dp", "fsdp"))
    square_total = lax.psum(local_squares, ("dp", "fsdp"))
    total_norm = jnp.sqrt(square_total + jnp.sum(gain_total * gain_total))
    factor = jnp.minimum(1.0, clip_limit / (total_norm + 1e-06))
    clipped = tuple((share * factor for share in reduced))
    gain_clipped = gain_total * factor
    weight_rate = 2.0 * D ** (-0.5)
    updates = [
        adam_update(
            masters[index], firsts[index], seconds[index], clipped[index], weight_rate, decay_rate
        )
        for index in range(7)
    ]
    new_masters = tuple((item[0] for item in updates))
    new_seconds = tuple((item[1] for item in updates))
    new_gains, gain_seconds = adam_update(
        gains, gain_first, gain_second, gain_clipped, gain_rate, 0.0
    )
    copies = tuple((item.astype(jnp.bfloat16) for item in new_masters))
    return (
        (jnp.stack(outputs), jnp.stack(input_grads))
        + clipped
        + (gain_clipped, total_norm)
        + new_masters
        + (new_gains,)
        + copies
        + new_seconds
        + (gain_seconds,)
    )


def solution(mesh):
    placed = (
        P(("dp", "fsdp"), None, None),
        P(("dp", "fsdp"), None, None),
        P(("dp", "fsdp"), None),
        P(("dp", "fsdp"), None),
        P(("dp", "fsdp"), None),
        P(("dp", "fsdp"), None),
        P(("dp", "fsdp"), None),
        P(("dp", "fsdp"), None),
        P(("dp", "fsdp"), None),
        P(("dp", "fsdp"), None),
        P(("dp", "fsdp"), None),
        P(("dp", "fsdp"), None),
        P(("dp", "fsdp"), None),
        P(("dp", "fsdp"), None),
        P(("dp", "fsdp"), None),
        P(("dp", "fsdp"), None),
        P(("dp", "fsdp"), None),
        P(("dp", "fsdp"), None),
        P(("dp", "fsdp"), None),
        P(("dp", "fsdp"), None),
        P(("dp", "fsdp"), None),
        P(("dp", "fsdp"), None),
        P(("dp", "fsdp"), None),
        P(("dp", "fsdp"), None),
        P(),
        P(),
        P(),
    )
    return jax.shard_map(
        shards,
        mesh=mesh,
        in_specs=placed,
        out_specs=(
            P(("dp", "fsdp"), None, None),
            P(("dp", "fsdp"), None, None),
            P(("dp", "fsdp"), None),
            P(("dp", "fsdp"), None),
            P(("dp", "fsdp"), None),
            P(("dp", "fsdp"), None),
            P(("dp", "fsdp"), None),
            P(("dp", "fsdp"), None),
            P(("dp", "fsdp"), None),
            P(),
            P(),
            P(("dp", "fsdp"), None),
            P(("dp", "fsdp"), None),
            P(("dp", "fsdp"), None),
            P(("dp", "fsdp"), None),
            P(("dp", "fsdp"), None),
            P(("dp", "fsdp"), None),
            P(("dp", "fsdp"), None),
            P(),
            P(("dp", "fsdp"), None),
            P(("dp", "fsdp"), None),
            P(("dp", "fsdp"), None),
            P(("dp", "fsdp"), None),
            P(("dp", "fsdp"), None),
            P(("dp", "fsdp"), None),
            P(("dp", "fsdp"), None),
            P(("dp", "fsdp"), None),
            P(("dp", "fsdp"), None),
            P(("dp", "fsdp"), None),
            P(("dp", "fsdp"), None),
            P(("dp", "fsdp"), None),
            P(("dp", "fsdp"), None),
            P(("dp", "fsdp"), None),
            P(),
        ),
        check_vma=False,
    )
```

profile of v0, /device:TPU:0, one launch (start us, length us, event | category | flops | bytes accessed | tf_op | source)
XLA Modules:
  0.0 1595.6 jit_solution(17871187641825608928)
XLA Ops:
  15.2 77.9 %all_gather.15 = bf16[1280,256]{1,0:T(8,128)(2,1)S(1)} all-gather(bf16[40,256]{1,0:T(8,128)(2,1)S(1)} %convert_element_type.248), channel_id=1, replica_groups=mesh['dp'=8,'fsdp'=4] {'dp','fsdp'}, dimensions={0}, use_global_device_ids=true | all-gather | bytes 675840 | tf_op jit(solution)/shard_map/all_gather | solution.py:146
  93.6 71.1 %all_gather.14 = bf16[1280,256]{1,0:T(8,128)(2,1)S(1)} all-gather(bf16[40,256]{1,0:T(8,128)(2,1)S(1)} %convert_element_type.243), channel_id=1, replica_groups=mesh['dp'=8,'fsdp'=4] {'dp','fsdp'}, dimensions={0}, use_global_device_ids=true | all-gather | bytes 675840 | tf_op jit(solution)/shard_map/all_gather | solution.py:147
  171.0 3.2 copy.81
  188.5 25.3 %all-gather.10.cloned.1.call-done = bf16[1280,3072]{1,0:T(8,128)(2,1)} async-done(((bf16[40,3072]{1,0:T(8,128)(2,1)}), bf16[1280,3072]{1,0:T(8,128)(2,1)}) %all-gather.10.cloned.1.call-update) | async-done | bytes 7864336 | tf_op jit(solution)/shard_map/all_gather | solution.py:171
  213.8 5.9 fusion.163
  219.7 71.3 %all-gather.12.cloned.1.call-done = bf16[1280,3072]{1,0:T(8,128)(2,1)} async-done(((bf16[40,3072]{1,0:T(8,128)(2,1)}), bf16[1280,3072]{1,0:T(8,128)(2,1)}) %all-gather.12.cloned.1.call-update) | async-done | bytes 7864336 | tf_op jit(solution)/shard_map/all_gather | solution.py:172
  291.0 6.0 fusion.164
  297.0 71.2 %all-gather.14.cloned.1.call-done = bf16[3072,1280]{1,0:T(8,128)(2,1)} async-done(((bf16[96,1280]{1,0:T(8,128)(2,1)}), bf16[3072,1280]{1,0:T(8,128)(2,1)}) %all-gather.14.cloned.1.call-update) | async-done | bytes 7864336 | tf_op jit(solution)/shard_map/all_gather | solution.py:178
  368.3 8.3 multiply_convert_fusion.1
  376.5 7.1 fusion.167
  383.8 4.4 multiply_reduce_fusion.7
  388.1 2.8 fusion.166
  393.7 6.9 multiply_convert_fusion
  400.5 4.1 fusion.169
  404.7 3.6 multiply_reduce_fusion.6
  414.5 3.8 fusion
  428.3 3.2 fusion.2
  445.6 3.3 convolution_add_fusion.4
  451.3 3.1 convolution_add_fusion.3
  458.0 7.7 convolution_add_fusion.2
  465.9 3.5 fusion.172
  469.4 7.7 convolution_add_fusion.1
  480.8 7.9 convolution_add_fusion
  500.6 4.8 fusion.9
  507.1 56.0 %reduce-scatter.12.cloned.1.call-done = f32[40,256]{1,0:T(8,128)} async-done(((f32[1280,256]{1,0:T(8,128)}), f32[40,256]{1,0:T(8,128)}) %reduce-scatter.12.cloned.1.call-update) | async-done | bytes 40976 | tf_op jit(solution)/shard_map/reduce_scatter | solution.py:264
  564.5 133.9 %reduce-scatter.10.cloned.1.call-done = f32[40,256]{1,0:T(8,128)} async-done(((f32[1280,256]{1,0:T(8,128)}), f32[40,256]{1,0:T(8,128)}) %reduce-scatter.10.cloned.1.call-update) | async-done | bytes 40976 | tf_op jit(solution)/shard_map/reduce_scatter | solution.py:261
  699.8 152.1 %reduce-scatter.8.cloned.1.call-done = f32[40,1024]{1,0:T(8,128)} async-done(((f32[1280,1024]{1,0:T(8,128)}), f32[40,1024]{1,0:T(8,128)}) %reduce-scatter.8.cloned.1.call-update) | async-done | bytes 163856 | tf_op jit(solution)/shard_map/reduce_scatter | solution.py:258
  855.4 151.7 %reduce-scatter.14.cloned.1.call-done = f32[32,1280]{1,0:T(8,128)} async-done(((f32[1024,1280]{1,0:T(8,128)}), f32[32,1280]{1,0:T(8,128)}) %reduce-scatter.14.cloned.1.call-update) | async-done | bytes 163856 | tf_op jit(solution)/shard_map/reduce_scatter | solution.py:267
  1009.3 172.9 %reduce-scatter.16.cloned.1.call-done = f32[40,3072]{1,0:T(8,128)} async-done(((f32[1280,3072]{1,0:T(8,128)}), f32[40,3072]{1,0:T(8,128)}) %reduce-scatter.16.cloned.1.call-update) | async-done | bytes 491536 | tf_op jit(solution)/shard_map/reduce_scatter | solution.py:198
  1184.6 173.4 %reduce-scatter.18.cloned.1.call-done = f32[40,3072]{1,0:T(8,128)} async-done(((f32[1280,3072]{1,0:T(8,128)}), f32[40,3072]{1,0:T(8,128)}) %reduce-scatter.18.cloned.1.call-update) | async-done | bytes 491536 | tf_op jit(solution)/shard_map/reduce_scatter | solution.py:199
  1360.5 173.2 %reduce-scatter.20.cloned.1.call-done = f32[96,1280]{1,0:T(8,128)} async-done(((f32[3072,1280]{1,0:T(8,128)}), f32[96,1280]{1,0:T(8,128)}) %reduce-scatter.20.cloned.1.call-update) | async-done | bytes 491536 | tf_op jit(solution)/shard_map/reduce_scatter | solution.py:184
  1537.1 40.1 %all-reduce.8 = (f32[]{:T(128)}, f32[2688]{0:T(1024)S(1)}) all-reduce(f32[]{:T(128)S(6)} %add.400, f32[2688]{0:T(1024)S(1)} %add.401), channel_id=1, replica_groups=mesh['dp'=8,'fsdp'=4] {'dp','fsdp'}, use_global_device_ids=true, to_apply=%region_36.37 | all-reduce | flops 2689 | bytes 21512 | tf_op jit(solution)/shard_map/psum | solution.py:285
  (474 shorter events, 104.2 us)
Async XLA Ops:
  7.2 163.7 %all-gather.6.cloned.1.call-start = ((), (), s32[]{:S(2)}) async-start(), calls=%async_computation.7 | async-start | bytes 2703360 | tf_op jit(solution)/shard_map/all_gather | solution.py:145
  8.9 84.4 %copy-start.110 = (f32[40,256]{1,0:T(8,128)S(1)}, f32[40,256]{1,0:T(8,128)}, u32[]{:S(2)}) copy-start(f32[40,256]{1,0:T(8,128)} %param.32) | copy-start | bytes 122884
  8.9 171.9 %all-gather.8.cloned.1.call-start = ((), (), s32[]{:S(2)}) async-start(), calls=%async_computation.8 | async-start | bytes 2703360 | tf_op jit(solution)/shard_map/all_gather | solution.py:148
  10.5 82.8 %copy-start.8 = (bf16[2,160,1280]{2,1,0:T(8,128)(2,1)S(1)}, bf16[2,160,1280]{2,1,0:T(8,128)(2,1)}, u32[]{:S(2)}) copy-start(bf16[2,160,1280]{2,1,0:T(8,128)(2,1)} %param.27) | copy-start | bytes 2457604
  10.6 203.2 %all-gather.10.cloned.1.call-start = ((), (), s32[]{:S(2)}) async-start(), calls=%async_computation.9 | async-start | bytes 8110080 | tf_op jit(solution)/shard_map/all_gather | solution.py:171
  12.4 81.2 %copy-start.120 = (f32[2688]{0:T(1024)S(1)}, f32[2688]{0:T(1024)}, u32[]{:S(2)}) copy-start(f32[2688]{0:T(1024)} %param.51) | copy-start | bytes 32260
  12.5 278.6 %all-gather.12.cloned.1.call-start = ((), (), s32[]{:S(2)}) async-start(), calls=%async_computation.10 | async-start | bytes 8110080 | tf_op jit(solution)/shard_map/all_gather | solution.py:172
  14.3 354.0 %all-gather.14.cloned.1.call-start = ((), (), s32[]{:S(2)}) async-start(), calls=%async_computation.11 | async-start | bytes 8110080 | tf_op jit(solution)/shard_map/all_gather | solution.py:178
  15.1 548.0 %reduce-scatter.12.cloned.1.call-start = ((), (), s32[]{:S(2)}) async-start(), calls=%async_computation.14 | async-start | bytes 1351680 | tf_op jit(solution)/shard_map/reduce_scatter | solution.py:264
  93.0 73.1 %copy-start.33 = (bf16[1280,256]{1,0:T(8,128)(2,1)}, bf16[1280,256]{1,0:T(8,128)(2,1)S(1)}, u32[]{:S(2)}) copy-start(bf16[1280,256]{1,0:T(8,128)(2,1)S(1)} %all_gather.15) | copy-start | bytes 1966084
  93.3 73.6 %copy-start.161 = (s32[2,160]{1,0:T(2,128)S(1)}, s32[2,160]{1,0:T(2,128)}, u32[]{:S(2)}) copy-start(s32[2,160]{1,0:T(2,128)} %param.29) | copy-start | bytes 3844
  93.6 71.1 %copy-start.153 = (f32[160]{0:T(256)}, f32[160]{0:T(256)S(1)}, u32[]{:S(2)}) copy-start(f32[160]{0:T(256)S(1)} %get-tuple-element.48) | copy-start | bytes 1924
  93.6 74.3 %copy-start.155 = (f32[160]{0:T(256)}, f32[160]{0:T(256)S(1)}, u32[]{:S(2)}) copy-start(f32[160]{0:T(256)S(1)} %get-tuple-element.49) | copy-start | bytes 1924
  93.6 74.3 %copy-start.136 = (f32[160]{0:T(256)}, f32[160]{0:T(256)S(1)}, u32[]{:S(2)}) copy-start(f32[160]{0:T(256)S(1)} %fusion.123) | copy-start | bytes 1924
  183.5 200.2 %copy-start.16 = (f32[160,1280]{1,0:T(8,128)}, f32[160,1280]{1,0:T(8,128)S(1)}, u32[]{:S(2)}) copy-start(f32[160,1280]{1,0:T(8,128)S(1)} %get-tuple-element.155) | copy-start | bytes 2457604
  183.5 200.2 %copy-start.149 = (f32[160]{0:T(256)}, f32[160]{0:T(256)S(1)}, u32[]{:S(2)}) copy-start(f32[160]{0:T(256)S(1)} %fusion.124) | copy-start | bytes 1924
  188.3 195.4 %copy-start.13 = (f32[160,1280]{1,0:T(8,128)}, f32[160,1280]{1,0:T(8,128)S(1)}, u32[]{:S(2)}) copy-start(f32[160,1280]{1,0:T(8,128)S(1)} %get-tuple-element.157) | copy-start | bytes 2457604
  188.3 216.3 %copy-start.144 = (f32[160]{0:T(256)}, f32[160]{0:T(256)S(1)}, u32[]{:S(2)}) copy-start(f32[160]{0:T(256)S(1)} %fusion.126) | copy-start | bytes 1924
  188.5 102.6 %copy-start.19 = (bf16[160,1280]{1,0:T(8,128)(2,1)}, bf16[160,1280]{1,0:T(8,128)(2,1)S(1)}, u32[]{:S(2)}) copy-start(bf16[160,1280]{1,0:T(8,128)(2,1)S(1)} %multiply_convert_fusion.5) | copy-start | bytes 1228804
  219.7 148.5 %copy-start.56 = (bf16[2,160,1280]{2,1,0:T(8,128)(2,1)S(1)}, bf16[2,160,1280]{2,1,0:T(8,128)(2,1)}, u32[]{:S(2)}) copy-start(bf16[2,160,1280]{2,1,0:T(8,128)(2,1)} %param.28) | copy-start | bytes 2457604
  428.3 270.1 %reduce-scatter.10.cloned.1.call-start = ((), (), s32[]{:S(2)}) async-start(), calls=%async_computation.13 | async-start | bytes 1351680 | tf_op jit(solution)/shard_map/reduce_scatter | solution.py:261
  438.7 413.1 %reduce-scatter.8.cloned.1.call-start = ((), (), s32[]{:S(2)}) async-start(), calls=%async_computation.12 | async-start | bytes 5406720 | tf_op jit(solution)/shard_map/reduce_scatter | solution.py:258
  449.0 558.1 %reduce-scatter.14.cloned.1.call-start = ((), (), s32[]{:S(2)}) async-start(), calls=%async_computation.15 | async-start | bytes 5406720 | tf_op jit(solution)/shard_map/reduce_scatter | solution.py:267
  454.5 727.7 %reduce-scatter.16.cloned.1.call-start = ((), (), s32[]{:S(2)}) async-start(), calls=%async_computation.16 | async-start | bytes 16220160 | tf_op jit(solution)/shard_map/reduce_scatter | solution.py:198
  465.8 892.2 %reduce-scatter.18.cloned.1.call-start = ((), (), s32[]{:S(2)}) async-start(), calls=%async_computation.17 | async-start | bytes 16220160 | tf_op jit(solution)/shard_map/reduce_scatter | solution.py:199
  477.1 1056.6 %reduce-scatter.20.cloned.1.call-start = ((), (), s32[]{:S(2)}) async-start(), calls=%async_computation.18 | async-start | bytes 16220160 | tf_op jit(solution)/shard_map/reduce_scatter | solution.py:184
  507.0 1072.2 %copy-start.121 = (f32[2688]{0:T(1024)S(1)}, f32[2688]{0:T(1024)}, u32[]{:S(2)}) copy-start(f32[2688]{0:T(1024)} %param.51) | copy-start | bytes 32260
  507.0 1072.2 %copy-start.151 = (f32[2688]{0:T(1024)S(1)}, f32[2688]{0:T(1024)}, u32[]{:S(2)}) copy-start(f32[2688]{0:T(1024)} %param.52) | copy-start | bytes 32260
  507.0 1072.2 %copy-start.152 = (f32[2688]{0:T(1024)S(1)}, f32[2688]{0:T(1024)}, u32[]{:S(2)}) copy-start(f32[2688]{0:T(1024)} %param.53) | copy-start | bytes 32260
  507.0 1072.8 %copy-start.68 = (f32[96,1280]{1,0:T(8,128)S(1)}, f32[96,1280]{1,0:T(8,128)}, u32[]{:S(2)}) copy-start(f32[96,1280]{1,0:T(8,128)} %param.36) | copy-start | bytes 1474564
  507.1 1072.8 %copy-start.96 = (f32[96,1280]{1,0:T(8,128)S(1)}, f32[96,1280]{1,0:T(8,128)}, u32[]{:S(2)}) copy-start(f32[96,1280]{1,0:T(8,128)} %param.43) | copy-start | bytes 1474564
  507.1 1072.8 %copy-start.97 = (f32[96,1280]{1,0:T(8,128)S(1)}, f32[96,1280]{1,0:T(8,128)}, u32[]{:S(2)}) copy-start(f32[96,1280]{1,0:T(8,128)} %param.50) | copy-start | bytes 1474564
  (148 other events, 762.6 us)
Sparse Core Ops, SparseCore 0:
  11.5 61.1 all-gather.5
  76.1 58.4 all-gather.7
  137.9 75.8 all-gather.9
  217.0 73.9 all-gather.11
  294.3 73.9 all-gather.13
  428.4 134.6 reduce-scatter.11
  565.4 132.9 reduce-scatter.9
  700.7 151.1 reduce-scatter.7
  854.2 152.8 reduce-scatter.13
  1012.9 169.2 reduce-scatter.15
  1188.2 169.7 reduce-scatter.17
  1363.9 169.7 reduce-scatter.19
where the time goes:
time: 1600 us
  waiting for transfers between devices  1180 us (74%)
  blocking collectives  189 us (12%)
  matrix products  131 us (8%)
  other arithmetic  43 us (3%)
  local copies, waits for them, and re-layouts  26.1 us (2%)
  between operations  23.9 us (1%)
    reduce_scatter x1, waiting for transfers between devices, shards(): lax.psum_scatter(inner_held[1], ('dp', 'fsdp'), scatter_dimension=0, tile...  173 us
    reduce_scatter x1, waiting for transfers between devices, shards(): lax.psum_scatter(down_held, ('dp', 'fsdp'), scatter_dimension=0, tiled=True)  173 us
    reduce_scatter x1, waiting for transfers between devices, shards(): lax.psum_scatter(inner_held[0], ('dp', 'fsdp'), scatter_dimension=0, tile...  173 us
    reduce_scatter x1, waiting for transfers between devices, shards(): lax.psum_scatter(attention_held[0], ('dp', 'fsdp'), scatter_dimension=0,...  152 us
    reduce_scatter x1, waiting for transfers between devices, shards(): lax.psum_scatter(attention_held[3], ('dp', 'fsdp'), scatter_dimension=0,...  152 us
    reduce_scatter x1, waiting for transfers between devices, shards(): lax.psum_scatter(attention_held[1], ('dp', 'fsdp'), scatter_dimension=0,...  134 us
    all_gather x1, blocking collectives, shards(): lax.all_gather(rounded[1], ('dp', 'fsdp'), axis=0, tiled=True)  77.9 us
    all_gather x1, waiting for transfers between devices, shards(): lax.all_gather(rounded[5], ('dp', 'fsdp'), axis=0, tiled=True)  71.3 us
  transfers between devices with their start and end apart: 12, of which 10 were waited for; matrix products, arithmetic and copies ran while one was open for 7% of the time, Pallas kernels for 0%

commit v1 on v0

v1 whole, which is shorter than its diff:
```python
import functools

import jax
import jax.numpy as jnp
from jax import lax
from jax.sharding import PartitionSpec as P

D = 1280
HQ = 16
KV = 4
HD = 64
STEP = 10
MEMBERS = 4

norm_eps = 1e-05
rope_base = 10000.0
beta_one = 0.9
beta_two = 0.95
adam_eps = 1e-08
decay_rate = 0.1
clip_limit = 1.0
gain_rate = 0.4
masked_score = -1e30

AXES = ("dp", "fsdp")


def rms_scale(values, gain):
    return values * lax.rsqrt(jnp.mean(values * values, -1, keepdims=True) + norm_eps) * gain


def rotary_tables(length, size):
    half = size // 2
    frequency = rope_base ** (-jnp.arange(half, dtype=jnp.float32) * 2.0 / size)
    angles = jnp.arange(length, dtype=jnp.float32)[:, None] * frequency[None, :]
    return (jnp.cos(angles), jnp.sin(angles))


def rotate(vectors, cosine, sine):
    half = vectors.shape[-1] // 2
    first = vectors[..., :half]
    second = vectors[..., half:]
    cosine = cosine[:, None, :]
    sine = sine[:, None, :]
    return jnp.concatenate([first * cosine - second * sine, second * cosine + first * sine], -1)


def head_norm(raw, gain, cosine, sine):
    size = gain.shape[0]
    shaped = raw.reshape(raw.shape[:-1] + (raw.shape[-1] // size, size))
    return rotate(rms_scale(shaped, gain), cosine, sine)


def swiglu(gate, upper):
    return jax.nn.silu(gate) * upper


def forward_product(left, right):
    return jnp.dot(left, right, preferred_element_type=jnp.float32)


def weight_product(left, right):
    return lax.dot_general(
        left, right, (((0,), (0,)), ((), ())), preferred_element_type=jnp.float32
    )


def back_product(left, right):
    return lax.dot_general(
        left, right, (((1,), (1,)), ((), ())), preferred_element_type=jnp.float32
    )


def adam_update(master, first, second, grad, rate, decay):
    first_new = beta_one * first + (1.0 - beta_one) * grad
    second_new = beta_two * second + (1.0 - beta_two) * grad * grad
    first_hat = first_new / (1.0 - beta_one**STEP)
    second_hat = second_new / (1.0 - beta_two**STEP)
    master_new = master - rate * (first_hat / (jnp.sqrt(second_hat) + adam_eps) + decay * master)
    return (master_new, second_new)


def put(buffer, block, axis, index):
    return lax.dynamic_update_index_in_dim(buffer, block, index, axis)


def pick(array, axis, index):
    return lax.dynamic_index_in_dim(array, index, axis, keepdims=False)


class Ring:
    def __init__(self, extent, place, target, nd, nf):
        self.extent = extent
        self.place = place
        self.target = target
        self.nd = nd
        self.nf = nf

    def move(self, block, step):
        pairs = []
        for d in range(self.nd):
            for f in range(self.nf):
                d2, f2 = self.target(d, f, step)
                pairs.append((d * self.nf + f, d2 * self.nf + f2))
        return lax.ppermute(block, AXES, pairs)

    def source(self, step):
        return lax.rem(self.place - step + self.extent, self.extent)

    def dest(self, step):
        return lax.rem(self.place + step, self.extent)

    def gather(self, block, axis):
        shape = block.shape[:axis] + (self.extent,) + block.shape[axis:]
        full = put(jnp.zeros(shape, block.dtype), block, axis, self.place)
        for step in range(1, self.extent):
            full = put(full, self.move(block, step), axis, self.source(step))
        return full

    def reduce(self, terms, axis):
        total = pick(terms, axis, self.place).astype(jnp.float32)
        for step in range(1, self.extent):
            got = self.move(pick(terms, axis, self.dest(step)), step)
            total = total + got.astype(jnp.float32)
        return total


def after(value, *others):
    return lax.optimization_barrier((value,) + others)[0]


def low(value):
    return value.astype(jnp.bfloat16)


def shards(
    nd,
    nf,
    tokens,
    cotangent,
    segment_ids,
    w_query,
    w_key,
    w_value,
    w_out,
    w_gate,
    w_up,
    w_down,
    m_query,
    m_key,
    m_value,
    m_out,
    m_gate,
    m_up,
    m_down,
    v_query,
    v_key,
    v_value,
    v_out,
    v_gate,
    v_up,
    v_down,
    gains,
    gain_first,
    gain_second,
):
    masters = (w_query, w_key, w_value, w_out, w_gate, w_up, w_down)
    firsts = (m_query, m_key, m_value, m_out, m_gate, m_up, m_down)
    seconds = (v_query, v_key, v_value, v_out, v_gate, v_up, v_down)
    outer = nd // MEMBERS
    dp = lax.axis_index("dp")
    ring_z = Ring(nf, lax.axis_index("fsdp"), lambda d, f, s: (d, (f + s) % nf), nd, nf)
    ring_y = Ring(
        outer,
        dp // MEMBERS,
        lambda d, f, s: ((d // MEMBERS + s) % outer * MEMBERS + d % MEMBERS, f),
        nd,
        nf,
    )
    ring_x = Ring(2, dp // 2 % 2, lambda d, f, s: (d ^ 2, f), nd, nf)
    ring_core = Ring(2, dp % 2, lambda d, f, s: (d ^ 1, f), nd, nf)
    member = dp % MEMBERS

    def trade(block, mask):
        return Ring(2, dp % 2, lambda d, f, s: (d ^ mask, f), nd, nf).move(block, 1)

    def swap(blocks):
        full = put(jnp.zeros_like(blocks), pick(blocks, 0, member), 0, member)
        for mask in range(1, MEMBERS):
            full = put(full, trade(pick(blocks, 0, member ^ mask), mask), 0, member ^ mask)
        return full

    def spread(rows):
        return ring_core.gather(ring_x.gather(rows, 0), 1)

    def collapse(terms):
        half = low(ring_core.reduce(terms, 1))
        return ring_x.reduce(half, 0)

    batch, length, width = tokens.shape
    count = batch * length
    hidden_rows = w_down.shape[0]
    hidden_all = w_gate.shape[1]
    span = nf * hidden_rows
    mine = outer * span
    in_rows = w_query.shape[0]
    out_rows = w_out.shape[0]
    attn_cols = (HQ + 2 * KV) * HD

    shard_in = jnp.concatenate([low(w_query), low(w_key), low(w_value)], 1)
    shard_out = low(w_out)
    in_z = ring_z.gather(shard_in, 0)
    out_z = ring_z.gather(shard_out, 0)
    in_xy = ring_x.gather(ring_y.gather(in_z, 0), 1)
    out_xy = ring_y.gather(ring_x.gather(out_z, 0), 0)
    in_w = ring_core.gather(in_xy, 2).reshape(D, attn_cols)
    out_w = ring_core.gather(out_xy, 2).reshape(HQ * HD, D)

    def member_columns(weight):
        return low(weight).reshape(in_rows, outer, MEMBERS, span).transpose(2, 0, 1, 3)

    columns = jnp.concatenate(
        [
            member_columns(w_gate).reshape(MEMBERS, in_rows, mine),
            member_columns(w_up).reshape(MEMBERS, in_rows, mine),
        ],
        2,
    )
    inner = swap(columns)
    inner = after(inner, in_z, out_z)
    inner_z = ring_z.gather(inner, 1)
    inner_w = ring_y.gather(inner_z, 0).reshape(D, 2 * mine)
    shard_down = after(low(w_down), inner_z)
    down_z = ring_z.gather(shard_down, 0)
    down_w = ring_y.gather(down_z, 0).reshape(mine, D)

    back_in = cotangent.reshape(count, width)
    back_all = spread(after(back_in, in_xy)).reshape(MEMBERS * count, width)

    cosine, sine = rotary_tables(length, HD)
    scale = HD ** (-0.5)
    group_size = HQ // KV
    gain_attn = gains[:D]
    gain_ffn = gains[D : 2 * D]
    gain_query = gains[2 * D : 2 * D + HD]
    gain_key = gains[2 * D + HD :]
    positions = jnp.arange(length)
    causal = positions[None, :] <= positions[:, None]
    allowed = causal[None] & (segment_ids[:, :, None] == segment_ids[:, None, :])
    allowed = allowed[:, None, None]

    def piece(raw, gain):
        return head_norm(raw.reshape(batch, length, -1), gain, cosine, sine)

    inputs = tokens.reshape(count, width).astype(jnp.float32)
    normed = low(rms_scale(inputs, gain_attn))
    raw = forward_product(normed, in_w)
    query_raw = raw[:, : HQ * HD]
    key_raw = raw[:, HQ * HD : (HQ + KV) * HD]
    values = low(raw[:, (HQ + KV) * HD :]).reshape(batch, length, KV, HD)
    queries = low(piece(query_raw, gain_query)).reshape(batch, length, KV, group_size, HD)
    keys = low(piece(key_raw, gain_key))
    scores = (
        jnp.einsum("blkrd,bmkd->bkrlm", queries, keys, preferred_element_type=jnp.float32) * scale
    )
    scores = jnp.where(allowed, scores, masked_score)
    top = jnp.max(scores, -1, keepdims=True)
    weights = jnp.exp(scores - top)
    attention_full = weights / jnp.sum(weights, -1, keepdims=True)
    attention = low(attention_full)
    mixed = jnp.einsum("bkrlm,bmkd->blkrd", attention, values, preferred_element_type=jnp.float32)
    mixed = low(mixed.reshape(count, HQ * HD))
    hidden_in = inputs + forward_product(mixed, out_w)

    ffn_all = spread(low(rms_scale(hidden_in, gain_ffn))).reshape(MEMBERS * count, width)
    inner_out = forward_product(ffn_all, inner_w)
    gate = inner_out[:, :mine]
    upper = inner_out[:, mine:]
    hidden = low(swiglu(gate, upper))
    down_terms = low(weight_product(hidden, back_all)).reshape(outer, nf, hidden_rows, width)
    down_sum = ring_z.reduce(low(ring_y.reduce(down_terms, 0)), 0)
    grad_hidden = back_product(back_all, down_w)
    _, swiglu_pull = jax.vjp(swiglu, gate, upper)
    grad_gate, grad_upper = swiglu_pull(grad_hidden)
    grad_inner = jnp.concatenate([low(grad_gate), low(grad_upper)], 1)
    grad_ffn_terms = low(back_product(grad_inner, inner_w)).reshape(2, 2, count, width)
    grad_ffn = collapse(grad_ffn_terms)
    inner_terms = low(weight_product(ffn_all, grad_inner)).reshape(
        outer, MEMBERS, nf, in_rows, 2 * mine
    )
    inner_sum = ring_z.reduce(low(ring_y.reduce(inner_terms, 0)), 1)
    inner_sum = swap(low(inner_sum)).astype(jnp.float32)
    inner_sum = inner_sum.reshape(MEMBERS, in_rows, 2, outer, span).transpose(2, 1, 3, 0, 4)
    inner_sum = inner_sum.reshape(2, in_rows, hidden_all)
    down_out = low(forward_product(hidden, down_w)).reshape(2, 2, count, width)
    output = low(hidden_in + collapse(down_out))

    _, ffn_pull = jax.vjp(rms_scale, hidden_in, gain_ffn)
    grad_hidden_in, grad_gain_ffn = ffn_pull(grad_ffn)
    grad_hidden_in = grad_hidden_in + back_in.astype(jnp.float32)
    grad_branch = low(grad_hidden_in)
    out_terms = low(weight_product(mixed, grad_branch)).reshape(
        outer, 2, 2, nf, out_rows, width
    )
    out_sum = low(ring_core.reduce(out_terms, 2))
    out_sum = low(ring_x.reduce(low(ring_y.reduce(out_sum, 0)), 0))
    out_sum = ring_z.reduce(out_sum, 0)
    grad_mixed = low(back_product(grad_branch, out_w)).reshape(batch, length, KV, group_size, HD)
    grad_attention = jnp.einsum(
        "blkrd,bmkd->bkrlm", grad_mixed, values, preferred_element_type=jnp.float32
    )
    grad_scores = low(
        attention_full
        * (grad_attention - jnp.sum(attention_full * grad_attention, -1, keepdims=True))
    )
    grad_values = jnp.einsum(
        "bkrlm,blkrd->bmkd", attention, grad_mixed, preferred_element_type=jnp.float32
    )
    grad_values = low(grad_values.reshape(count, KV * HD))
    grad_queries = (
        jnp.einsum("bkrlm,bmkd->blkrd", grad_scores, keys, preferred_element_type=jnp.float32)
        * scale
    )
    grad_keys = (
        jnp.einsum("bkrlm,blkrd->bmkd", grad_scores, queries, preferred_element_type=jnp.float32)
        * scale
    )
    _, query_pull = jax.vjp(piece, query_raw, gain_query)
    grad_query_raw, grad_gain_query = query_pull(grad_queries.reshape(batch, length, HQ, HD))
    _, key_pull = jax.vjp(piece, key_raw, gain_key)
    grad_key_raw, grad_gain_key = key_pull(grad_keys)
    grad_raw = jnp.concatenate([low(grad_query_raw), low(grad_key_raw), grad_values], 1)
    in_terms = low(weight_product(normed, grad_raw)).reshape(
        outer, 2, 2, nf, in_rows, attn_cols
    )
    in_sum = low(ring_core.reduce(in_terms, 2))
    in_sum = low(ring_y.reduce(low(ring_x.reduce(in_sum, 1)), 0))
    in_sum = ring_z.reduce(in_sum, 0)
    grad_normed = back_product(grad_raw, in_w)
    _, attn_pull = jax.vjp(rms_scale, inputs, gain_attn)
    grad_inputs, grad_gain_attn = attn_pull(grad_normed)
    input_grad = low(grad_inputs + grad_hidden_in)
    gain_terms = jnp.concatenate([grad_gain_attn, grad_gain_ffn, grad_gain_query, grad_gain_key])

    reduced = (
        in_sum[:, : HQ * HD],
        in_sum[:, HQ * HD : (HQ + KV) * HD],
        in_sum[:, (HQ + KV) * HD :],
        out_sum,
        inner_sum[0],
        inner_sum[1],
        down_sum,
    )
    local_squares = (
        jnp.sum(in_sum * in_sum)
        + jnp.sum(out_sum * out_sum)
        + jnp.sum(inner_sum * inner_sum)
        + jnp.sum(down_sum * down_sum)
    )
    gain_total = lax.psum(gain_terms, AXES)
    square_total = lax.psum(local_squares, AXES)
    total_norm = jnp.sqrt(square_total + jnp.sum(gain_total * gain_total))
    factor = jnp.minimum(1.0, clip_limit / (total_norm + 1e-06))
    clipped = tuple((share * factor for share in reduced))
    gain_clipped = gain_total * factor
    weight_rate = 2.0 * D ** (-0.5)
    updates = [
        adam_update(
            masters[index], firsts[index], seconds[index], clipped[index], weight_rate, decay_rate
        )
        for index in range(7)
    ]
    new_masters = tuple((item[0] for item in updates))
    new_seconds = tuple((item[1] for item in updates))
    new_gains, gain_seconds = adam_update(
        gains, gain_first, gain_second, gain_clipped, gain_rate, 0.0
    )
    copies = tuple((low(item) for item in new_masters))
    return (
        (output.reshape(tokens.shape), input_grad.reshape(tokens.shape))
        + clipped
        + (gain_clipped, total_norm)
        + new_masters
        + (new_gains,)
        + copies
        + new_seconds
        + (gain_seconds,)
    )


def solution(mesh):
    rows3 = P(AXES, None, None)
    rows2 = P(AXES, None)
    whole = P()
    return jax.shard_map(
        functools.partial(shards, mesh.shape["dp"], mesh.shape["fsdp"]),
        mesh=mesh,
        in_specs=(rows3, rows3) + (rows2,) * 22 + (whole,) * 3,
        out_specs=(rows3, rows3)
        + (rows2,) * 7
        + (whole, whole)
        + (rows2,) * 7
        + (whole,)
        + (rows2,) * 14
        + (whole,),
        check_vma=False,
    )
```

time: 1600 us -> 520 us (0.33)
  waiting for transfers between devices: 1180 us -> 173 us
  blocking collectives: 189 us -> 40.3 us
  starting transfers between devices: 0.96 us -> 75.8 us
  matrix products: 131 us -> 56.3 us
  local copies, waits for them, and re-layouts: 26.1 us -> 91.4 us
  other arithmetic: 43 us -> 66.2 us
    reduce_scatter x7 -> x0, waiting for transfers between devices: 1010 us -> none  [the longest x1 173 us: shards(): lax.psum_scatter(inner_held[1], ('dp', 'fsdp'), scatter_dimension=0, tile...]
    ppermute x0 -> x54, waiting for transfers between devices: none -> 173 us  [move(): return lax.ppermute(block, AXES, pairs)]
    all_gather x5 -> x0, waiting for transfers between devices: 168 us -> none  [the longest x1 71.3 us: shards(): lax.all_gather(rounded[5], ('dp', 'fsdp'), axis=0, tiled=True)]
    all_gather x2 -> x0, blocking collectives: 149 us -> none  [the longest x1 77.9 us: shards(): lax.all_gather(rounded[1], ('dp', 'fsdp'), axis=0, tiled=True)]
    ppermute x0 -> x54, starting transfers between devices: none -> 75.8 us  [move(): return lax.ppermute(block, AXES, pairs)]
    dot_general x14 -> x4, matrix products: 43.7 us -> 14.5 us  [weight_product(): lax.dot_general(left, right, (((0,), (0,)), ((), ())), preferred_element_...]
    dot_general x14 -> x4, matrix products: 43.7 us -> 15.2 us  [back_product(): lax.dot_general(left, right, (((1,), (1,)), ((), ())), preferred_element_...]
    dynamic_update_slice x0 -> x43, local copies, waits for them, and re-layouts: none -> 22.6 us  [put(): return lax.dynamic_update_index_in_dim(buffer, block, index, axis)]
  transfers between devices with their start and end apart: 12 -> 54, of which waited for: 10 -> 20; matrix products, arithmetic and copies ran while one was open for 7% -> 33% of each run, Pallas kernels for 0% -> 0%
where the time goes in v1:
time: 520 us; the launch traced here: 511 us
  waiting for transfers between devices  173 us (33%)
  local copies, waits for them, and re-layouts  91.4 us (18%)
  starting transfers between devices  75.8 us (15%)
  other arithmetic  66.2 us (13%)
  matrix products  56.3 us (11%)
  blocking collectives  40.3 us (8%)
  between operations  8.14 us (2%)
    ppermute x54, waiting for transfers between devices, move(): return lax.ppermute(block, AXES, pairs)  173 us
    ppermute x54, starting transfers between devices, move(): return lax.ppermute(block, AXES, pairs)  75.8 us
    psum x1, blocking collectives, shards(): square_total = lax.psum(local_squares, AXES)  40.3 us
    convert_element_type x27, other arithmetic, low(): return value.astype(jnp.bfloat16)  37.4 us
    dynamic_update_slice x43, local copies, waits for them, and re-layouts, put(): return lax.dynamic_update_index_in_dim(buffer, block, index, axis)  22.6 us
    dot_general x4, matrix products, back_product(): lax.dot_general(left, right, (((1,), (1,)), ((), ())), preferred_element_...  15.2 us
    dot_general x4, matrix products, weight_product(): lax.dot_general(left, right, (((0,), (0,)), ((), ())), preferred_element_...  14.5 us
    dot_general x4, matrix products, forward_product(): return jnp.dot(left, right, preferred_element_type=jnp.float32)  12.7 us
  transfers between devices with their start and end apart: 54, of which 20 were waited for; matrix products, arithmetic and copies ran while one was open for 33% of the time, Pallas kernels for 0%

profile of v1, /device:TPU:0, one launch (start us, length us, event | category | flops | bytes accessed | tf_op | source)
XLA Modules:
  0.0 511.3 jit_solution(17850512557971516821)
XLA Ops:
  27.7 3.3 collective-permute-done.15
  43.8 6.2 %collective-permute-done.17 = bf16[4,40,1536]{2,1,0:T(8,128)(2,1)S(1)} collective-permute-done((bf16[4,40,1536]{2,1,0:T(8,128)(2,1)S(1)}, bf16[4,40,1536]{2,1,0:T(8,128)(2,1)S(1)}, u32[]{:S(2)}, u32[]{:S(2)}) %collective-permute-start.17) | collective-permute-done | bytes 491552 | tf_op jit(solution)/shard_map/ppermute | solution.py:105
  50.9 19.8 %collective-permute-done.18 = bf16[4,40,1536]{2,1,0:T(8,128)(2,1)S(1)} collective-permute-done((bf16[4,40,1536]{2,1,0:T(8,128)(2,1)S(1)}, bf16[4,40,1536]{2,1,0:T(8,128)(2,1)S(1)}, u32[]{:S(2)}, u32[]{:S(2)}) %collective-permute-start.18) | collective-permute-done | bytes 491552 | tf_op jit(solution)/shard_map/ppermute | solution.py:105
  72.3 9.6 %collective-permute-start.21 = (bf16[96,1280]{1,0:T(8,128)(2,1)S(1)}, bf16[96,1280]{1,0:T(8,128)(2,1)S(1)}, u32[]{:S(2)}, u32[]{:S(2)}) collective-permute-start(bf16[96,1280]{1,0:T(8,128)(2,1)S(1)} %convert_element_type.366), channel_id=1, source_target_pairs={{0,1},{1,2},{2,3},{3,0},{4,5},{5,6},{6,7},{7,4},{8,9},{9,10},{10,1... | collective-permute-start | bytes 737288 | tf_op jit(solution)/shard_map/ppermute | solution.py:105
  92.4 8.0 %collective-permute-done.22 = bf16[96,1280]{1,0:T(8,128)(2,1)S(1)} collective-permute-done((bf16[96,1280]{1,0:T(8,128)(2,1)S(1)}, bf16[96,1280]{1,0:T(8,128)(2,1)S(1)}, u32[]{:S(2)}, u32[]{:S(2)}) %collective-permute-start.22) | collective-permute-done | bytes 245792 | tf_op jit(solution)/shard_map/ppermute | solution.py:105
  102.8 4.5 collective-permute-done.4
  113.1 41.7 %collective-permute-done.24 = bf16[4,96,1280]{2,1,0:T(8,128)(2,1)S(1)} collective-permute-done((bf16[4,96,1280]{2,1,0:T(8,128)(2,1)S(1)}, bf16[4,96,1280]{2,1,0:T(8,128)(2,1)S(1)}, u32[]{:S(2)}, u32[]{:S(2)}) %collective-permute-start.24) | collective-permute-done | bytes 983072 | tf_op jit(solution)/shard_map/ppermute | solution.py:105
  162.3 3.4 reshape_reshape.7
  184.0 3.9 convert_element_type.360
  187.9 3.2 multiply_reduce_fusion.7
  197.9 11.5 %collective-permute-done.12 = bf16[320,1280]{1,0:T(8,128)(2,1)S(1)} collective-permute-done((bf16[320,1280]{1,0:T(8,128)(2,1)S(1)}, bf16[320,1280]{1,0:T(8,128)(2,1)S(1)}, u32[]{:S(2)}, u32[]{:S(2)}) %collective-permute-start.12) | collective-permute-done | bytes 819232 | tf_op jit(solution)/shard_map/ppermute | solution.py:105
  213.3 5.3 %fusion.108 = f32[1280,1536]{1,0:T(8,128)S(1)} fusion(bf16[1280,1280]{1,0:T(8,128)(2,1)S(1)} %bitcast.394, bf16[1280,1536]{1,0:T(8,128)(2,1)S(1)} %bitcast.383), kind=kOutput, calls=%fused_computation.298 | convolution fusion | flops 5033164800 | bytes 15073280 | tf_op jit(solution)/shard_map/dot_general | solution.py:59
  218.5 5.8 %fusion.7 = (bf16[1280,768]{1,0:T(8,128)(2,1)}, bf16[1280,768]{1,0:T(8,128)(2,1)}, bf16[1280,768]{1,0:T(8,128)(2,1)S(1)}) fusion(f32[1280,1536]{1,0:T(8,128)S(1)} %fusion.108, bf16[1280,1280]{1,0:T(8,128)(2,1)S(1)} %bitcast.392, bf16[768,1280]{1,0:T(8,128)(2,1)S(1)} %bitcast.398), kind=kOutput, calls=%fused_computation.16 | convolution fusion | flops 2532311040 | bytes 19005440 | tf_op jit(solution)/shard_map/dot_general | solution.py:69
  233.3 6.3 %convolution_convert_fusion = bf16[1280,1536]{1,0:T(8,128)(2,1)S(1)} fusion(bf16[1280,1280]{1,0:T(8,128)(2,1)S(1)} %bitcast.395, bf16[1280,768]{1,0:T(8,128)(2,1)S(1)} %copy-done.81, bf16[1280,768]{1,0:T(8,128)(2,1)S(1)} %copy-done.80), kind=kOutput, calls=%fused_computation.1 | convolution fusion | flops 5042995200 | bytes 11141120 | tf_op jit(solution)/shard_map/dot_general | solution.py:63
  239.5 5.5 %convolution_convert_fusion.1 = bf16[1280,1280]{1,0:T(8,128)(2,1)S(1)} fusion(bf16[1280,1536]{1,0:T(8,128)(2,1)S(1)} %bitcast.384, bf16[1280,768]{1,0:T(8,128)(2,1)S(1)} %copy-done.81, bf16[1280,768]{1,0:T(8,128)(2,1)S(1)} %copy-done.80), kind=kOutput, calls=%fused_computation.2 | convolution fusion | flops 5042667520 | bytes 11141120 | tf_op jit(solution)/shard_map/dot_general | solution.py:69
  246.5 9.2 %collective-permute-done.50 = bf16[4,96,1280]{2,1,0:T(8,128)(2,1)S(1)} collective-permute-done((bf16[4,96,1280]{2,1,0:T(8,128)(2,1)S(1)}, bf16[4,96,1280]{2,1,0:T(8,128)(2,1)S(1)}, u32[]{:S(2)}, u32[]{:S(2)}) %collective-permute-start.50) | collective-permute-done | bytes 983072 | tf_op jit(solution)/shard_map/ppermute | solution.py:105
  263.8 4.0 collective-permute-done.51
  271.9 5.0 collective-permute-done.52
  285.7 24.4 %collective-permute-done.43 = bf16[4,4,40,1536]{3,2,0,1:T(8,128)(2,1)} collective-permute-done((bf16[4,4,40,1536]{3,2,0,1:T(8,128)(2,1)}, bf16[4,4,40,1536]{3,2,0,1:T(8,128)(2,1)}, u32[]{:S(2)}, u32[]{:S(2)}) %collective-permute-start.43) | collective-permute-done | bytes 1966112 | tf_op jit(solution)/shard_map/ppermute | solution.py:105
  326.1 3.9 reshape.408
  330.0 3.8 copy.345
  333.8 3.9 fusion.39
  337.8 3.6 fusion.1
  359.8 3.9 multiply_reduce_fusion
  400.0 9.3 %collective-permute-done.38 = bf16[2,4,32,1280]{3,2,1,0:T(8,128)(2,1)} collective-permute-done((bf16[2,4,32,1280]{3,2,1,0:T(8,128)(2,1)}, bf16[2,4,32,1280]{3,2,1,0:T(8,128)(2,1)}, u32[]{:S(2)}, u32[]{:S(2)}) %collective-permute-start.38) | collective-permute-done | bytes 655392 | tf_op jit(solution)/shard_map/ppermute | solution.py:105
  411.4 10.4 %collective-permute-done.32 = bf16[2,4,40,1536]{3,2,1,0:T(8,128)(2,1)} collective-permute-done((bf16[2,4,40,1536]{3,2,1,0:T(8,128)(2,1)}, bf16[2,4,40,1536]{3,2,1,0:T(8,128)(2,1)}, u32[]{:S(2)}, u32[]{:S(2)}) %collective-permute-start.32) | collective-permute-done | bytes 983072 | tf_op jit(solution)/shard_map/ppermute | solution.py:105
  423.8 3.9 collective-permute-done.39
  427.8 5.9 %collective-permute-start.40 = (bf16[32,1280]{1,0:T(8,128)(2,1)S(1)}, bf16[32,1280]{1,0:T(8,128)(2,1)S(1)}, u32[]{:S(2)}, u32[]{:S(2)}) collective-permute-start(bf16[32,1280]{1,0:T(8,128)(2,1)S(1)} %get-tuple-element.123), channel_id=1, source_target_pairs={{0,1},{1,2},{2,3},{3,0},{4,5},{5,6},{6,7},{7,4},{8,9},{9,10},{10,1... | collective-permute-start | bytes 245768 | tf_op jit(solution)/shard_map/ppermute | solution.py:105
  436.3 4.3 collective-permute-start.34
  444.9 5.2 %collective-permute-done.35 = bf16[40,1536]{1,0:T(8,128)(2,1)S(1)} collective-permute-done((bf16[40,1536]{1,0:T(8,128)(2,1)S(1)}, bf16[40,1536]{1,0:T(8,128)(2,1)S(1)}, u32[]{:S(2)}, u32[]{:S(2)}) %collective-permute-start.35) | collective-permute-done | bytes 122912 | tf_op jit(solution)/shard_map/ppermute | solution.py:105
  453.4 40.3 %all-reduce.4 = (f32[]{:T(128)}, f32[2688]{0:T(1024)S(1)}) all-reduce(f32[]{:T(128)S(6)} %add.582, f32[2688]{0:T(1024)S(1)} %concatenate.36), channel_id=1, replica_groups=mesh['dp'=8,'fsdp'=4] {'dp','fsdp'}, use_global_device_ids=true, to_apply=%region_15.16 | all-reduce | flops 2689 | bytes 21512 | tf_op jit(solution)/shard_map/psum | solution.py:361
  501.6 3.5 fusion.88
  (454 shorter events, 221.0 us)
Async XLA Ops:
  2.3 17.6 %collective-permute-start.6 = (bf16[32,1280]{1,0:T(8,128)(2,1)}, bf16[32,1280]{1,0:T(8,128)(2,1)}, u32[]{:S(2)}, u32[]{:S(2)}) collective-permute-start(bf16[32,1280]{1,0:T(8,128)(2,1)} %get-tuple-element.84), channel_id=1, source_target_pairs={{0,1},{1,2},{2,3},{3,0},{4,5},{5,6},{6,7},{7,4},{8,9},{9,10},{10,1... | collective-permute-start | bytes 245768 | tf_op jit(solution)/shard_map/ppermute | solution.py:105
  5.4 18.4 %collective-permute-start.7 = (bf16[32,1280]{1,0:T(8,128)(2,1)}, bf16[32,1280]{1,0:T(8,128)(2,1)}, u32[]{:S(2)}, u32[]{:S(2)}) collective-permute-start(bf16[32,1280]{1,0:T(8,128)(2,1)} %get-tuple-element.84), channel_id=1, source_target_pairs={{0,2},{1,3},{2,0},{3,1},{4,6},{5,7},{6,4},{7,5},{8,10},{9,11},{10,... | collective-permute-start | bytes 245768 | tf_op jit(solution)/shard_map/ppermute | solution.py:105
  11.8 21.2 %collective-permute-start = (bf16[40,1536]{1,0:T(8,128)(2,1)S(1)}, bf16[40,1536]{1,0:T(8,128)(2,1)}, u32[]{:S(2)}, u32[]{:S(2)}) collective-permute-start(bf16[40,1536]{1,0:T(8,128)(2,1)S(1)} %pad_maximum_fusion.6), channel_id=1, source_target_pairs={{0,1},{1,2},{2,3},{3,0},{4,5},{5,6},{6,7},{7,4},{8,9},{9,10},{10,1... | collective-permute-start | bytes 368648 | tf_op jit(solution)/shard_map/ppermute | solution.py:105
  12.5 21.4 %collective-permute-start.1 = (bf16[40,1536]{1,0:T(8,128)(2,1)S(1)}, bf16[40,1536]{1,0:T(8,128)(2,1)S(1)}, u32[]{:S(2)}, u32[]{:S(2)}) collective-permute-start(bf16[40,1536]{1,0:T(8,128)(2,1)S(1)} %pad_maximum_fusion.6), channel_id=1, source_target_pairs={{0,2},{1,3},{2,0},{3,1},{4,6},{5,7},{6,4},{7,5},{8,10},{9,11},{10,... | collective-permute-start | bytes 368648 | tf_op jit(solution)/shard_map/ppermute | solution.py:105
  34.7 36.0 %collective-permute-start.18 = (bf16[4,40,1536]{2,1,0:T(8,128)(2,1)S(1)}, bf16[4,40,1536]{2,1,0:T(8,128)(2,1)S(1)}, u32[]{:S(2)}, u32[]{:S(2)}) collective-permute-start(bf16[4,40,1536]{2,1,0:T(8,128)(2,1)S(1)} %bitcast_dynamic-update-slice_fusion.35), channel_id=1, source_target_pairs={{0,2},{1,3},{2,0},{3,1},{4,6},{5,7},{6,4},{7,5},{8,10},{9,11},{10,... | collective-permute-start | bytes 1474568 | tf_op jit(solution)/shard_map/ppermute | solution.py:105
  36.2 35.3 %collective-permute-start.19 = (bf16[4,40,1536]{2,1,0:T(8,128)(2,1)S(1)}, bf16[4,40,1536]{2,1,0:T(8,128)(2,1)S(1)}, u32[]{:S(2)}, u32[]{:S(2)}) collective-permute-start(bf16[4,40,1536]{2,1,0:T(8,128)(2,1)S(1)} %bitcast_dynamic-update-slice_fusion.35), channel_id=1, source_target_pairs={{0,3},{1,0},{2,1},{3,2},{4,7},{5,4},{6,5},{7,6},{8,11},{9,8},{10,9... | collective-permute-start | bytes 1474568 | tf_op jit(solution)/shard_map/ppermute | solution.py:105
  39.1 45.4 %collective-permute-start.3 = (bf16[4,40,1536]{2,1,0:T(8,128)(2,1)S(1)}, bf16[4,40,1536]{2,1,0:T(8,128)(2,1)S(1)}, u32[]{:S(2)}, u32[]{:S(2)}) collective-permute-start(bf16[4,40,1536]{2,1,0:T(8,128)(2,1)S(1)} %bitcast_dynamic-update-slice_fusion.38), channel_id=1, source_target_pairs={{0,16},{1,17},{2,18},{3,19},{4,20},{5,21},{6,22},{7,23},{8,24},{9,... | collective-permute-start | bytes 1474568 | tf_op jit(solution)/shard_map/ppermute | solution.py:105
  43.1 59.1 %collective-permute-start.10 = (bf16[2,4,32,1280]{3,2,1,0:T(8,128)(2,1)S(1)}, bf16[2,4,32,1280]{3,2,1,0:T(8,128)(2,1)S(1)}, u32[]{:S(2)}, u32[]{:S(2)}) collective-permute-start(bf16[2,4,32,1280]{3,2,1,0:T(8,128)(2,1)S(1)} %bitcast_dynamic-update-slice_fusion.26), channel_id=1, source_target_pairs={{0,16},{1,17},{2,18},{3,19},{4,20},{5,21},{6,22},{7,23},{8,24},{9,... | collective-permute-start | bytes 1966088 | tf_op jit(solution)/shard_map/ppermute | solution.py:105
  72.3 18.5 %collective-permute-start.21 = (bf16[96,1280]{1,0:T(8,128)(2,1)S(1)}, bf16[96,1280]{1,0:T(8,128)(2,1)S(1)}, u32[]{:S(2)}, u32[]{:S(2)}) collective-permute-start(bf16[96,1280]{1,0:T(8,128)(2,1)S(1)} %convert_element_type.366), channel_id=1, source_target_pairs={{0,1},{1,2},{2,3},{3,0},{4,5},{5,6},{6,7},{7,4},{8,9},{9,10},{10,1... | collective-permute-start | bytes 737288 | tf_op jit(solution)/shard_map/ppermute | solution.py:105
  81.9 18.4 %collective-permute-start.22 = (bf16[96,1280]{1,0:T(8,128)(2,1)S(1)}, bf16[96,1280]{1,0:T(8,128)(2,1)S(1)}, u32[]{:S(2)}, u32[]{:S(2)}) collective-permute-start(bf16[96,1280]{1,0:T(8,128)(2,1)S(1)} %convert_element_type.366), channel_id=1, source_target_pairs={{0,2},{1,3},{2,0},{3,1},{4,6},{5,7},{6,4},{7,5},{8,10},{9,11},{10,... | collective-permute-start | bytes 737288 | tf_op jit(solution)/shard_map/ppermute | solution.py:105
  84.5 22.8 %collective-permute-start.4 = (bf16[2,4,40,1536]{3,2,1,0:T(8,128)(2,1)S(1)}, bf16[2,4,40,1536]{3,2,1,0:T(8,128)(2,1)S(1)}, u32[]{:S(2)}, u32[]{:S(2)}) collective-permute-start(bf16[2,4,40,1536]{3,2,1,0:T(8,128)(2,1)S(1)} %bitcast_dynamic-update-slice_fusion.24), channel_id=1, source_target_pairs={{0,8},{1,9},{2,10},{3,11},{4,12},{5,13},{6,14},{7,15},{8,0},{9,1},... | collective-permute-start | bytes 2949128 | tf_op jit(solution)/shard_map/ppermute | solution.py:105
  90.8 118.8 %collective-permute-start.20 = (bf16[4,4,40,1536]{3,2,1,0:T(8,128)(2,1)}, bf16[4,4,40,1536]{3,2,1,0:T(8,128)(2,1)}, u32[]{:S(2)}, u32[]{:S(2)}) collective-permute-start(bf16[4,4,40,1536]{3,2,1,0:T(8,128)(2,1)} %bitcast_dynamic-update-slice_fusion.20), channel_id=1, source_target_pairs={{0,16},{1,17},{2,18},{3,19},{4,20},{5,21},{6,22},{7,23},{8,24},{9,... | collective-permute-start | bytes 5898248 | tf_op jit(solution)/shard_map/ppermute | solution.py:105
  100.4 54.4 %collective-permute-start.24 = (bf16[4,96,1280]{2,1,0:T(8,128)(2,1)S(1)}, bf16[4,96,1280]{2,1,0:T(8,128)(2,1)S(1)}, u32[]{:S(2)}, u32[]{:S(2)}) collective-permute-start(bf16[4,96,1280]{2,1,0:T(8,128)(2,1)S(1)} %bitcast_dynamic-update-slice_fusion.28), channel_id=1, source_target_pairs={{0,16},{1,17},{2,18},{3,19},{4,20},{5,21},{6,22},{7,23},{8,24},{9,... | collective-permute-start | bytes 2949128 | tf_op jit(solution)/shard_map/ppermute | solution.py:105
  102.3 52.6 %collective-permute-start.11 = (bf16[2,2,4,32,1280]{4,3,2,1,0:T(8,128)(2,1)S(1)}, bf16[2,2,4,32,1280]{4,3,2,1,0:T(8,128)(2,1)S(1)}, u32[]{:S(2)}, u32[]{:S(2)}) collective-permute-start(bf16[2,2,4,32,1280]{4,3,2,1,0:T(8,128)(2,1)S(1)} %bitcast_dynamic-update-slice_fusion.18), channel_id=1, source_target_pairs={{0,4},{1,5},{2,6},{3,7},{4,0},{5,1},{6,2},{7,3},{8,12},{9,13},{10,... | collective-permute-start | bytes 3932168 | tf_op jit(solution)/shard_map/ppermute | solution.py:105
  107.4 47.7 %collective-permute-start.5 = (bf16[2,2,4,40,1536]{4,3,2,1,0:T(8,128)(2,1)S(1)}, bf16[2,2,4,40,1536]{4,3,2,1,0:T(8,128)(2,1)S(1)}, u32[]{:S(2)}, u32[]{:S(2)}) collective-permute-start(bf16[2,2,4,40,1536]{4,3,2,1,0:T(8,128)(2,1)S(1)} %bitcast_dynamic-update-slice_fusion.13), channel_id=1, source_target_pairs={{0,4},{1,5},{2,6},{3,7},{4,0},{5,1},{6,2},{7,3},{8,12},{9,13},{10,... | collective-permute-start | bytes 5898248 | tf_op jit(solution)/shard_map/ppermute | solution.py:105
  107.5 86.3 %collective-permute-start.27 = (bf16[320,1280]{1,0:T(8,128)(2,1)}, bf16[320,1280]{1,0:T(8,128)(2,1)}, u32[]{:S(2)}, u32[]{:S(2)}) collective-permute-start(bf16[320,1280]{1,0:T(8,128)(2,1)} %bitcast.74), channel_id=1, source_target_pairs={{0,8},{1,9},{2,10},{3,11},{4,12},{5,13},{6,14},{7,15},{8,0},{9,1},... | collective-permute-start | bytes 2457608 | tf_op jit(solution)/shard_map/ppermute | solution.py:105
  192.2 17.2 %collective-permute-start.12 = (bf16[320,1280]{1,0:T(8,128)(2,1)S(1)}, bf16[320,1280]{1,0:T(8,128)(2,1)S(1)}, u32[]{:S(2)}, u32[]{:S(2)}) collective-permute-start(bf16[320,1280]{1,0:T(8,128)(2,1)S(1)} %get-tuple-element.82), channel_id=1, source_target_pairs={{0,8},{1,9},{2,10},{3,11},{4,12},{5,13},{6,14},{7,15},{8,0},{9,1},... | collective-permute-start | bytes 2457608 | tf_op jit(solution)/shard_map/ppermute | solution.py:105
  231.4 47.6 %collective-permute-start.25 = (bf16[2,320,1280]{2,1,0:T(8,128)(2,1)}, bf16[2,320,1280]{2,1,0:T(8,128)(2,1)}, u32[]{:S(2)}, u32[]{:S(2)}) collective-permute-start(bf16[2,320,1280]{2,1,0:T(8,128)(2,1)} %dynamic-slice_bitcast_fusion.1), channel_id=1, source_target_pairs={{0,4},{1,5},{2,6},{3,7},{4,0},{5,1},{6,2},{7,3},{8,12},{9,13},{10,... | collective-permute-start | bytes 4915208 | tf_op jit(solution)/shard_map/ppermute | solution.py:105
  231.6 24.1 %collective-permute-start.50 = (bf16[4,96,1280]{2,1,0:T(8,128)(2,1)S(1)}, bf16[4,96,1280]{2,1,0:T(8,128)(2,1)S(1)}, u32[]{:S(2)}, u32[]{:S(2)}) collective-permute-start(bf16[4,96,1280]{2,1,0:T(8,128)(2,1)S(1)} %dynamic-slice_bitcast_fusion.3), channel_id=1, source_target_pairs={{0,16},{1,17},{2,18},{3,19},{4,20},{5,21},{6,22},{7,23},{8,24},{9,... | collective-permute-start | bytes 2949128 | tf_op jit(solution)/shard_map/ppermute | solution.py:105
  246.4 36.8 %collective-permute-start.29 = (bf16[2,320,1280]{2,1,0:T(8,128)(2,1)}, bf16[2,320,1280]{2,1,0:T(8,128)(2,1)}, u32[]{:S(2)}, u32[]{:S(2)}) collective-permute-start(bf16[2,320,1280]{2,1,0:T(8,128)(2,1)} %dynamic-slice_bitcast_fusion), channel_id=1, source_target_pairs={{0,4},{1,5},{2,6},{3,7},{4,0},{5,1},{6,2},{7,3},{8,12},{9,13},{10,... | collective-permute-start | bytes 4915208 | tf_op jit(solution)/shard_map/ppermute | solution.py:105
  257.7 19.2 %collective-permute-start.52 = (bf16[96,1280]{1,0:T(8,128)(2,1)}, bf16[96,1280]{1,0:T(8,128)(2,1)}, u32[]{:S(2)}, u32[]{:S(2)}) collective-permute-start(bf16[96,1280]{1,0:T(8,128)(2,1)} %get-tuple-element.107), channel_id=1, source_target_pairs={{0,2},{1,3},{2,0},{3,1},{4,6},{5,7},{6,4},{7,5},{8,10},{9,11},{10,... | collective-permute-start | bytes 737288 | tf_op jit(solution)/shard_map/ppermute | solution.py:105
  260.0 17.0 %collective-permute-start.53 = (bf16[96,1280]{1,0:T(8,128)(2,1)}, bf16[96,1280]{1,0:T(8,128)(2,1)}, u32[]{:S(2)}, u32[]{:S(2)}) collective-permute-start(bf16[96,1280]{1,0:T(8,128)(2,1)} %get-tuple-element.106), channel_id=1, source_target_pairs={{0,3},{1,0},{2,1},{3,2},{4,7},{5,4},{6,5},{7,6},{8,11},{9,8},{10,9... | collective-permute-start | bytes 737288 | tf_op jit(solution)/shard_map/ppermute | solution.py:105
  267.8 42.3 %collective-permute-start.43 = (bf16[4,4,40,1536]{3,2,0,1:T(8,128)(2,1)}, bf16[4,4,40,1536]{3,2,0,1:T(8,128)(2,1)}, u32[]{:S(2)}, u32[]{:S(2)}) collective-permute-start(bf16[4,4,40,1536]{3,2,0,1:T(8,128)(2,1)} %bitcast.362), channel_id=1, source_target_pairs={{0,16},{1,17},{2,18},{3,19},{4,20},{5,21},{6,22},{7,23},{8,24},{9,... | collective-permute-start | bytes 5898248 | tf_op jit(solution)/shard_map/ppermute | solution.py:105
  281.5 38.5 %collective-permute-start.26 = (bf16[320,1280]{1,0:T(8,128)(2,1)S(1)}, bf16[320,1280]{1,0:T(8,128)(2,1)S(1)}, u32[]{:S(2)}, u32[]{:S(2)}) collective-permute-start(bf16[320,1280]{1,0:T(8,128)(2,1)S(1)} %dynamic-slice_bitcast_fusion.6), channel_id=1, source_target_pairs={{0,8},{1,9},{2,10},{3,11},{4,12},{5,13},{6,14},{7,15},{8,0},{9,1},... | collective-permute-start | bytes 2457608 | tf_op jit(solution)/shard_map/ppermute | solution.py:105
  285.3 33.6 %collective-permute-start.30 = (bf16[320,1280]{1,0:T(8,128)(2,1)S(1)}, bf16[320,1280]{1,0:T(8,128)(2,1)S(1)}, u32[]{:S(2)}, u32[]{:S(2)}) collective-permute-start(bf16[320,1280]{1,0:T(8,128)(2,1)S(1)} %dynamic-slice_bitcast_fusion.5), channel_id=1, source_target_pairs={{0,8},{1,9},{2,10},{3,11},{4,12},{5,13},{6,14},{7,15},{8,0},{9,1},... | collective-permute-start | bytes 2457608 | tf_op jit(solution)/shard_map/ppermute | solution.py:105
  313.3 60.9 %collective-permute-start.44 = (bf16[4,40,1536]{2,1,0:T(8,128)(2,1)}, bf16[4,40,1536]{2,1,0:T(8,128)(2,1)}, u32[]{:S(2)}, u32[]{:S(2)}) collective-permute-start(bf16[4,40,1536]{2,1,0:T(8,128)(2,1)} %get-tuple-element.98), channel_id=1, source_target_pairs={{0,1},{1,2},{2,3},{3,0},{4,5},{5,6},{6,7},{7,4},{8,9},{9,10},{10,1... | collective-permute-start | bytes 1474568 | tf_op jit(solution)/shard_map/ppermute | solution.py:105
  313.3 60.9 %collective-permute-start.45 = (bf16[4,40,1536]{2,1,0:T(8,128)(2,1)}, bf16[4,40,1536]{2,1,0:T(8,128)(2,1)}, u32[]{:S(2)}, u32[]{:S(2)}) collective-permute-start(bf16[4,40,1536]{2,1,0:T(8,128)(2,1)} %get-tuple-element.100), channel_id=1, source_target_pairs={{0,2},{1,3},{2,0},{3,1},{4,6},{5,7},{6,4},{7,5},{8,10},{9,11},{10,... | collective-permute-start | bytes 1474568 | tf_op jit(solution)/shard_map/ppermute | solution.py:105
  315.0 59.2 %collective-permute-start.46 = (bf16[4,40,1536]{2,1,0:T(8,128)(2,1)}, bf16[4,40,1536]{2,1,0:T(8,128)(2,1)}, u32[]{:S(2)}, u32[]{:S(2)}) collective-permute-start(bf16[4,40,1536]{2,1,0:T(8,128)(2,1)} %get-tuple-element.99), channel_id=1, source_target_pairs={{0,3},{1,0},{2,1},{3,2},{4,7},{5,4},{6,5},{7,6},{8,11},{9,8},{10,9... | collective-permute-start | bytes 1474568 | tf_op jit(solution)/shard_map/ppermute | solution.py:105
  378.4 19.2 %collective-permute-start.49 = (bf16[40,1536]{1,0:T(8,128)(2,1)}, bf16[40,1536]{1,0:T(8,128)(2,1)}, u32[]{:S(2)}, u32[]{:S(2)}) collective-permute-start(bf16[40,1536]{1,0:T(8,128)(2,1)} %get-tuple-element.112), channel_id=1, source_target_pairs={{0,12},{1,13},{2,14},{3,15},{4,8},{5,9},{6,10},{7,11},{8,4},{9,5},... | collective-permute-start | bytes 368648 | tf_op jit(solution)/shard_map/ppermute | solution.py:105
  392.1 17.2 %collective-permute-start.38 = (bf16[2,4,32,1280]{3,2,1,0:T(8,128)(2,1)}, bf16[2,4,32,1280]{3,2,1,0:T(8,128)(2,1)}, u32[]{:S(2)}, u32[]{:S(2)}) collective-permute-start(bf16[2,4,32,1280]{3,2,1,0:T(8,128)(2,1)} %dynamic-slice_bitcast_fusion.7), channel_id=1, source_target_pairs={{0,16},{1,17},{2,18},{3,19},{4,20},{5,21},{6,22},{7,23},{8,24},{9,... | collective-permute-start | bytes 1966088 | tf_op jit(solution)/shard_map/ppermute | solution.py:105
  396.9 24.9 %collective-permute-start.32 = (bf16[2,4,40,1536]{3,2,1,0:T(8,128)(2,1)}, bf16[2,4,40,1536]{3,2,1,0:T(8,128)(2,1)}, u32[]{:S(2)}, u32[]{:S(2)}) collective-permute-start(bf16[2,4,40,1536]{3,2,1,0:T(8,128)(2,1)} %dynamic-slice_bitcast_fusion.4), channel_id=1, source_target_pairs={{0,8},{1,9},{2,10},{3,11},{4,12},{5,13},{6,14},{7,15},{8,0},{9,1},... | collective-permute-start | bytes 2949128 | tf_op jit(solution)/shard_map/ppermute | solution.py:105
  410.6 17.1 %collective-permute-start.39 = (bf16[4,32,1280]{2,1,0:T(8,128)(2,1)S(1)}, bf16[4,32,1280]{2,1,0:T(8,128)(2,1)S(1)}, u32[]{:S(2)}, u32[]{:S(2)}) collective-permute-start(bf16[4,32,1280]{2,1,0:T(8,128)(2,1)S(1)} %dynamic-slice_bitcast_fusion.12), channel_id=1, source_target_pairs={{0,8},{1,9},{2,10},{3,11},{4,12},{5,13},{6,14},{7,15},{8,0},{9,1},... | collective-permute-start | bytes 983048 | tf_op jit(solution)/shard_map/ppermute | solution.py:105
  (106 other events, 614.6 us)

commit v2 on v1

--- a/solution.py
+++ b/solution.py
@@ -3,6 +3,8 @@
 import jax
 import jax.numpy as jnp
 from jax import lax
+from jax.experimental import pallas as pl
+from jax.experimental.pallas import tpu as pltpu
 from jax.sharding import PartitionSpec as P
 
 D = 1280
@@ -23,6 +25,10 @@
 masked_score = -1e30
 
 AXES = ("dp", "fsdp")
+LANES = 128
+MESH = pl.DeviceIdType.MESH
+ANYWHERE = pl.BlockSpec(memory_space=pl.ANY)
+ON_CHIP = pl.BlockSpec(memory_space=pltpu.VMEM)
 
 
 def rms_scale(values, gain):
@@ -123,6 +129,656 @@
             got = self.move(pick(terms, axis, self.dest(step)), step)
             total = total + got.astype(jnp.float32)
         return total
+
+
+def start_all(copies):
+    for copy in copies:
+        copy.start()
+    return copies
+
+
+def weights_kernel(
+    nd,
+    nf,
+    in_ref,
+    out_ref,
+    inner_ref,
+    in_w,
+    out_w,
+    gate_w,
+    upper_x,
+    z_send,
+    z_recv,
+    y_send,
+    y_recv,
+    x_send,
+    x_recv,
+    hop_send,
+    hop_recv,
+    core_send,
+    core_recv,
+    swap_send,
+    swap_recv,
+    gate_send,
+    gate_recv,
+    over_send,
+    over_recv,
+    local_sem,
+):
+    outer = nd // MEMBERS
+    dp = lax.axis_index("dp")
+    z = lax.axis_index("fsdp")
+    y = dp // MEMBERS
+    member = dp % MEMBERS
+    x = member // 2
+    c = member % 2
+
+    def z_peer(step):
+        return (dp, lax.rem(z + step, nf))
+
+    def y_peer(step):
+        return (lax.rem(y + step, outer) * MEMBERS + member, z)
+
+    def in_group(k):
+        return (y * MEMBERS + k, z)
+
+    def from_z(step):
+        return lax.rem(z - step + nf, nf)
+
+    def from_y(step):
+        return lax.rem(y - step + outer, outer)
+
+    x_peer = in_group((1 - x) * 2 + c)
+    core_peer = in_group(x * 2 + 1 - c)
+    barrier = pltpu.get_barrier_semaphore()
+    peers = [z_peer(step) for step in range(1, nf)] + [y_peer(step) for step in range(1, outer)]
+    peers += [x_peer, core_peer, in_group(MEMBERS - 1 - member)]
+    for peer in peers:
+        pl.semaphore_signal(barrier, inc=1, device_id=peer, device_id_type=MESH)
+    pl.semaphore_wait(barrier, len(peers))
+
+    def remote(source, target, send, recv, device):
+        return pltpu.make_async_remote_copy(
+            src_ref=source,
+            dst_ref=target,
+            send_sem=send,
+            recv_sem=recv,
+            device_id=device,
+            device_id_type=MESH,
+        )
+
+    shards_here = (in_ref, out_ref)
+    wholes = (in_w, out_w)
+    sent = []
+
+    def send(copy):
+        copy.start()
+        sent.append(copy)
+        return copy
+
+    local = [
+        pltpu.make_async_copy(shards_here[a], wholes[a].at[y, x, c, z], local_sem.at[a])
+        for a in range(2)
+    ]
+    start_all(local)
+    z_copies = {}
+    for a in range(2):
+        for step in range(1, nf):
+            z_copies[a, step] = send(
+                remote(
+                    shards_here[a],
+                    wholes[a].at[y, x, c, z],
+                    z_send.at[a, step],
+                    z_recv.at[a, step],
+                    z_peer(step),
+                )
+            )
+    masks = (2, 1, 3)
+    trades = {}
+    for half, target in ((0, gate_w.at[y, :, z]), (1, upper_x)):
+        for mask in masks:
+            other = member ^ mask
+            trades[half, mask] = send(
+                remote(
+                    inner_ref.at[half, other],
+                    target.at[member],
+                    swap_send.at[half, mask],
+                    swap_recv.at[half, mask],
+                    in_group(other),
+                )
+            )
+        kept = pltpu.make_async_copy(
+            inner_ref.at[half, member], target.at[member], local_sem.at[2 + half]
+        )
+        kept.start()
+        local.append(kept)
+
+    def block(a, step, oy=None, ox=None):
+        return wholes[a].at[y if oy is None else oy, x if ox is None else ox, c, from_z(step)]
+
+    y_copies = {}
+    x_copies = {}
+    for a in range(2):
+        for step in range(nf):
+            if step:
+                z_copies[a, step].wait_recv()
+            source = shards_here[a] if step == 0 else block(a, step)
+            for hop in range(1, outer):
+                y_copies[a, hop, step] = send(
+                    remote(
+                        source,
+                        block(a, step),
+                        y_send.at[a, hop, step],
+                        y_recv.at[a, hop, step],
+                        y_peer(hop),
+                    )
+                )
+            x_copies[a, step] = send(
+                remote(
+                    source, block(a, step), x_send.at[a, step], x_recv.at[a, step], x_peer
+                )
+            )
+    for mask in masks:
+        trades[0, mask].wait_recv()
+    local[2].wait()
+    gates = {}
+    gate_own = gate_w.at[y, :, z]
+    for step in range(1, nf):
+        gates[step] = send(
+            remote(gate_own, gate_own, gate_send.at[step], gate_recv.at[step], z_peer(step))
+        )
+    for hop in range(1, outer):
+        gates[-hop] = send(
+            remote(gate_own, gate_own, over_send.at[hop], over_recv.at[hop], y_peer(hop))
+        )
+    hops = {}
+    for step in range(nf):
+        x_copies[0, step].wait_recv()
+        for hop in range(1, outer):
+            hops[0, hop, step] = send(
+                remote(
+                    block(0, step, ox=1 - x),
+                    block(0, step, ox=1 - x),
+                    hop_send.at[0, hop, step],
+                    hop_recv.at[0, hop, step],
+                    y_peer(hop),
+                )
+            )
+    for step in range(nf):
+        for hop in range(1, outer):
+            y_copies[1, hop, step].wait_recv()
+            hops[1, hop, step] = send(
+                remote(
+                    block(1, step, oy=from_y(hop)),
+                    block(1, step, oy=from_y(hop)),
+                    hop_send.at[1, hop, step],
+                    hop_recv.at[1, hop, step],
+                    x_peer,
+                )
+            )
+    cores = {}
+
+    def to_core(a, hop, far):
+        place = wholes[a].at[y if hop == 0 else from_y(hop), 1 - x if far else x, c]
+        cores[a, hop, far] = send(
+            remote(
+                place,
+                place,
+                core_send.at[a, hop, far],
+                core_recv.at[a, hop, far],
+                core_peer,
+            )
+        )
+
+    local[0].wait()
+    local[1].wait()
+    for a in range(2):
+        to_core(a, 0, 0)
+    to_core(0, 0, 1)
+    for hop in range(1, outer):
+        for step in range(nf):
+            y_copies[0, hop, step].wait_recv()
+        to_core(0, hop, 0)
+        to_core(1, hop, 0)
+    for step in range(nf):
+        x_copies[1, step].wait_recv()
+    to_core(1, 0, 1)
+    for a in range(2):
+        for hop in range(1, outer):
+            for step in range(nf):
+                hops[a, hop, step].wait_recv()
+            to_core(a, hop, 1)
+    for mask in masks:
+        trades[1, mask].wait_recv()
+    local[3].wait()
+    for key in gates:
+        gates[key].wait_recv()
+    for key in cores:
+        cores[key].wait_recv()
+    for copy in sent:
+        copy.wait_send()
+
+
+def gather_weights(nd, nf, shard_in, shard_out, inner):
+    outer = nd // MEMBERS
+    dma = pltpu.SemaphoreType.DMA
+    lead = (outer, 2, 2, nf)
+    low_type = jnp.bfloat16
+    pairs = [(2, nf), (2, outer, nf), (2, nf), (2, outer, nf), (2, outer, 2), (2, 4), (nf,), (outer,)]
+    moved = 2 * nd * nf * (shard_in.size + shard_out.size)
+    return pl.pallas_call(
+        functools.partial(weights_kernel, nd, nf),
+        name="gather_weights",
+        out_shape=(
+            jax.ShapeDtypeStruct(lead + shard_in.shape, low_type),
+            jax.ShapeDtypeStruct(lead + shard_out.shape, low_type),
+            jax.ShapeDtypeStruct((outer, MEMBERS, nf) + inner.shape[2:], low_type),
+            jax.ShapeDtypeStruct((MEMBERS,) + inner.shape[2:], low_type),
+        ),
+        in_specs=[ANYWHERE] * 3,
+        out_specs=(ANYWHERE,) * 4,
+        scratch_shapes=[dma(shape) for shape in pairs for _ in range(2)] + [dma((4,))],
+        cost_estimate=pl.CostEstimate(flops=0, bytes_accessed=16 * moved, transcendentals=0),
+        compiler_params=pltpu.CompilerParams(collective_id=0, has_side_effects=True),
+    )(shard_in, shard_out, inner)
+
+
+def totals_kernel(nd, nf, part_ref, square_ref, all_ref, pieces, own, p_send, p_recv, q_send, q_recv):
+    total = nd * nf
+    dp = lax.axis_index("dp")
+    z = lax.axis_index("fsdp")
+    me = dp * nf + z
+
+    def device(step):
+        index = lax.rem(me + step, total)
+        return index, (index // nf, lax.rem(index, nf))
+
+    barrier = pltpu.get_barrier_semaphore()
+
+    def greet(step, carry):
+        pl.semaphore_signal(barrier, inc=1, device_id=device(step)[1], device_id_type=MESH)
+        return carry
+
+    lax.fori_loop(1, total, greet, 0)
+    pl.semaphore_wait(barrier, total - 1)
+
+    def part(step):
+        index, there = device(step)
+        return pltpu.make_async_remote_copy(
+            src_ref=part_ref.at[index],
+            dst_ref=pieces.at[me],
+            send_sem=p_send.at[step],
+            recv_sem=p_recv.at[step],
+            device_id=there,
+            device_id_type=MESH,
+        )
+
+    def share(step):
+        _, there = device(step)
+        return pltpu.make_async_remote_copy(
+            src_ref=own,
+            dst_ref=all_ref.at[me],
+            send_sem=q_send.at[step],
+            recv_sem=q_recv.at[step],
+            device_id=there,
+            device_id_type=MESH,
+        )
+
+    def begin(make):
+        def step_once(step, carry):
+            make(step).start()
+            return carry
+
+        lax.fori_loop(1, total, step_once, 0)
+
+    def finish(make):
+        def step_once(step, carry):
+            make(step).wait()
+            return carry
+
+        lax.fori_loop(1, total, step_once, 0)
+
+    begin(part)
+    pieces[me] = part_ref[me]
+    finish(part)
+    summed = jnp.sum(pieces[...], 0)
+    own[...] = jnp.concatenate([summed[:1], square_ref[...]], 0)
+    begin(share)
+    all_ref[me] = own[...]
+    finish(share)
+
+
+def all_totals(nd, nf, parts, square):
+    total = nd * nf
+    parts = jnp.pad(parts[:, None, :], ((0, 0), (0, 7), (0, 0)))
+    square = jnp.broadcast_to(square, (7, LANES))
+    dma = pltpu.SemaphoreType.DMA
+    result = pl.pallas_call(
+        functools.partial(totals_kernel, nd, nf),
+        name="all_totals",
+        out_shape=jax.ShapeDtypeStruct((total, 8, LANES), jnp.float32),
+        in_specs=[ON_CHIP] * 2,
+        out_specs=ON_CHIP,
+        scratch_shapes=[
+            pltpu.VMEM((total, 8, LANES), jnp.float32),
+            pltpu.VMEM((8, LANES), jnp.float32),
+        ]
+        + [dma((total,))] * 4,
+        compiler_params=pltpu.CompilerParams(collective_id=1, has_side_effects=True),
+    )(parts, square)
+    return result[:, 0], jnp.sum(result[:, 1, 0])
+
+
+def block_mean():
+    row = lax.broadcasted_iota(jnp.int32, (LANES, LANES), 0) // HD
+    column = lax.broadcasted_iota(jnp.int32, (LANES, LANES), 1) // HD
+    return jnp.where(row == column, 1.0 / HD, 0.0)
+
+
+def head_mean(values, averages):
+    return jnp.dot(
+        values, averages, preferred_element_type=jnp.float32, precision=lax.Precision.HIGHEST
+    )
+
+
+def swap_halves(values):
+    lane = lax.broadcasted_iota(jnp.int32, values.shape, 1) // (HD // 2)
+    ahead = pltpu.roll(values, LANES - HD // 2, 1)
+    behind = pltpu.roll(values, HD // 2, 1)
+    return jnp.where(lane % 2 == 0, ahead, behind)
+
+
+def in_half(values, source, target):
+    lane = lax.broadcasted_iota(jnp.int32, values.shape, 1) // HD
+    wide = values.astype(jnp.float32)
+    if source != target:
+        wide = pltpu.roll(wide, HD, 1)
+    return jnp.where(lane == target, wide, 0.0).astype(values.dtype)
+
+
+def tile_of(index, width=LANES):
+    return pl.ds(pl.multiple_of(index * width, LANES), width)
+
+
+def rows_of(index, size):
+    return pl.ds(pl.multiple_of(index * size, 16), size)
+
+
+def dot_last(left, right):
+    return lax.dot_general(
+        left, right, (((1,), (1,)), ((), ())), preferred_element_type=jnp.float32
+    )
+
+
+def probabilities(query, key, keep):
+    scores = dot_last(query, key) * HD**-0.5
+    scores = jnp.where(keep, scores, masked_score)
+    weights = jnp.exp(scores - jnp.max(scores, -1, keepdims=True))
+    return weights / jnp.sum(weights, -1, keepdims=True)
+
+
+def attend_kernel(
+    nd,
+    nf,
+    length,
+    tokens,
+    in_w,
+    out_w,
+    gain_attn,
+    gain_ffn,
+    gain_heads,
+    cosine,
+    sine,
+    mask,
+    cot,
+    gate_in,
+    upper_x,
+    down_x,
+    gate_w,
+    upper_w,
+    down_w,
+    back_all,
+    ffn_all,
+    raw,
+    heads,
+    values,
+    mixed,
+    hidden_in,
+    normed,
+    ffn_in,
+    gate_send,
+    gate_recv,
+    uz_send,
+    uz_recv,
+    uy_send,
+    uy_recv,
+    dz_send,
+    dz_recv,
+    dy_send,
+    dy_recv,
+    row_send,
+    row_recv,
+    local_sem,
+):
+    outer = nd // MEMBERS
+    dp = lax.axis_index("dp")
+    z = lax.axis_index("fsdp")
+    y = dp // MEMBERS
+    member = dp % MEMBERS
+    x = member // 2
+    c = member % 2
+
+    def z_peer(step):
+        return (dp, lax.rem(z + step, nf))
+
+    def y_peer(step):
+        return (lax.rem(y + step, outer) * MEMBERS + member, z)
+
+    def from_z(step):
+        return lax.rem(z - step + nf, nf)
+
+    x_peer = (y * MEMBERS + (1 - x) * 2 + c, z)
+    core_peer = (y * MEMBERS + x * 2 + 1 - c, z)
+    barrier = pltpu.get_barrier_semaphore()
+    peers = [z_peer(step) for step in range(1, nf)] + [y_peer(step) for step in range(1, outer)]
+    peers += [x_peer, core_peer]
+    for peer in peers:
+        pl.semaphore_signal(barrier, inc=1, device_id=peer, device_id_type=MESH)
+    pl.semaphore_wait(barrier, len(peers))
+    sent = []
+
+    def remote(source, target, send, recv, device):
+        copy = pltpu.make_async_remote_copy(
+            src_ref=source,
+            dst_ref=target,
+            send_sem=send,
+            recv_sem=recv,
+            device_id=device,
+            device_id_type=MESH,
+        )
+        copy.start()
+        sent.append(copy)
+        return copy
+
+    def keep(index, source, target):
+        copy = pltpu.make_async_copy(source, target, local_sem.at[index])
+        copy.start()
+        return copy
+
+    arrivals = []
+    for step in range(1, nf):
+        piece = gate_w.at[y, :, from_z(step)]
+        for hop in range(1, outer):
+            arrivals.append(
+                remote(piece, piece, gate_send.at[hop, step], gate_recv.at[hop, step], y_peer(hop))
+            )
+    upper_own = upper_w.at[y, :, z]
+    down_own = down_w.at[y, z]
+    upper_z = [
+        remote(upper_x, upper_own, uz_send.at[step], uz_recv.at[step], z_peer(step))
+        for step in range(1, nf)
+    ]
+    for hop in range(1, outer):
+        arrivals.append(
+            remote(upper_x, upper_own, uy_send.at[hop, 0], uy_recv.at[hop, 0], y_peer(hop))
+        )
+    kept = [keep(0, upper_x, upper_own), keep(1, down_x, down_own), keep(2, cot, back_all.at[0])]
+    cot_near = remote(cot, back_all.at[1], row_send.at[0], row_recv.at[0], core_peer)
+    cot_far = remote(cot, back_all.at[2], row_send.at[1], row_recv.at[1], x_peer)
+
+    count = tokens.shape[0]
+    width = tokens.shape[1]
+    chunk = 32
+
+    def norm_rows(index, carry):
+        rows = rows_of(index, chunk)
+        part = tokens[rows, :].astype(jnp.float32)
+        scale = lax.rsqrt(jnp.mean(part * part, -1, keepdims=True) + norm_eps)
+        normed[rows, :] = (part * scale * gain_attn[...]).astype(jnp.bfloat16)
+        return carry
+
+    lax.fori_loop(0, count // chunk, norm_rows, 0)
+    head_tiles = (HQ + KV) * HD // LANES
+
+    def project(index, carry):
+        columns = tile_of(index, 2 * LANES)
+        raw[:, columns] = jnp.dot(
+            normed[...], in_w[:, columns], preferred_element_type=jnp.float32
+        )
+        return carry
+
+    lax.fori_loop(0, head_tiles // 2, project, 0)
+    values[...] = jnp.dot(
+        normed[...], in_w[:, pl.ds(head_tiles * LANES, KV * HD)], preferred_element_type=jnp.float32
+    ).astype(jnp.bfloat16)
+    averages = block_mean()
+
+    def turn(index, carry):
+        columns = tile_of(index)
+        for row in range(count // length):
+            rows = pl.ds(row * length, length)
+            part = raw[rows, columns]
+            scale = lax.rsqrt(head_mean(part * part, averages) + norm_eps)
+            part = part * scale * gain_heads[:, columns]
+            part = part * cosine[...] + swap_halves(part) * sine[...]
+            heads[rows, columns] = part.astype(jnp.bfloat16)
+        return carry
+
+    lax.fori_loop(0, head_tiles, turn, 0)
+
+    def attend(row):
+        rows = pl.ds(row * length, length)
+        allowed = mask[row] > 0.5
+
+        def pair(tile, carry):
+            key_tile = heads[rows, tile_of(HQ * HD // LANES + tile)]
+            value_tile = values[rows, tile_of(tile)]
+            for own in range(2):
+                key = [in_half(key_tile, own, half) for half in range(2)]
+                value = [in_half(value_tile, own, half) for half in range(2)]
+                for quarter in range(2):
+                    columns = tile_of(tile * 4 + own * 2 + quarter)
+                    query = heads[rows, columns]
+                    total = None
+                    for half in range(2):
+                        weights = probabilities(query, key[half], allowed).astype(jnp.bfloat16)
+                        term = jnp.dot(weights, value[half], preferred_element_type=jnp.float32)
+                        total = term if total is None else total + term
+                    mixed[rows, columns] = total.astype(jnp.bfloat16)
+            return carry
+
+        lax.fori_loop(0, KV * HD // LANES, pair, 0)
+
+    for row in range(count // length):
+        attend(row)
+
+    def project_out(index, carry):
+        columns = tile_of(index, 2 * LANES)
+        hidden_in[:, columns] = tokens[:, columns].astype(jnp.float32) + jnp.dot(
+            mixed[...], out_w[:, columns], preferred_element_type=jnp.float32
+        )
+        return carry
+
+    lax.fori_loop(0, width // (2 * LANES), project_out, 0)
+
+    def norm_hidden(index, carry):
+        rows = rows_of(index, chunk)
+        part = hidden_in[rows, :]
+        scale = lax.rsqrt(jnp.mean(part * part, -1, keepdims=True) + norm_eps)
+        ffn_in[rows, :] = (part * scale * gain_ffn[...]).astype(jnp.bfloat16)
+        return carry
+
+    lax.fori_loop(0, count // chunk, norm_hidden, 0)
+    ffn_far = remote(ffn_in, ffn_all.at[2], row_send.at[3], row_recv.at[3], x_peer)
+    ffn_near = remote(ffn_in, ffn_all.at[1], row_send.at[4], row_recv.at[4], core_peer)
+    kept.append(keep(3, ffn_in, ffn_all.at[0]))
+
+    cot_far.wait_recv()
+    cot_cross = remote(back_all.at[2], back_all.at[3], row_send.at[2], row_recv.at[2], core_peer)
+    for step in range(1, nf):
+        upper_z[step - 1].wait_recv()
+        piece = upper_w.at[y, :, from_z(step)]
+        for hop in range(1, outer):
+            arrivals.append(
+                remote(piece, piece, uy_send.at[hop, step], uy_recv.at[hop, step], y_peer(hop))
+            )
+    down_z = [
+        remote(down_x, down_own, dz_send.at[step], dz_recv.at[step], z_peer(step))
+        for step in range(1, nf)
+    ]
+    for hop in range(1, outer):
+        arrivals.append(
+            remote(down_x, down_own, dy_send.at[hop, 0], dy_recv.at[hop, 0], y_peer(hop))
+        )
+    ffn_far.wait_recv()
+    ffn_cross = remote(ffn_all.at[2], ffn_all.at[3], row_send.at[5], row_recv.at[5], core_peer)
+    for step in range(1, nf):
+        down_z[step - 1].wait_recv()
+        piece = down_w.at[y, from_z(step)]
+        for hop in range(1, outer):
+            arrivals.append(
+                remote(piece, piece, dy_send.at[hop, step], dy_recv.at[hop, step], y_peer(hop))
+            )
+    for copy in arrivals + [cot_near, cot_cross, ffn_near, ffn_cross]:
+        copy.wait_recv()
+    for copy in sent:
+        copy.wait_send()
+    for copy in kept:
+        copy.wait()
+
+
+def attend(nd, nf, length, tokens, in_w, out_w, small, cot, gate_w, upper_x, down_x):
+    outer = nd // MEMBERS
+    count, width = tokens.shape
+    lo, hi = jnp.bfloat16, jnp.float32
+    dma = pltpu.SemaphoreType.DMA
+    moves = [(outer, nf), (nf,), (outer, nf), (nf,), (outer, nf), (6,)]
+    shapes = [
+        (gate_w.shape, lo),
+        (gate_w.shape, lo),
+        ((outer, nf) + down_x.shape, lo),
+        ((MEMBERS, count, width), lo),
+        ((MEMBERS, count, width), lo),
+        ((count, (HQ + KV) * HD), hi),
+        ((count, (HQ + KV) * HD), lo),
+        ((count, KV * HD), lo),
+        ((count, HQ * HD), lo),
+        ((count, width), hi),
+    ]
+    return pl.pallas_call(
+        functools.partial(attend_kernel, nd, nf, length),
+        name="attend",
+        out_shape=tuple(jax.ShapeDtypeStruct(*item) for item in shapes),
+        in_specs=[ON_CHIP] * 9 + [ANYWHERE] * 4,
+        out_specs=(ANYWHERE,) * 5 + (ON_CHIP,) * 5,
+        input_output_aliases={10: 0},
+        scratch_shapes=[pltpu.VMEM((count, width), lo), pltpu.VMEM((count, width), lo)]
+        + [dma(shape) for shape in moves for _ in range(2)]
+        + [dma((4,))],
+        compiler_params=pltpu.CompilerParams(
+            collective_id=2, has_side_effects=True, vmem_limit_bytes=40 * 2**20
+        ),
+    )(tokens, in_w, out_w, *small, cot, gate_w, upper_x, down_x)
 
 
 def after(value, *others):
@@ -191,11 +847,17 @@
         return full
 
     def spread(rows):
-        return ring_core.gather(ring_x.gather(rows, 0), 1)
-
-    def collapse(terms):
-        half = low(ring_core.reduce(terms, 1))
-        return ring_x.reduce(half, 0)
+        far = ring_x.move(rows, 1)
+        near = jnp.concatenate([rows, ring_core.move(rows, 1)], 0)
+        return near, jnp.concatenate([far, ring_core.move(far, 1)], 0)
+
+    def collapse(near, far):
+        rows = near.shape[0] // 2
+        got = ring_core.move(far[rows:], 1).astype(jnp.float32)
+        got = ring_x.move(low(far[:rows].astype(jnp.float32) + got), 1)
+        total = near[:rows].astype(jnp.float32)
+        total = total + ring_core.move(near[rows:], 1).astype(jnp.float32)
+        return total + got.astype(jnp.float32)
 
     batch, length, width = tokens.shape
     count = batch * length
@@ -209,37 +871,16 @@
 
     shard_in = jnp.concatenate([low(w_query), low(w_key), low(w_value)], 1)
     shard_out = low(w_out)
-    in_z = ring_z.gather(shard_in, 0)
-    out_z = ring_z.gather(shard_out, 0)
-    in_xy = ring_x.gather(ring_y.gather(in_z, 0), 1)
-    out_xy = ring_y.gather(ring_x.gather(out_z, 0), 0)
-    in_w = ring_core.gather(in_xy, 2).reshape(D, attn_cols)
-    out_w = ring_core.gather(out_xy, 2).reshape(HQ * HD, D)
 
     def member_columns(weight):
-        return low(weight).reshape(in_rows, outer, MEMBERS, span).transpose(2, 0, 1, 3)
-
-    columns = jnp.concatenate(
-        [
-            member_columns(w_gate).reshape(MEMBERS, in_rows, mine),
-            member_columns(w_up).reshape(MEMBERS, in_rows, mine),
-        ],
-        2,
-    )
-    inner = swap(columns)
-    inner = after(inner, in_z, out_z)
-    inner_z = ring_z.gather(inner, 1)
-    inner_w = ring_y.gather(inner_z, 0).reshape(D, 2 * mine)
-    shard_down = after(low(w_down), inner_z)
-    down_z = ring_z.gather(shard_down, 0)
-    down_w = ring_y.gather(down_z, 0).reshape(mine, D)
-
-    back_in = cotangent.reshape(count, width)
-    back_all = spread(after(back_in, in_xy)).reshape(MEMBERS * count, width)
-
-    cosine, sine = rotary_tables(length, HD)
-    scale = HD ** (-0.5)
-    group_size = HQ // KV
+        cut = low(weight).reshape(in_rows, outer, MEMBERS, span).transpose(2, 0, 1, 3)
+        return cut.reshape(MEMBERS, in_rows, mine)
+
+    columns = jnp.stack([member_columns(w_gate), member_columns(w_up)])
+    in_w, out_w, gate_w, upper_x = gather_weights(nd, nf, shard_in, shard_out, columns)
+    in_w = in_w.reshape(D, attn_cols)
+    out_w = out_w.reshape(HQ * HD, D)
+
     gain_attn = gains[:D]
     gain_ffn = gains[D : 2 * D]
     gain_query = gains[2 * D : 2 * D + HD]
@@ -247,54 +888,90 @@
     positions = jnp.arange(length)
     causal = positions[None, :] <= positions[:, None]
     allowed = causal[None] & (segment_ids[:, :, None] == segment_ids[:, None, :])
-    allowed = allowed[:, None, None]
+    cosine, sine = rotary_tables(length, HD)
+    scale = HD ** (-0.5)
+    group_size = HQ // KV
+    small = (
+        gain_attn[None],
+        gain_ffn[None],
+        jnp.concatenate([jnp.tile(gain_query, HQ), jnp.tile(gain_key, KV)])[None],
+        jnp.tile(cosine, (1, 2 * LANES // HD)),
+        jnp.tile(jnp.concatenate([-sine, sine], 1), (1, LANES // HD)),
+        allowed.astype(jnp.float32),
+    )
+    back_in = cotangent.reshape(count, width)
+    token_rows = tokens.reshape(count, width)
+    (
+        gate_w,
+        upper_w,
+        down_w,
+        back_all,
+        ffn_all,
+        raw,
+        heads,
+        values,
+        mixed,
+        hidden_in,
+    ) = attend(
+        nd, nf, length, token_rows, in_w, out_w, small, back_in, gate_w, upper_x, low(w_down)
+    )
+    gate_w = gate_w.reshape(D, mine)
+    upper_w = upper_w.reshape(D, mine)
+    down_w = down_w.reshape(mine, D)
+    back_all = back_all.reshape(MEMBERS * count, width)
+    ffn_all = ffn_all.reshape(MEMBERS * count, width)
+    back_halves = (back_all[: 2 * count], back_all[2 * count :])
+    ffn_halves = (ffn_all[: 2 * count], ffn_all[2 * count :])
+    query_raw = raw[:, : HQ * HD]
+    key_raw = raw[:, HQ * HD :]
+    queries = heads[:, : HQ * HD].reshape(batch, length, KV, group_size, HD)
+    keys = heads[:, HQ * HD :].reshape(batch, length, KV, HD)
+    values = values.reshape(batch, length, KV, HD)
 
     def piece(raw, gain):
         return head_norm(raw.reshape(batch, length, -1), gain, cosine, sine)
 
-    inputs = tokens.reshape(count, width).astype(jnp.float32)
+    gates = [forward_product(half, gate_w) for half in ffn_halves]
+    uppers = [forward_product(half, upper_w) for half in ffn_halves]
+    hiddens = [low(swiglu(gate, upper)) for gate, upper in zip(gates, uppers)]
+    down_terms = low(weight_product(jnp.concatenate(hiddens, 0), back_all))
+    down_terms = down_terms.reshape(outer, nf, hidden_rows, width)
+    down_sum = ring_z.reduce(low(ring_y.reduce(down_terms, 0)), 0)
+
+    def inner_grads(half):
+        grad_hidden = back_product(back_halves[half], down_w)
+        _, pull = jax.vjp(swiglu, gates[half], uppers[half])
+        grad_gate, grad_upper = pull(grad_hidden)
+        grad_gate, grad_upper = low(grad_gate), low(grad_upper)
+        back = back_product(grad_gate, gate_w) + back_product(grad_upper, upper_w)
+        return grad_gate, grad_upper, low(back)
+
+    far_gate, far_upper, far_ffn = inner_grads(1)
+    near_gate, near_upper, near_ffn = inner_grads(0)
+    grad_ffn = collapse(near_ffn, far_ffn)
+
+    def inner_reduce(near, far):
+        terms = low(weight_product(ffn_all, jnp.concatenate([near, far], 0)))
+        terms = terms.reshape(outer, MEMBERS, nf, in_rows, mine)
+        total = ring_z.reduce(low(ring_y.reduce(terms, 0)), 1)
+        total = swap(low(total)).astype(jnp.float32)
+        total = total.reshape(MEMBERS, in_rows, outer, span).transpose(1, 2, 0, 3)
+        return total.reshape(in_rows, hidden_all)
+
+    gate_sum = inner_reduce(near_gate, far_gate)
+    upper_sum = inner_reduce(near_upper, far_upper)
+    down_out = [low(forward_product(after(half, grad_ffn), down_w)) for half in hiddens]
+    output = low(hidden_in + collapse(*down_out))
+
+    inputs = token_rows.astype(jnp.float32)
     normed = low(rms_scale(inputs, gain_attn))
-    raw = forward_product(normed, in_w)
-    query_raw = raw[:, : HQ * HD]
-    key_raw = raw[:, HQ * HD : (HQ + KV) * HD]
-    values = low(raw[:, (HQ + KV) * HD :]).reshape(batch, length, KV, HD)
-    queries = low(piece(query_raw, gain_query)).reshape(batch, length, KV, group_size, HD)
-    keys = low(piece(key_raw, gain_key))
     scores = (
         jnp.einsum("blkrd,bmkd->bkrlm", queries, keys, preferred_element_type=jnp.float32) * scale
     )
-    scores = jnp.where(allowed, scores, masked_score)
-    top = jnp.max(scores, -1, keepdims=True)
-    weights = jnp.exp(scores - top)
+    scores = jnp.where(allowed[:, None, None], scores, masked_score)
+    weights = jnp.exp(scores - jnp.max(scores, -1, keepdims=True))
     attention_full = weights / jnp.sum(weights, -1, keepdims=True)
     attention = low(attention_full)
-    mixed = jnp.einsum("bkrlm,bmkd->blkrd", attention, values, preferred_element_type=jnp.float32)
-    mixed = low(mixed.reshape(count, HQ * HD))
-    hidden_in = inputs + forward_product(mixed, out_w)
-
-    ffn_all = spread(low(rms_scale(hidden_in, gain_ffn))).reshape(MEMBERS * count, width)
-    inner_out = forward_product(ffn_all, inner_w)
-    gate = inner_out[:, :mine]
-    upper = inner_out[:, mine:]
-    hidden = low(swiglu(gate, upper))
-    down_terms = low(weight_product(hidden, back_all)).reshape(outer, nf, hidden_rows, width)
-    down_sum = ring_z.reduce(low(ring_y.reduce(down_terms, 0)), 0)
-    grad_hidden = back_product(back_all, down_w)
-    _, swiglu_pull = jax.vjp(swiglu, gate, upper)
-    grad_gate, grad_upper = swiglu_pull(grad_hidden)
-    grad_inner = jnp.concatenate([low(grad_gate), low(grad_upper)], 1)
-    grad_ffn_terms = low(back_product(grad_inner, inner_w)).reshape(2, 2, count, width)
-    grad_ffn = collapse(grad_ffn_terms)
-    inner_terms = low(weight_product(ffn_all, grad_inner)).reshape(
-        outer, MEMBERS, nf, in_rows, 2 * mine
-    )
-    inner_sum = ring_z.reduce(low(ring_y.reduce(inner_terms, 0)), 1)
-    inner_sum = swap(low(inner_sum)).astype(jnp.float32)
-    inner_sum = inner_sum.reshape(MEMBERS, in_rows, 2, outer, span).transpose(2, 1, 3, 0, 4)
-    inner_sum = inner_sum.reshape(2, in_rows, hidden_all)
-    down_out = low(forward_product(hidden, down_w)).reshape(2, 2, count, width)
-    output = low(hidden_in + collapse(down_out))
-
     _, ffn_pull = jax.vjp(rms_scale, hidden_in, gain_ffn)
     grad_hidden_in, grad_gain_ffn = ffn_pull(grad_ffn)
     grad_hidden_in = grad_hidden_in + back_in.astype(jnp.float32)
@@ -347,18 +1024,23 @@
         in_sum[:, HQ * HD : (HQ + KV) * HD],
         in_sum[:, (HQ + KV) * HD :],
         out_sum,
-        inner_sum[0],
-        inner_sum[1],
+        gate_sum,
+        upper_sum,
         down_sum,
     )
     local_squares = (
         jnp.sum(in_sum * in_sum)
         + jnp.sum(out_sum * out_sum)
-        + jnp.sum(inner_sum * inner_sum)
+        + jnp.sum(gate_sum * gate_sum)
+        + jnp.sum(upper_sum * upper_sum)
         + jnp.sum(down_sum * down_sum)
     )
-    gain_total = lax.psum(gain_terms, AXES)
-    square_total = lax.psum(local_squares, AXES)
+    gain_size = gains.shape[0]
+    share = -(-gain_size // (nd * nf))
+    gain_terms = jnp.pad(gain_terms, (0, share * nd * nf - gain_size)).reshape(nd * nf, share)
+    gain_terms = jnp.pad(gain_terms, ((0, 0), (0, LANES - share)))
+    gain_total, square_total = all_totals(nd, nf, gain_terms, local_squares)
+    gain_total = gain_total[:, :share].reshape(-1)[:gain_size]
     total_norm = jnp.sqrt(square_total + jnp.sum(gain_total * gain_total))
     factor = jnp.minimum(1.0, clip_limit / (total_norm + 1e-06))
     clipped = tuple((share * factor for share in reduced))

time: 520 us -> 483 us (0.929)
  Pallas kernels: 0 us -> 135 us
  waiting for transfers between devices: 173 us -> 99.8 us
  blocking collectives: 40.3 us -> 0 us
  starting transfers between devices: 75.8 us -> 37.2 us
  local copies, waits for them, and re-layouts: 91.4 us -> 76.6 us
  other arithmetic: 66.2 us -> 56.7 us
  matrix products: 56.3 us -> 62.4 us
    pallas_call x0 -> x3, Pallas kernels: none -> 135 us  [the longest x1 69 us: attend(): pl.pallas_call(functools.partial(attend_kernel, nd, nf, length), name='at...]
    ppermute x54 -> x36, waiting for transfers between devices: 173 us -> 99.8 us  [move(): return lax.ppermute(block, AXES, pairs)]
    psum x1 -> x0, blocking collectives: 40.3 us -> none  [shards(): square_total = lax.psum(local_squares, AXES)]
    ppermute x54 -> x36, starting transfers between devices: 75.8 us -> 37.2 us  [move(): return lax.ppermute(block, AXES, pairs)]
    dynamic_update_slice x43 -> x6, local copies, waits for them, and re-layouts: 22.6 us -> 0.89 us  [put(): return lax.dynamic_update_index_in_dim(buffer, block, index, axis)]
    reshape x3 -> x7, local copies, waits for them, and re-layouts: 2.08 us -> 16.2 us  [the longest x2 7.97 us: shards(): queries = heads[:, :HQ * HD].reshape(batch, length, KV, group_size, HD)]
    slice x5 -> x12, local copies, waits for them, and re-layouts: 3.19 us -> 16.8 us  [the longest x1 7.66 us: shards(): back_halves = (back_all[:2 * count], back_all[2 * count:])]
    convert_element_type x27 -> x30, other arithmetic: 37.4 us -> 28.9 us  [low(): return value.astype(jnp.bfloat16)]
  transfers between devices with their start and end apart: 54 -> 36, of which waited for: 20 -> 13; matrix products, arithmetic and copies ran while one was open for 33% -> 27% of each run, Pallas kernels for 0% -> 0%
where the time goes in v2:
time: 483 us; the launch traced here: 477 us
  Pallas kernels  135 us (28%)
  waiting for transfers between devices  99.8 us (21%)
  local copies, waits for them, and re-layouts  76.6 us (16%)
  matrix products  62.4 us (13%)
  other arithmetic  56.7 us (12%)
  starting transfers between devices  37.2 us (8%)
  between operations  8.94 us (2%)
    ppermute x36, waiting for transfers between devices, move(): return lax.ppermute(block, AXES, pairs)  99.8 us
    pallas_call x1, Pallas kernels, attend(): pl.pallas_call(functools.partial(attend_kernel, nd, nf, length), name='at...  69 us
    pallas_call x1, Pallas kernels, gather_weights(): pl.pallas_call(functools.partial(weights_kernel, nd, nf), name='gather_we...  48.7 us
    ppermute x36, starting transfers between devices, move(): return lax.ppermute(block, AXES, pairs)  37.2 us
    convert_element_type x30, other arithmetic, low(): return value.astype(jnp.bfloat16)  28.9 us
    pallas_call x1, Pallas kernels, all_totals(): pl.pallas_call(functools.partial(totals_kernel, nd, nf), name='all_totals...  17.7 us
    dot_general x8, matrix products, back_product(): lax.dot_general(left, right, (((1,), (1,)), ((), ())), preferred_element_...  17.2 us
    dot_general x5, matrix products, weight_product(): lax.dot_general(left, right, (((0,), (0,)), ((), ())), preferred_element_...  15.1 us
  transfers between devices with their start and end apart: 36, of which 13 were waited for; matrix products, arithmetic and copies ran while one was open for 27% of the time, Pallas kernels for 0%

profile of v2, /device:TPU:0, one launch (start us, length us, event | category | flops | bytes accessed | tf_op | source)
XLA Modules:
  0.0 477.1 jit_solution(11607258519406823182)
XLA Ops:
  10.3 48.7 %gather_weights.1 = (bf16[2,2,2,4,40,1536]{5,4,3,2,1,0:T(8,128)(2,1)}, bf16[2,2,2,4,32,1280]{5,4,3,2,1,0:T(8,128)(2,1)}, bf16[2,4,4,40,768]{4,3,2,1,0:T(8,128)(2,1)}, bf16[4,40,768]{2,1,0:T(8,128)(2,1)}) custom-call(bf16[40,1536]{1,0:T(8,128)(2,1)} %pad_maximum_fusion.1.in_ref, bf16[32,1280]{1,0:T(8,128)(2,1)} %convert_element_type.379.out_ref, ...), custom_call_target="tpu_custom_call" | custom-call | bytes 104857600 | tf_op jit(solution)/shard_map/gather_weights/pallas_call | solution.py:369
  64.3 69.0 %attend.1 = (bf16[2,4,4,40,768]{4,3,2,1,0:T(8,128)(2,1)S(1)}, bf16[2,4,4,40,768]{4,3,2,1,0:T(8,128)(2,1)S(1)}, bf16[2,4,96,1280]{3,2,1,0:T(8,128)(2,1)S(1)}, bf1...) custom-call(bf16[320,1280]{1,0:T(8,128)(2,1)S(1)} %bitcast.266, ...), custom_call_target="tpu_custom_call", output_to_operand_aliasing={{0}: (10, {})} | custom-call | tf_op jit(solution)/shard_map/attend/pallas_call | solution.py:768
  133.4 7.7 %fusion.129 = (bf16[2,320,1280]{2,1,0:T(8,128)(2,1)S(1)}, bf16[2,320,1280]{2,1,0:T(8,128)(2,1)}, bf16[2,320,1280]{2,1,0:T(8,128)(2,1)S(1)}, bf16[2,320,1280]{2,1,0:T(8,128)(2,1)S(1)}) fusion(bf16[4,320,1280]{2,1,0:T(8,128)(2,1)} %get-tuple-element.58, bf16[4,320,1280]{2,1,0:T(8,128)(2,1)} %get-tuple-element.55), kind=kLoop, calls=%fused_computation.273 | loop fusion | bytes 13107200 | tf_op jit(solution)/shard_map/slice | solution.py:923
  149.5 3.6 multiply_convert_fusion.3
  153.2 6.7 %multiply_convert_fusion.1 = (bf16[640,768]{1,0:T(8,128)(2,1)}, bf16[640,768]{1,0:T(8,128)(2,1)}, bf16[640,768]{1,0:T(8,128)(2,1)S(1)}) fusion(f32[640,768]{1,0:T(8,128)} %fusion.143, f32[640,768]{1,0:T(8,128)} %fusion.142, bf16[640,1280]{1,0:T(8,128)(2,1)} %bitcast.302, bf16[768,1280]{1,0:T(8,128)(2,1)} %bitcast.275), kind=kOutput, calls=%fused_computation.69 | convolution fusion | flops 1266155520 | bytes 10485760 | tf_op jit(solution)/shard_map/dot_general | solution.py:75
  166.5 5.5 %convolution_convert_fusion.3 = bf16[1280,768]{1,0:T(8,128)(2,1)S(1)} fusion(bf16[1280,1280]{1,0:T(8,128)(2,1)} %bitcast.288, bf16[640,768]{1,0:T(8,128)(2,1)} %get-tuple-element.110, bf16[640,768]{1,0:T(8,128)(2,1)} %get-tuple-element.109), kind=kOutput, calls=%fused_computation.16 | convolution fusion | flops 2521497600 | bytes 7208960 | tf_op jit(solution)/shard_map/dot_general | solution.py:69
  175.4 2.8 convolution_convert_fusion.4
  194.9 4.1 reshape.404
  199.0 3.8 copy.286
  212.2 2.9 copy.295
  215.2 4.1 reshape.373
  222.5 6.1 %fusion.134 = (f32[2,4,4,160]{3,2,1,0:T(4,128)}, f32[2,4,4,160,160]{3,4,2,1,0:T(8,128)}) fusion(pred[2,160,160]{1,2,0:T(8,128)(4,1)S(1)} %copy-done.93, bf16[2,160,4,4,64]{1,4,3,2,0:T(8,128)(2,1)} %copy.286, bf16[2,160,4,64,1]{1,0,3,2,4:T(2,128)(2,1)} %bitcast.308), kind=kOutput, calls=%fused_computation.278 | convolution fusion | flops 108134560 | bytes 4167680 | tf_op jit(solution)/shard_map/sub | solution.py:972
  244.2 3.6 collective-permute-done.26
  247.9 17.3 %collective-permute-done.27 = bf16[4,40,768]{2,1,0:T(8,128)(2,1)S(1)} collective-permute-done((bf16[4,40,768]{2,1,0:T(8,128)(2,1)S(1)}, bf16[4,40,768]{2,1,0:T(8,128)(2,1)S(1)}, u32[]{:S(2)}, u32[]{:S(2)}) %collective-permute-start.27) | collective-permute-done | bytes 245792 | tf_op jit(solution)/shard_map/ppermute | solution.py:111
  265.1 3.4 collective-permute-start.21
  268.7 7.5 %collective-permute-start.33 = (bf16[96,1280]{1,0:T(8,128)(2,1)S(1)}, bf16[96,1280]{1,0:T(8,128)(2,1)S(1)}, u32[]{:S(2)}, u32[]{:S(2)}) collective-permute-start(bf16[96,1280]{1,0:T(8,128)(2,1)S(1)} %get-tuple-element.127), channel_id=1, source_target_pairs={{0,1},{1,2},{2,3},{3,0},{4,5},{5,6},{6,7},{7,4},{8,9},{9,10},{10,1... | collective-permute-start | bytes 737288 | tf_op jit(solution)/shard_map/ppermute | solution.py:111
  276.2 10.0 %collective-permute-done.20 = bf16[4,40,768]{2,1,0:T(8,128)(2,1)S(1)} collective-permute-done((bf16[4,40,768]{2,1,0:T(8,128)(2,1)S(1)}, bf16[4,40,768]{2,1,0:T(8,128)(2,1)S(1)}, u32[]{:S(2)}, u32[]{:S(2)}) %collective-permute-start.20) | collective-permute-done | bytes 245792 | tf_op jit(solution)/shard_map/ppermute | solution.py:111
  287.3 12.1 %collective-permute-done.34 = bf16[96,1280]{1,0:T(8,128)(2,1)S(1)} collective-permute-done((bf16[96,1280]{1,0:T(8,128)(2,1)S(1)}, bf16[96,1280]{1,0:T(8,128)(2,1)S(1)}, u32[]{:S(2)}, u32[]{:S(2)}) %collective-permute-start.34) | collective-permute-done | bytes 245792 | tf_op jit(solution)/shard_map/ppermute | solution.py:111
  300.0 3.9 collective-permute-done.35
  315.9 18.6 %collective-permute-done.5 = bf16[320,1280]{1,0:T(8,128)(2,1)S(1)} collective-permute-done((bf16[320,1280]{1,0:T(8,128)(2,1)S(1)}, bf16[320,1280]{1,0:T(8,128)(2,1)S(1)}, u32[]{:S(2)}, u32[]{:S(2)}) %collective-permute-start.5) | collective-permute-done | bytes 819232 | tf_op jit(solution)/shard_map/ppermute | solution.py:111
  340.6 3.5 fusion.53
  344.2 3.5 fusion.1
  363.7 3.6 multiply_reduce_fusion
  367.5 3.1 fusion.14
  370.6 3.0 convert_element_type.412
  390.6 11.1 %collective-permute-done.13 = bf16[2,4,32,1280]{3,2,1,0:T(8,128)(2,1)} collective-permute-done((bf16[2,4,32,1280]{3,2,1,0:T(8,128)(2,1)}, bf16[2,4,32,1280]{3,2,1,0:T(8,128)(2,1)}, u32[]{:S(2)}, u32[]{:S(2)}) %collective-permute-start.13) | collective-permute-done | bytes 655392 | tf_op jit(solution)/shard_map/ppermute | solution.py:111
  404.5 7.5 %collective-permute-done.7 = bf16[2,4,40,1536]{3,2,1,0:T(8,128)(2,1)} collective-permute-done((bf16[2,4,40,1536]{3,2,1,0:T(8,128)(2,1)}, bf16[2,4,40,1536]{3,2,1,0:T(8,128)(2,1)}, u32[]{:S(2)}, u32[]{:S(2)}) %collective-permute-start.7) | collective-permute-done | bytes 983072 | tf_op jit(solution)/shard_map/ppermute | solution.py:111
  414.3 3.8 collective-permute-done.14
  422.1 3.1 collective-permute-done.8
  425.5 3.0 collective-permute-start.11
  429.5 7.7 %collective-permute-done.10 = bf16[40,1536]{1,0:T(8,128)(2,1)S(1)} collective-permute-done((bf16[40,1536]{1,0:T(8,128)(2,1)S(1)}, bf16[40,1536]{1,0:T(8,128)(2,1)S(1)}, u32[]{:S(2)}, u32[]{:S(2)}) %collective-permute-start.10) | collective-permute-done | bytes 122912 | tf_op jit(solution)/shard_map/ppermute | solution.py:111
  441.7 17.7 %all_totals.1 = f32[32,8,128]{2,1,0:T(8,128)} custom-call(f32[32,8,128]{2,1,0:T(8,128)} %pad.25.part_ref, f32[7,128]{1,0:T(8,128)} %broadcast_in_dim.105.square_ref), custom_call_target="tpu_custom_call" | custom-call | tf_op jit(solution)/shard_map/all_totals/pallas_call | solution.py:456
  (486 shorter events, 155.8 us)
Async XLA Ops:
  165.0 75.6 %collective-permute-start.32 = (bf16[4,96,1280]{2,1,0:T(8,128)(2,1)}, bf16[4,96,1280]{2,1,0:T(8,128)(2,1)}, u32[]{:S(2)}, u32[]{:S(2)}) collective-permute-start(bf16[4,96,1280]{2,1,0:T(8,128)(2,1)} %dynamic-slice_bitcast_fusion.1), channel_id=1, source_target_pairs={{0,16},{1,17},{2,18},{3,19},{4,20},{5,21},{6,22},{7,23},{8,24},{9,... | collective-permute-start | bytes 2949128 | tf_op jit(solution)/shard_map/ppermute | solution.py:111
  174.1 61.3 %collective-permute-start.25 = (bf16[4,4,40,768]{3,2,0,1:T(8,128)(2,1)}, bf16[4,4,40,768]{3,2,0,1:T(8,128)(2,1)}, u32[]{:S(2)}, u32[]{:S(2)}) collective-permute-start(bf16[4,4,40,768]{3,2,0,1:T(8,128)(2,1)} %bitcast.262), channel_id=1, source_target_pairs={{0,16},{1,17},{2,18},{3,19},{4,20},{5,21},{6,22},{7,23},{8,24},{9,... | collective-permute-start | bytes 2949128 | tf_op jit(solution)/shard_map/ppermute | solution.py:111
  180.4 57.3 %collective-permute-start.18 = (bf16[4,4,40,768]{3,2,0,1:T(8,128)(2,1)}, bf16[4,4,40,768]{3,2,0,1:T(8,128)(2,1)}, u32[]{:S(2)}, u32[]{:S(2)}) collective-permute-start(bf16[4,4,40,768]{3,2,0,1:T(8,128)(2,1)} %bitcast.263), channel_id=1, source_target_pairs={{0,16},{1,17},{2,18},{3,19},{4,20},{5,21},{6,22},{7,23},{8,24},{9,... | collective-permute-start | bytes 2949128 | tf_op jit(solution)/shard_map/ppermute | solution.py:111
  185.2 119.6 %collective-permute-start = (bf16[320,1280]{1,0:T(8,128)(2,1)}, bf16[320,1280]{1,0:T(8,128)(2,1)}, u32[]{:S(2)}, u32[]{:S(2)}) collective-permute-start(bf16[320,1280]{1,0:T(8,128)(2,1)} %slice.121), channel_id=1, source_target_pairs={{0,4},{1,5},{2,6},{3,7},{4,0},{5,1},{6,2},{7,3},{8,12},{9,13},{10,... | collective-permute-start | bytes 2457608 | tf_op jit(solution)/shard_map/ppermute | solution.py:111
  189.2 43.1 %collective-permute-start.1 = (bf16[320,1280]{1,0:T(8,128)(2,1)}, bf16[320,1280]{1,0:T(8,128)(2,1)}, u32[]{:S(2)}, u32[]{:S(2)}) collective-permute-start(bf16[320,1280]{1,0:T(8,128)(2,1)} %slice.123), channel_id=1, source_target_pairs={{0,4},{1,5},{2,6},{3,7},{4,0},{5,1},{6,2},{7,3},{8,12},{9,13},{10,... | collective-permute-start | bytes 2457608 | tf_op jit(solution)/shard_map/ppermute | solution.py:111
  233.9 71.4 %collective-permute-start.2 = (bf16[320,1280]{1,0:T(8,128)(2,1)S(1)}, bf16[320,1280]{1,0:T(8,128)(2,1)S(1)}, u32[]{:S(2)}, u32[]{:S(2)}) collective-permute-start(bf16[320,1280]{1,0:T(8,128)(2,1)S(1)} %add_convert_fusion.2), channel_id=1, source_target_pairs={{0,8},{1,9},{2,10},{3,11},{4,12},{5,13},{6,14},{7,15},{8,0},{9,1},... | collective-permute-start | bytes 2457608 | tf_op jit(solution)/shard_map/ppermute | solution.py:111
  237.1 10.8 %collective-permute-start.26 = (bf16[4,40,768]{2,1,0:T(8,128)(2,1)S(1)}, bf16[4,40,768]{2,1,0:T(8,128)(2,1)S(1)}, u32[]{:S(2)}, u32[]{:S(2)}) collective-permute-start(bf16[4,40,768]{2,1,0:T(8,128)(2,1)S(1)} %get-tuple-element.130), channel_id=1, source_target_pairs={{0,1},{1,2},{2,3},{3,0},{4,5},{5,6},{6,7},{7,4},{8,9},{9,10},{10,1... | collective-permute-start | bytes 737288 | tf_op jit(solution)/shard_map/ppermute | solution.py:111
  237.7 27.4 %collective-permute-start.27 = (bf16[4,40,768]{2,1,0:T(8,128)(2,1)S(1)}, bf16[4,40,768]{2,1,0:T(8,128)(2,1)S(1)}, u32[]{:S(2)}, u32[]{:S(2)}) collective-permute-start(bf16[4,40,768]{2,1,0:T(8,128)(2,1)S(1)} %get-tuple-element.132), channel_id=1, source_target_pairs={{0,2},{1,3},{2,0},{3,1},{4,6},{5,7},{6,4},{7,5},{8,10},{9,11},{10,... | collective-permute-start | bytes 737288 | tf_op jit(solution)/shard_map/ppermute | solution.py:111
  240.6 24.5 %collective-permute-start.28 = (bf16[4,40,768]{2,1,0:T(8,128)(2,1)S(1)}, bf16[4,40,768]{2,1,0:T(8,128)(2,1)S(1)}, u32[]{:S(2)}, u32[]{:S(2)}) collective-permute-start(bf16[4,40,768]{2,1,0:T(8,128)(2,1)S(1)} %get-tuple-element.131), channel_id=1, source_target_pairs={{0,3},{1,0},{2,1},{3,2},{4,7},{5,4},{6,5},{7,6},{8,11},{9,8},{10,9... | collective-permute-start | bytes 737288 | tf_op jit(solution)/shard_map/ppermute | solution.py:111
  247.9 20.8 %collective-permute-start.19 = (bf16[4,40,768]{2,1,0:T(8,128)(2,1)S(1)}, bf16[4,40,768]{2,1,0:T(8,128)(2,1)S(1)}, u32[]{:S(2)}, u32[]{:S(2)}) collective-permute-start(bf16[4,40,768]{2,1,0:T(8,128)(2,1)S(1)} %get-tuple-element.133), channel_id=1, source_target_pairs={{0,1},{1,2},{2,3},{3,0},{4,5},{5,6},{6,7},{7,4},{8,9},{9,10},{10,1... | collective-permute-start | bytes 737288 | tf_op jit(solution)/shard_map/ppermute | solution.py:111
  265.1 21.1 %collective-permute-start.20 = (bf16[4,40,768]{2,1,0:T(8,128)(2,1)S(1)}, bf16[4,40,768]{2,1,0:T(8,128)(2,1)S(1)}, u32[]{:S(2)}, u32[]{:S(2)}) collective-permute-start(bf16[4,40,768]{2,1,0:T(8,128)(2,1)S(1)} %get-tuple-element.135), channel_id=1, source_target_pairs={{0,2},{1,3},{2,0},{3,1},{4,6},{5,7},{6,4},{7,5},{8,10},{9,11},{10,... | collective-permute-start | bytes 737288 | tf_op jit(solution)/shard_map/ppermute | solution.py:111
  265.1 21.1 %collective-permute-start.21 = (bf16[4,40,768]{2,1,0:T(8,128)(2,1)S(1)}, bf16[4,40,768]{2,1,0:T(8,128)(2,1)S(1)}, u32[]{:S(2)}, u32[]{:S(2)}) collective-permute-start(bf16[4,40,768]{2,1,0:T(8,128)(2,1)S(1)} %get-tuple-element.134), channel_id=1, source_target_pairs={{0,3},{1,0},{2,1},{3,2},{4,7},{5,4},{6,5},{7,6},{8,11},{9,8},{10,9... | collective-permute-start | bytes 737288 | tf_op jit(solution)/shard_map/ppermute | solution.py:111
  268.7 18.6 %collective-permute-start.33 = (bf16[96,1280]{1,0:T(8,128)(2,1)S(1)}, bf16[96,1280]{1,0:T(8,128)(2,1)S(1)}, u32[]{:S(2)}, u32[]{:S(2)}) collective-permute-start(bf16[96,1280]{1,0:T(8,128)(2,1)S(1)} %get-tuple-element.127), channel_id=1, source_target_pairs={{0,1},{1,2},{2,3},{3,0},{4,5},{5,6},{6,7},{7,4},{8,9},{9,10},{10,1... | collective-permute-start | bytes 737288 | tf_op jit(solution)/shard_map/ppermute | solution.py:111
  286.2 13.2 %collective-permute-start.34 = (bf16[96,1280]{1,0:T(8,128)(2,1)S(1)}, bf16[96,1280]{1,0:T(8,128)(2,1)S(1)}, u32[]{:S(2)}, u32[]{:S(2)}) collective-permute-start(bf16[96,1280]{1,0:T(8,128)(2,1)S(1)} %get-tuple-element.129), channel_id=1, source_target_pairs={{0,2},{1,3},{2,0},{3,1},{4,6},{5,7},{6,4},{7,5},{8,10},{9,11},{10,... | collective-permute-start | bytes 737288 | tf_op jit(solution)/shard_map/ppermute | solution.py:111
  286.2 17.7 %collective-permute-start.35 = (bf16[96,1280]{1,0:T(8,128)(2,1)S(1)}, bf16[96,1280]{1,0:T(8,128)(2,1)S(1)}, u32[]{:S(2)}, u32[]{:S(2)}) collective-permute-start(bf16[96,1280]{1,0:T(8,128)(2,1)S(1)} %get-tuple-element.128), channel_id=1, source_target_pairs={{0,3},{1,0},{2,1},{3,2},{4,7},{5,4},{6,5},{7,6},{8,11},{9,8},{10,9... | collective-permute-start | bytes 737288 | tf_op jit(solution)/shard_map/ppermute | solution.py:111
  287.3 23.6 %collective-permute-start.29 = (bf16[40,768]{1,0:T(8,128)(2,1)S(1)}, bf16[40,768]{1,0:T(8,128)(2,1)S(1)}, u32[]{:S(2)}, u32[]{:S(2)}) collective-permute-start(bf16[40,768]{1,0:T(8,128)(2,1)S(1)} %get-tuple-element.150), channel_id=1, source_target_pairs={{0,4},{1,5},{2,6},{3,7},{4,0},{5,1},{6,2},{7,3},{8,12},{9,13},{10,... | collective-permute-start | bytes 184328 | tf_op jit(solution)/shard_map/ppermute | solution.py:111
  299.5 11.6 %collective-permute-start.30 = (bf16[40,768]{1,0:T(8,128)(2,1)S(1)}, bf16[40,768]{1,0:T(8,128)(2,1)S(1)}, u32[]{:S(2)}, u32[]{:S(2)}) collective-permute-start(bf16[40,768]{1,0:T(8,128)(2,1)S(1)} %get-tuple-element.149), channel_id=1, source_target_pairs={{0,8},{1,9},{2,10},{3,11},{4,12},{5,13},{6,14},{7,15},{8,0},{9,1},... | collective-permute-start | bytes 184328 | tf_op jit(solution)/shard_map/ppermute | solution.py:111
  303.9 9.9 %collective-permute-start.31 = (bf16[40,768]{1,0:T(8,128)(2,1)S(1)}, bf16[40,768]{1,0:T(8,128)(2,1)S(1)}, u32[]{:S(2)}, u32[]{:S(2)}) collective-permute-start(bf16[40,768]{1,0:T(8,128)(2,1)S(1)} %get-tuple-element.148), channel_id=1, source_target_pairs={{0,12},{1,13},{2,14},{3,15},{4,8},{5,9},{6,10},{7,11},{8,4},{9,5},... | collective-permute-start | bytes 184328 | tf_op jit(solution)/shard_map/ppermute | solution.py:111
  304.8 10.3 %collective-permute-start.22 = (bf16[40,768]{1,0:T(8,128)(2,1)S(1)}, bf16[40,768]{1,0:T(8,128)(2,1)S(1)}, u32[]{:S(2)}, u32[]{:S(2)}) collective-permute-start(bf16[40,768]{1,0:T(8,128)(2,1)S(1)} %get-tuple-element.154), channel_id=1, source_target_pairs={{0,4},{1,5},{2,6},{3,7},{4,0},{5,1},{6,2},{7,3},{8,12},{9,13},{10,... | collective-permute-start | bytes 184328 | tf_op jit(solution)/shard_map/ppermute | solution.py:111
  305.4 9.8 %collective-permute-start.23 = (bf16[40,768]{1,0:T(8,128)(2,1)S(1)}, bf16[40,768]{1,0:T(8,128)(2,1)S(1)}, u32[]{:S(2)}, u32[]{:S(2)}) collective-permute-start(bf16[40,768]{1,0:T(8,128)(2,1)S(1)} %get-tuple-element.153), channel_id=1, source_target_pairs={{0,8},{1,9},{2,10},{3,11},{4,12},{5,13},{6,14},{7,15},{8,0},{9,1},... | collective-permute-start | bytes 184328 | tf_op jit(solution)/shard_map/ppermute | solution.py:111
  311.0 67.0 %collective-permute-start.24 = (bf16[40,768]{1,0:T(8,128)(2,1)}, bf16[40,768]{1,0:T(8,128)(2,1)}, u32[]{:S(2)}, u32[]{:S(2)}) collective-permute-start(bf16[40,768]{1,0:T(8,128)(2,1)} %get-tuple-element.152), channel_id=1, source_target_pairs={{0,12},{1,13},{2,14},{3,15},{4,8},{5,9},{6,10},{7,11},{8,4},{9,5},... | collective-permute-start | bytes 184328 | tf_op jit(solution)/shard_map/ppermute | solution.py:111
  313.8 20.7 %collective-permute-start.5 = (bf16[320,1280]{1,0:T(8,128)(2,1)S(1)}, bf16[320,1280]{1,0:T(8,128)(2,1)S(1)}, u32[]{:S(2)}, u32[]{:S(2)}) collective-permute-start(bf16[320,1280]{1,0:T(8,128)(2,1)S(1)} %add_convert_fusion.1), channel_id=1, source_target_pairs={{0,8},{1,9},{2,10},{3,11},{4,12},{5,13},{6,14},{7,15},{8,0},{9,1},... | collective-permute-start | bytes 2457608 | tf_op jit(solution)/shard_map/ppermute | solution.py:111
  357.8 23.8 %collective-permute-start.12 = (bf16[2,2,4,32,1280]{4,3,2,1,0:T(8,128)(2,1)}, bf16[2,2,4,32,1280]{4,3,2,1,0:T(8,128)(2,1)}, u32[]{:S(2)}, u32[]{:S(2)}) collective-permute-start(bf16[2,2,4,32,1280]{4,3,2,1,0:T(8,128)(2,1)} %dynamic-slice_bitcast_fusion), channel_id=1, source_target_pairs={{0,4},{1,5},{2,6},{3,7},{4,0},{5,1},{6,2},{7,3},{8,12},{9,13},{10,... | collective-permute-start | bytes 3932168 | tf_op jit(solution)/shard_map/ppermute | solution.py:111
  376.7 8.8 %collective-permute-start.6 = (bf16[2,2,4,40,1536]{4,3,2,0,1:T(8,128)(2,1)S(1)}, bf16[2,2,4,40,1536]{4,3,2,0,1:T(8,128)(2,1)S(1)}, u32[]{:S(2)}, u32[]{:S(2)}) collective-permute-start(bf16[2,2,4,40,1536]{4,3,2,0,1:T(8,128)(2,1)S(1)} %bitcast.297), channel_id=1, source_target_pairs={{0,4},{1,5},{2,6},{3,7},{4,0},{5,1},{6,2},{7,3},{8,12},{9,13},{10,... | collective-permute-start | bytes 5898248 | tf_op jit(solution)/shard_map/ppermute | solution.py:111
  384.3 17.4 %collective-permute-start.13 = (bf16[2,4,32,1280]{3,2,1,0:T(8,128)(2,1)}, bf16[2,4,32,1280]{3,2,1,0:T(8,128)(2,1)}, u32[]{:S(2)}, u32[]{:S(2)}) collective-permute-start(bf16[2,4,32,1280]{3,2,1,0:T(8,128)(2,1)} %dynamic-slice_bitcast_fusion.3), channel_id=1, source_target_pairs={{0,16},{1,17},{2,18},{3,19},{4,20},{5,21},{6,22},{7,23},{8,24},{9,... | collective-permute-start | bytes 1966088 | tf_op jit(solution)/shard_map/ppermute | solution.py:111
  387.1 24.9 %collective-permute-start.7 = (bf16[2,4,40,1536]{3,2,1,0:T(8,128)(2,1)}, bf16[2,4,40,1536]{3,2,1,0:T(8,128)(2,1)}, u32[]{:S(2)}, u32[]{:S(2)}) collective-permute-start(bf16[2,4,40,1536]{3,2,1,0:T(8,128)(2,1)} %dynamic-slice_bitcast_fusion.2), channel_id=1, source_target_pairs={{0,8},{1,9},{2,10},{3,11},{4,12},{5,13},{6,14},{7,15},{8,0},{9,1},... | collective-permute-start | bytes 2949128 | tf_op jit(solution)/shard_map/ppermute | solution.py:111
  403.1 15.0 %collective-permute-start.14 = (bf16[4,32,1280]{2,1,0:T(8,128)(2,1)S(1)}, bf16[4,32,1280]{2,1,0:T(8,128)(2,1)S(1)}, u32[]{:S(2)}, u32[]{:S(2)}) collective-permute-start(bf16[4,32,1280]{2,1,0:T(8,128)(2,1)S(1)} %dynamic-slice_bitcast_fusion.5), channel_id=1, source_target_pairs={{0,8},{1,9},{2,10},{3,11},{4,12},{5,13},{6,14},{7,15},{8,0},{9,1},... | collective-permute-start | bytes 983048 | tf_op jit(solution)/shard_map/ppermute | solution.py:111
  413.5 11.8 %collective-permute-start.8 = (bf16[4,40,1536]{2,1,0:T(8,128)(2,1)S(1)}, bf16[4,40,1536]{2,1,0:T(8,128)(2,1)S(1)}, u32[]{:S(2)}, u32[]{:S(2)}) collective-permute-start(bf16[4,40,1536]{2,1,0:T(8,128)(2,1)S(1)} %dynamic-slice_bitcast_fusion.4), channel_id=1, source_target_pairs={{0,16},{1,17},{2,18},{3,19},{4,20},{5,21},{6,22},{7,23},{8,24},{9,... | collective-permute-start | bytes 1474568 | tf_op jit(solution)/shard_map/ppermute | solution.py:111
  418.3 10.2 %collective-permute-start.15 = (bf16[32,1280]{1,0:T(8,128)(2,1)S(1)}, bf16[32,1280]{1,0:T(8,128)(2,1)S(1)}, u32[]{:S(2)}, u32[]{:S(2)}) collective-permute-start(bf16[32,1280]{1,0:T(8,128)(2,1)S(1)} %get-tuple-element.141), channel_id=1, source_target_pairs={{0,1},{1,2},{2,3},{3,0},{4,5},{5,6},{6,7},{7,4},{8,9},{9,10},{10,1... | collective-permute-start | bytes 245768 | tf_op jit(solution)/shard_map/ppermute | solution.py:111
  418.9 9.8 %collective-permute-start.16 = (bf16[32,1280]{1,0:T(8,128)(2,1)S(1)}, bf16[32,1280]{1,0:T(8,128)(2,1)S(1)}, u32[]{:S(2)}, u32[]{:S(2)}) collective-permute-start(bf16[32,1280]{1,0:T(8,128)(2,1)S(1)} %get-tuple-element.143), channel_id=1, source_target_pairs={{0,2},{1,3},{2,0},{3,1},{4,6},{5,7},{6,4},{7,5},{8,10},{9,11},{10,... | collective-permute-start | bytes 245768 | tf_op jit(solution)/shard_map/ppermute | solution.py:111
  425.4 11.7 %collective-permute-start.10 = (bf16[40,1536]{1,0:T(8,128)(2,1)S(1)}, bf16[40,1536]{1,0:T(8,128)(2,1)S(1)}, u32[]{:S(2)}, u32[]{:S(2)}) collective-permute-start(bf16[40,1536]{1,0:T(8,128)(2,1)S(1)} %get-tuple-element.140), channel_id=1, source_target_pairs={{0,2},{1,3},{2,0},{3,1},{4,6},{5,7},{6,4},{7,5},{8,10},{9,11},{10,... | collective-permute-start | bytes 368648 | tf_op jit(solution)/shard_map/ppermute | solution.py:111
  425.5 11.6 %collective-permute-start.11 = (bf16[40,1536]{1,0:T(8,128)(2,1)S(1)}, bf16[40,1536]{1,0:T(8,128)(2,1)S(1)}, u32[]{:S(2)}, u32[]{:S(2)}) collective-permute-start(bf16[40,1536]{1,0:T(8,128)(2,1)S(1)} %get-tuple-element.139), channel_id=1, source_target_pairs={{0,3},{1,0},{2,1},{3,2},{4,7},{5,4},{6,5},{7,6},{8,11},{9,8},{10,9... | collective-permute-start | bytes 368648 | tf_op jit(solution)/shard_map/ppermute | solution.py:111
  (133 other events, 784.6 us)

commit v3 on v2

--- a/solution.py
+++ b/solution.py
@@ -1,4 +1,5 @@
 import functools
+import math
 
 import jax
 import jax.numpy as jnp
@@ -781,6 +782,612 @@
     )(tokens, in_w, out_w, *small, cot, gate_w, upper_x, down_x)
 
 
+def backward_kernel(
+    nd,
+    nf,
+    length,
+    ffn_near,
+    ffn_far,
+    out_near,
+    out_far,
+    down_terms,
+    gate_terms,
+    upper_terms,
+    tokens,
+    cot,
+    hidden_in,
+    raw,
+    heads,
+    values,
+    mixed,
+    in_w,
+    out_w,
+    gain_attn,
+    gain_ffn,
+    gain_heads,
+    cosine,
+    sine,
+    mask,
+    out_core,
+    out_x,
+    gate_parts,
+    upper_parts,
+    input_grad,
+    in_sum,
+    out_sum,
+    down_sum,
+    sum_attn,
+    sum_ffn,
+    sum_heads,
+    mine_ref,
+    pass_ref,
+    core_near,
+    core_far,
+    from_x,
+    out_pass,
+    out_core_far,
+    normed,
+    branch,
+    grad_mixed,
+    grad_hidden,
+    grad_raw,
+    wide,
+    in_terms,
+    out_terms,
+    in_core,
+    out_core_terms,
+    in_x,
+    out_x_terms,
+    in_y,
+    out_y_terms,
+    in_total,
+    out_total,
+    in_zs,
+    out_zs,
+    in_zr,
+    out_zr,
+    down_own,
+    gate_own,
+    upper_own,
+    down_y,
+    gate_y,
+    upper_y,
+    down_z,
+    gate_z,
+    upper_z,
+    row_send,
+    row_recv,
+    fy_send,
+    fy_recv,
+    fz_send,
+    fz_recv,
+    swap_send,
+    swap_recv,
+    ac_send,
+    ac_recv,
+    ax_send,
+    ax_recv,
+    ay_send,
+    ay_recv,
+    az_send,
+    az_recv,
+    load_sem,
+    local_sem,
+):
+    outer = nd // MEMBERS
+    dp = lax.axis_index("dp")
+    z = lax.axis_index("fsdp")
+    y = dp // MEMBERS
+    member = dp % MEMBERS
+    x = member // 2
+    c = member % 2
+    lo, hi = jnp.bfloat16, jnp.float32
+
+    def z_to(step):
+        return lax.rem(z + step, nf)
+
+    def z_peer(step):
+        return (dp, z_to(step))
+
+    def y_to(step):
+        return lax.rem(y + step, outer)
+
+    def y_peer(step):
+        return (y_to(step) * MEMBERS + member, z)
+
+    def in_group(k):
+        return (y * MEMBERS + k, z)
+
+    x_peer = in_group((1 - x) * 2 + c)
+    core_peer = in_group(x * 2 + 1 - c)
+    barrier = pltpu.get_barrier_semaphore()
+    peers = [z_peer(step) for step in range(1, nf)] + [y_peer(step) for step in range(1, outer)]
+    peers += [x_peer, core_peer, in_group(MEMBERS - 1 - member)]
+    for peer in peers:
+        pl.semaphore_signal(barrier, inc=1, device_id=peer, device_id_type=MESH)
+    pl.semaphore_wait(barrier, len(peers))
+    sent = []
+
+    def remote(source, target, send, recv, device):
+        copy = pltpu.make_async_remote_copy(
+            src_ref=source,
+            dst_ref=target,
+            send_sem=send,
+            recv_sem=recv,
+            device_id=device,
+            device_id_type=MESH,
+        )
+        copy.start()
+        sent.append(copy)
+        return copy
+
+    def keep(semaphore, source, target):
+        copy = pltpu.make_async_copy(source, target, semaphore)
+        copy.start()
+        return copy
+
+    count, width = tokens.shape
+    here, there = pl.ds(0, count), pl.ds(count, count)
+
+    far_copy = remote(ffn_far.at[there], core_far, row_send.at[0], row_recv.at[0], core_peer)
+    pass_copy = keep(local_sem.at[0], ffn_far.at[here], pass_ref)
+    near_copy = remote(ffn_near.at[there], core_near, row_send.at[1], row_recv.at[1], core_peer)
+    mine_copy = keep(local_sem.at[1], ffn_near.at[here], mine_ref)
+    out_far_copy = remote(out_far.at[there], out_core_far, row_send.at[2], row_recv.at[2], core_peer)
+    out_pass_copy = keep(local_sem.at[2], out_far.at[here], out_pass)
+    out_near_copy = remote(out_near.at[there], out_core, row_send.at[3], row_recv.at[3], core_peer)
+
+    terms = (down_terms, gate_terms, upper_terms)
+    owns = (down_own, gate_own, upper_own)
+    over_y = (down_y, gate_y, upper_y)
+    over_z = (down_z, gate_z, upper_z)
+
+    def piece_of(matrix, place, step):
+        if matrix == 0:
+            return terms[0].at[place, z_to(step)]
+        return terms[matrix].at[place, :, z_to(step)]
+
+    order = [(matrix, step) for matrix in range(3) for step in list(range(1, nf)) + [0]]
+    y_copies, loads = {}, {}
+    for matrix, step in order:
+        loads[matrix, step] = keep(
+            load_sem.at[matrix, step], piece_of(matrix, y, step), owns[matrix].at[step]
+        )
+        for hop in range(1, outer):
+            y_copies[matrix, step, hop] = remote(
+                piece_of(matrix, y_to(hop), step),
+                over_y[matrix].at[hop - 1, step],
+                fy_send.at[matrix, hop, step],
+                fy_recv.at[matrix, hop, step],
+                y_peer(hop),
+            )
+    z_copies = {}
+    waiting = list(order)
+
+    def pieces(number):
+        for _ in range(min(number, len(waiting))):
+            matrix, step = waiting.pop(0)
+            loads[matrix, step].wait()
+            total = owns[matrix][step].astype(hi)
+            for hop in range(1, outer):
+                y_copies[matrix, step, hop].wait_recv()
+                total = total + over_y[matrix][hop - 1, step].astype(hi)
+            owns[matrix][step] = total.astype(lo)
+            if step:
+                z_copies[matrix, step] = remote(
+                    owns[matrix].at[step],
+                    over_z[matrix].at[step - 1],
+                    fz_send.at[matrix, step],
+                    fz_recv.at[matrix, step],
+                    z_peer(step),
+                )
+
+    def piece_total(matrix):
+        total = owns[matrix][0].astype(hi)
+        for step in range(1, nf):
+            z_copies[matrix, step].wait_recv()
+            total = total + over_z[matrix][step - 1].astype(hi)
+        return total
+
+    swaps = []
+
+    def trade(matrix, parts):
+        owns[matrix][0] = piece_total(matrix).astype(lo)
+        for mask_bits in range(1, MEMBERS):
+            other = member ^ mask_bits
+            swaps.append(
+                remote(
+                    owns[matrix].at[0, other],
+                    parts.at[member],
+                    swap_send.at[matrix - 1, mask_bits],
+                    swap_recv.at[matrix - 1, mask_bits],
+                    in_group(other),
+                )
+            )
+        swaps_local.append(
+            keep(local_sem.at[2 + matrix], owns[matrix].at[0, member], parts.at[member])
+        )
+
+    swaps_local = []
+    chunk = 32
+
+    far_copy.wait_recv()
+    pass_copy.wait()
+
+    def add_rows(target, other):
+        def step_once(index, carry):
+            rows = rows_of(index, chunk)
+            target[rows, :] = (target[rows, :].astype(hi) + other[rows, :].astype(hi)).astype(lo)
+            return carry
+
+        lax.fori_loop(0, count // chunk, step_once, 0)
+
+    add_rows(pass_ref, core_far)
+    x_copy = remote(pass_ref, from_x, row_send.at[4], row_recv.at[4], x_peer)
+    out_far_copy.wait_recv()
+    out_pass_copy.wait()
+    add_rows(out_pass, out_core_far)
+    out_x_copy = remote(out_pass, out_x, row_send.at[5], row_recv.at[5], x_peer)
+
+    def norm_rows(index, carry):
+        rows = rows_of(index, chunk)
+        part = tokens[rows, :].astype(hi)
+        scale = lax.rsqrt(jnp.mean(part * part, -1, keepdims=True) + norm_eps)
+        normed[rows, :] = (part * scale * gain_attn[...]).astype(lo)
+        return carry
+
+    lax.fori_loop(0, count // chunk, norm_rows, 0)
+    sum_attn[...] = jnp.zeros_like(sum_attn)
+    sum_ffn[...] = jnp.zeros_like(sum_ffn)
+    sum_heads[...] = jnp.zeros_like(sum_heads)
+    pieces(3)
+    near_copy.wait_recv()
+    mine_copy.wait()
+    x_copy.wait_recv()
+
+    def norm_back(part, gain, grad):
+        scale = lax.rsqrt(jnp.mean(part * part, -1, keepdims=True) + norm_eps)
+        unit = part * scale
+        inner = grad * gain
+        back = scale * (inner - unit * jnp.mean(inner * unit, -1, keepdims=True))
+        return back, jnp.sum(grad * unit, 0, keepdims=True)
+
+    def ffn_norm_back(index, carry):
+        rows = rows_of(index, chunk)
+        grad = mine_ref[rows, :].astype(hi) + core_near[rows, :].astype(hi)
+        grad = grad + from_x[rows, :].astype(hi)
+        back, gain_term = norm_back(hidden_in[rows, :], gain_ffn[...], grad)
+        sum_ffn[...] += gain_term
+        back = back + cot[rows, :].astype(hi)
+        grad_hidden[rows, :] = back
+        branch[rows, :] = back.astype(lo)
+        return carry
+
+    lax.fori_loop(0, count // chunk, ffn_norm_back, 0)
+    pair = 2 * LANES
+
+    def mixed_back(index, carry):
+        columns = tile_of(index, pair)
+        grad_mixed[:, columns] = dot_last(branch[...], out_w[columns, :]).astype(lo)
+        return carry
+
+    lax.fori_loop(0, HQ * HD // pair, mixed_back, 0)
+
+    def outer_product(left, right, target):
+        def step_once(index, carry):
+            columns = tile_of(index, pair)
+            turned = left[:, columns].T
+            for part in range(right.shape[1] // (2 * pair)):
+                across = pl.ds(part * 2 * pair, 2 * pair)
+                target[columns, across] = jnp.dot(
+                    turned, right[:, across], preferred_element_type=hi
+                ).astype(lo)
+            rest = right.shape[1] % (2 * pair)
+            if rest:
+                across = pl.ds(right.shape[1] - rest, rest)
+                target[columns, across] = jnp.dot(
+                    turned, right[:, across], preferred_element_type=hi
+                ).astype(lo)
+            return carry
+
+        lax.fori_loop(0, left.shape[1] // pair, step_once, 0)
+
+    all_terms = (in_terms, out_terms)
+    sizes = (in_terms.shape[0] // (nd), out_terms.shape[0] // (nd))
+    core_terms = (in_core, out_core_terms)
+    x_terms = (in_x, out_x_terms)
+    y_terms = (in_y, out_y_terms)
+    totals = (in_total, out_total)
+    zs = (in_zs, out_zs)
+    zr = (in_zr, out_zr)
+    hops = list(range(1, outer)) + [0]
+    core_copies, ax_copies, ay_copies, az_copies = {}, {}, {}, {}
+
+    def block(a, hop, bx, bc):
+        index = (y_to(hop) * 2 + bx) * 2 + bc
+        return pl.ds(pl.multiple_of(index * sizes[a], 16), sizes[a])
+
+    def core_out(a):
+        for far in (1, 0):
+            for hop in hops:
+                bx = 1 - x if far else x
+                core_copies[a, hop, far] = remote(
+                    all_terms[a].at[block(a, hop, bx, 1 - c)],
+                    core_terms[a].at[hop, far],
+                    ac_send.at[a, hop, far],
+                    ac_recv.at[a, hop, far],
+                    core_peer,
+                )
+
+    def add_block(a, rows, others):
+        some = math.gcd(sizes[a], 32)
+
+        def step_once(index, carry):
+            base = rows.start + index * some
+            place = pl.ds(pl.multiple_of(base, 16), some)
+            total = all_terms[a][place, :].astype(hi)
+            for other in others:
+                total = total + other[rows_of(index, some), :].astype(hi)
+            all_terms[a][place, :] = total.astype(lo)
+            return carry
+
+        lax.fori_loop(0, sizes[a] // some, step_once, 0)
+
+    def core_in(a):
+        for hop in hops:
+            core_copies[a, hop, 1].wait_recv()
+            rows = block(a, hop, 1 - x, c)
+            add_block(a, rows, [core_terms[a].at[hop, 1]])
+            ax_copies[a, hop] = remote(
+                all_terms[a].at[rows],
+                x_terms[a].at[hop],
+                ax_send.at[a, hop],
+                ax_recv.at[a, hop],
+                x_peer,
+            )
+
+    def x_in(a):
+        for hop in range(1, outer):
+            core_copies[a, hop, 0].wait_recv()
+            ax_copies[a, hop].wait_recv()
+            rows = block(a, hop, x, c)
+            add_block(a, rows, [core_terms[a].at[hop, 0], x_terms[a].at[hop]])
+            ay_copies[a, hop] = remote(
+                all_terms[a].at[rows],
+                y_terms[a].at[hop - 1],
+                ay_send.at[a, hop],
+                ay_recv.at[a, hop],
+                y_peer(hop),
+            )
+
+    def y_in(a):
+        core_copies[a, 0, 0].wait_recv()
+        ax_copies[a, 0].wait_recv()
+        others = [core_terms[a].at[0, 0], x_terms[a].at[0]]
+        for hop in range(1, outer):
+            ay_copies[a, hop].wait_recv()
+            others.append(y_terms[a].at[hop - 1])
+        start = block(a, 0, x, c).start
+        some = math.gcd(sizes[a], 32)
+
+        def step_once(index, carry):
+            place = rows_of(index, some)
+            own = pl.ds(pl.multiple_of(start + index * some, 16), some)
+            total = all_terms[a][own, :].astype(hi)
+            for other in others:
+                total = total + other[place, :].astype(hi)
+            totals[a][place, :] = total
+            return carry
+
+        lax.fori_loop(0, sizes[a] // some, step_once, 0)
+        rows = sizes[a] // nf
+        for place in range(nf):
+            zs[a][place] = totals[a][place * rows : (place + 1) * rows, :].astype(lo)
+        for step in range(1, nf):
+            az_copies[a, step] = remote(
+                zs[a].at[z_to(step)],
+                zr[a].at[step - 1],
+                az_send.at[a, step],
+                az_recv.at[a, step],
+                z_peer(step),
+            )
+
+    def z_in(a, target):
+        total = zs[a][z].astype(hi)
+        for step in range(1, nf):
+            az_copies[a, step].wait_recv()
+            total = total + zr[a][step - 1].astype(hi)
+        target[...] = total
+
+    outer_product(mixed, branch, out_terms)
+    core_out(1)
+    pieces(2)
+    query_tiles = HQ * HD // LANES
+    head_tiles = (HQ + KV) * HD // LANES
+    key_tiles = KV * HD // LANES
+
+    def over_rows(left, right):
+        return lax.dot_general(left, right, (((0,), (0,)), ((), ())), preferred_element_type=hi)
+
+    def attend_back(row):
+        rows = pl.ds(row * length, length)
+        allowed = mask[row] > 0.5
+
+        def pair_back(tile, carry):
+            key_tile = heads[rows, tile_of(query_tiles + tile)]
+            value_tile = values[rows, tile_of(tile)]
+            grad_key = None
+            grad_value = None
+            for own in range(2):
+                key = [in_half(key_tile, own, half) for half in range(2)]
+                value = [in_half(value_tile, own, half) for half in range(2)]
+                for half in range(2):
+                    key_total, value_total = None, None
+                    for quarter in range(2):
+                        columns = tile_of(tile * 4 + own * 2 + quarter)
+                        query = heads[rows, columns]
+                        grad = grad_mixed[rows, columns]
+                        weights = probabilities(query, key[half], allowed)
+                        slope = dot_last(grad, value[half])
+                        inner = jnp.sum(weights * slope, -1, keepdims=True)
+                        score = (weights * (slope - inner)).astype(lo)
+                        back = jnp.dot(score, key[half], preferred_element_type=hi) * HD**-0.5
+                        if half == 0:
+                            wide[rows, columns] = back
+                        else:
+                            wide[rows, columns] += back
+                        key_term = over_rows(score, query)
+                        value_term = over_rows(weights.astype(lo), grad)
+                        key_total = key_term if key_total is None else key_total + key_term
+                        value_total = value_term if value_total is None else value_total + value_term
+                    key_term = in_half(key_total, half, own)
+                    value_term = in_half(value_total, half, own)
+                    grad_key = key_term if grad_key is None else grad_key + key_term
+                    grad_value = value_term if grad_value is None else grad_value + value_term
+            wide[rows, tile_of(query_tiles + tile)] = grad_key * HD**-0.5
+            grad_raw[rows, tile_of(head_tiles + tile)] = grad_value.astype(lo)
+            return carry
+
+        lax.fori_loop(0, key_tiles, pair_back, 0)
+
+    batch = count // length
+    for row in range(batch):
+        attend_back(row)
+        pieces(2)
+        if row == 0:
+            core_in(1)
+    averages = block_mean()
+
+    def turn_back(index, carry):
+        columns = tile_of(index)
+        gain = gain_heads[:, columns]
+        for row in range(batch):
+            rows = pl.ds(row * length, length)
+            grad = wide[rows, columns]
+            grad = grad * cosine[...] - swap_halves(grad) * sine[...]
+            part = raw[rows, columns]
+            scale = lax.rsqrt(head_mean(part * part, averages) + norm_eps)
+            unit = part * scale
+            sum_heads[:, columns] += jnp.sum(grad * unit, 0, keepdims=True)
+            inner = grad * gain
+            back = scale * (inner - unit * head_mean(inner * unit, averages))
+            grad_raw[rows, columns] = back.astype(lo)
+        return carry
+
+    lax.fori_loop(0, head_tiles, turn_back, 0)
+    outer_product(normed, grad_raw, in_terms)
+    core_out(0)
+    pieces(1)
+    x_in(1)
+
+    def normed_back(index, carry):
+        columns = tile_of(index, pair)
+        wide[:, columns] = dot_last(grad_raw[...], in_w[columns, :])
+        return carry
+
+    core_in(0)
+    lax.fori_loop(0, width // pair, normed_back, 0)
+
+    def attn_norm_back(index, carry):
+        rows = rows_of(index, chunk)
+        back, gain_term = norm_back(tokens[rows, :].astype(hi), gain_attn[...], wide[rows, :])
+        sum_attn[...] += gain_term
+        input_grad[rows, :] = (back + grad_hidden[rows, :]).astype(lo)
+        return carry
+
+    lax.fori_loop(0, count // chunk, attn_norm_back, 0)
+    down_sum[...] = piece_total(0)
+    pieces(2)
+    x_in(0)
+    y_in(1)
+    pieces(2 * nf)
+    trade(1, gate_parts)
+    y_in(0)
+    z_in(1, out_sum)
+    trade(2, upper_parts)
+    z_in(0, in_sum)
+    for copy in swaps + [out_near_copy, out_x_copy]:
+        copy.wait_recv()
+    for copy in sent:
+        copy.wait_send()
+    for copy in swaps_local:
+        copy.wait()
+
+
+def backward(nd, nf, length, halves, terms, rows, weights, small):
+    outer = nd // MEMBERS
+    count, width = rows[0].shape
+    in_w, out_w = weights
+    down_terms, gate_terms, _ = terms
+    lo, hi = jnp.bfloat16, jnp.float32
+    dma = pltpu.SemaphoreType.DMA
+    in_rows, in_cols = in_w.shape[0] // (nd * nf), in_w.shape[1]
+    out_rows, out_cols = out_w.shape[0] // (nd * nf), out_w.shape[1]
+    inner = (MEMBERS,) + gate_terms.shape[3:]
+    down = down_terms.shape[2:]
+    shapes = [
+        ((count, width), lo),
+        ((count, width), lo),
+        (inner, lo),
+        (inner, lo),
+        ((count, width), lo),
+        ((in_rows, in_cols), hi),
+        ((out_rows, out_cols), hi),
+        (down, hi),
+        ((1, width), hi),
+        ((1, width), hi),
+        ((1, (HQ + KV) * HD), hi),
+    ]
+    in_block, out_block = (nf * in_rows, in_cols), (nf * out_rows, out_cols)
+    scratch = [((count, width), lo)] * 7
+    scratch += [
+        ((count, width), lo),
+        ((count, width), lo),
+        ((count, HQ * HD), lo),
+        ((count, width), hi),
+        ((count, in_cols), lo),
+        ((count, width), hi),
+        (in_w.shape, lo),
+        (out_w.shape, lo),
+        ((outer, 2) + in_block, lo),
+        ((outer, 2) + out_block, lo),
+        ((outer,) + in_block, lo),
+        ((outer,) + out_block, lo),
+        ((outer - 1,) + in_block, lo),
+        ((outer - 1,) + out_block, lo),
+        (in_block, hi),
+        (out_block, hi),
+        ((nf, in_rows, in_cols), lo),
+        ((nf, out_rows, out_cols), lo),
+        ((nf - 1, in_rows, in_cols), lo),
+        ((nf - 1, out_rows, out_cols), lo),
+        ((nf,) + down, lo),
+        ((nf,) + inner, lo),
+        ((nf,) + inner, lo),
+        ((outer - 1, nf) + down, lo),
+        ((outer - 1, nf) + inner, lo),
+        ((outer - 1, nf) + inner, lo),
+        ((nf - 1,) + down, lo),
+        ((nf - 1,) + inner, lo),
+        ((nf - 1,) + inner, lo),
+    ]
+    moves = [(6,), (3, outer, nf), (3, nf), (2, MEMBERS), (2, outer, 2), (2, outer), (2, outer)]
+    moves += [(2, nf)]
+    return pl.pallas_call(
+        functools.partial(backward_kernel, nd, nf, length),
+        name="backward",
+        out_shape=tuple(jax.ShapeDtypeStruct(*item) for item in shapes),
+        in_specs=[ANYWHERE] * 7 + [ON_CHIP] * 15,
+        out_specs=(ANYWHERE,) * 4 + (ON_CHIP,) * 7,
+        scratch_shapes=[pltpu.VMEM(*item) for item in scratch]
+        + [dma(shape) for shape in moves for _ in range(2)]
+        + [dma((3, nf)), dma((5,))],
+        compiler_params=pltpu.CompilerParams(
+            collective_id=3, has_side_effects=True, vmem_limit_bytes=58 * 2**20
+        ),
+    )(*halves, *terms, *rows, *weights, *small)
+
+
 def after(value, *others):
     return lax.optimization_barrier((value,) + others)[0]
 
@@ -922,21 +1529,10 @@
     ffn_all = ffn_all.reshape(MEMBERS * count, width)
     back_halves = (back_all[: 2 * count], back_all[2 * count :])
     ffn_halves = (ffn_all[: 2 * count], ffn_all[2 * count :])
-    query_raw = raw[:, : HQ * HD]
-    key_raw = raw[:, HQ * HD :]
-    queries = heads[:, : HQ * HD].reshape(batch, length, KV, group_size, HD)
-    keys = heads[:, HQ * HD :].reshape(batch, length, KV, HD)
-    values = values.reshape(batch, length, KV, HD)
-
-    def piece(raw, gain):
-        return head_norm(raw.reshape(batch, length, -1), gain, cosine, sine)
-
     gates = [forward_product(half, gate_w) for half in ffn_halves]
     uppers = [forward_product(half, upper_w) for half in ffn_halves]
     hiddens = [low(swiglu(gate, upper)) for gate, upper in zip(gates, uppers)]
     down_terms = low(weight_product(jnp.concatenate(hiddens, 0), back_all))
-    down_terms = down_terms.reshape(outer, nf, hidden_rows, width)
-    down_sum = ring_z.reduce(low(ring_y.reduce(down_terms, 0)), 0)
 
     def inner_grads(half):
         grad_hidden = back_product(back_halves[half], down_w)
@@ -948,76 +1544,54 @@
 
     far_gate, far_upper, far_ffn = inner_grads(1)
     near_gate, near_upper, near_ffn = inner_grads(0)
-    grad_ffn = collapse(near_ffn, far_ffn)
-
-    def inner_reduce(near, far):
-        terms = low(weight_product(ffn_all, jnp.concatenate([near, far], 0)))
-        terms = terms.reshape(outer, MEMBERS, nf, in_rows, mine)
-        total = ring_z.reduce(low(ring_y.reduce(terms, 0)), 1)
-        total = swap(low(total)).astype(jnp.float32)
-        total = total.reshape(MEMBERS, in_rows, outer, span).transpose(1, 2, 0, 3)
-        return total.reshape(in_rows, hidden_all)
-
-    gate_sum = inner_reduce(near_gate, far_gate)
-    upper_sum = inner_reduce(near_upper, far_upper)
-    down_out = [low(forward_product(after(half, grad_ffn), down_w)) for half in hiddens]
-    output = low(hidden_in + collapse(*down_out))
-
-    inputs = token_rows.astype(jnp.float32)
-    normed = low(rms_scale(inputs, gain_attn))
-    scores = (
-        jnp.einsum("blkrd,bmkd->bkrlm", queries, keys, preferred_element_type=jnp.float32) * scale
+    gate_terms = low(weight_product(ffn_all, jnp.concatenate([near_gate, far_gate], 0)))
+    upper_terms = low(weight_product(ffn_all, jnp.concatenate([near_upper, far_upper], 0)))
+    near_out, far_out = [low(forward_product(half, down_w)) for half in hiddens]
+    inner_shape = (outer, MEMBERS, nf, in_rows, mine)
+    (
+        out_core,
+        out_x,
+        gate_parts,
+        upper_parts,
+        input_grad,
+        in_sum,
+        out_sum,
+        down_sum,
+        grad_gain_attn,
+        grad_gain_ffn,
+        grad_gain_heads,
+    ) = backward(
+        nd,
+        nf,
+        length,
+        (near_ffn, far_ffn, near_out, far_out),
+        (
+            down_terms.reshape(outer, nf, hidden_rows, width),
+            gate_terms.reshape(inner_shape),
+            upper_terms.reshape(inner_shape),
+        ),
+        (token_rows, back_in, hidden_in, raw, heads, values, mixed),
+        (in_w, out_w),
+        small,
     )
-    scores = jnp.where(allowed[:, None, None], scores, masked_score)
-    weights = jnp.exp(scores - jnp.max(scores, -1, keepdims=True))
-    attention_full = weights / jnp.sum(weights, -1, keepdims=True)
-    attention = low(attention_full)
-    _, ffn_pull = jax.vjp(rms_scale, hidden_in, gain_ffn)
-    grad_hidden_in, grad_gain_ffn = ffn_pull(grad_ffn)
-    grad_hidden_in = grad_hidden_in + back_in.astype(jnp.float32)
-    grad_branch = low(grad_hidden_in)
-    out_terms = low(weight_product(mixed, grad_branch)).reshape(
-        outer, 2, 2, nf, out_rows, width
+    output = hidden_in + near_out[:count].astype(jnp.float32)
+    output = low(output + out_core.astype(jnp.float32) + out_x.astype(jnp.float32))
+
+    def all_columns(parts):
+        parts = parts.astype(jnp.float32).reshape(MEMBERS, in_rows, outer, span)
+        return parts.transpose(1, 2, 0, 3).reshape(in_rows, hidden_all)
+
+    gate_sum = all_columns(gate_parts)
+    upper_sum = all_columns(upper_parts)
+    head_sums = grad_gain_heads.reshape(HQ + KV, HD)
+    gain_terms = jnp.concatenate(
+        [
+            grad_gain_attn[0],
+            grad_gain_ffn[0],
+            jnp.sum(head_sums[:HQ], 0),
+            jnp.sum(head_sums[HQ:], 0),
+        ]
     )
-    out_sum = low(ring_core.reduce(out_terms, 2))
-    out_sum = low(ring_x.reduce(low(ring_y.reduce(out_sum, 0)), 0))
-    out_sum = ring_z.reduce(out_sum, 0)
-    grad_mixed = low(back_product(grad_branch, out_w)).reshape(batch, length, KV, group_size, HD)
-    grad_attention = jnp.einsum(
-        "blkrd,bmkd->bkrlm", grad_mixed, values, preferred_element_type=jnp.float32
-    )
-    grad_scores = low(
-        attention_full
-        * (grad_attention - jnp.sum(attention_full * grad_attention, -1, keepdims=True))
-    )
-    grad_values = jnp.einsum(
-        "bkrlm,blkrd->bmkd", attention, grad_mixed, preferred_element_type=jnp.float32
-    )
-    grad_values = low(grad_values.reshape(count, KV * HD))
-    grad_queries = (
-        jnp.einsum("bkrlm,bmkd->blkrd", grad_scores, keys, preferred_element_type=jnp.float32)
-        * scale
-    )
-    grad_keys = (
-        jnp.einsum("bkrlm,blkrd->bmkd", grad_scores, queries, preferred_element_type=jnp.float32)
-        * scale
-    )
-    _, query_pull = jax.vjp(piece, query_raw, gain_query)
-    grad_query_raw, grad_gain_query = query_pull(grad_queries.reshape(batch, length, HQ, HD))
-    _, key_pull = jax.vjp(piece, key_raw, gain_key)
-    grad_key_raw, grad_gain_key = key_pull(grad_keys)
-    grad_raw = jnp.concatenate([low(grad_query_raw), low(grad_key_raw), grad_values], 1)
-    in_terms = low(weight_product(normed, grad_raw)).reshape(
-        outer, 2, 2, nf, in_rows, attn_cols
-    )
-    in_sum = low(ring_core.reduce(in_terms, 2))
-    in_sum = low(ring_y.reduce(low(ring_x.reduce(in_sum, 1)), 0))
-    in_sum = ring_z.reduce(in_sum, 0)
-    grad_normed = back_product(grad_raw, in_w)
-    _, attn_pull = jax.vjp(rms_scale, inputs, gain_attn)
-    grad_inputs, grad_gain_attn = attn_pull(grad_normed)
-    input_grad = low(grad_inputs + grad_hidden_in)
-    gain_terms = jnp.concatenate([grad_gain_attn, grad_gain_ffn, grad_gain_query, grad_gain_key])
 
     reduced = (
         in_sum[:, : HQ * HD],

time: 483 us -> 334 us (0.69)
  Pallas kernels: 135 us -> 242 us
  waiting for transfers between devices: 99.8 us -> 0 us
  local copies, waits for them, and re-layouts: 76.6 us -> 18 us
  starting transfers between devices: 37.2 us -> 0 us
  other arithmetic: 56.7 us -> 26.4 us
  matrix products: 62.4 us -> 35.8 us
    pallas_call x0 -> x1, Pallas kernels: none -> 105 us  [backward(): pl.pallas_call(functools.partial(backward_kernel, nd, nf, length), name='...]
    ppermute x36 -> x0, waiting for transfers between devices: 99.8 us -> none  [move(): return lax.ppermute(block, AXES, pairs)]
    ppermute x36 -> x0, starting transfers between devices: 37.2 us -> none  [move(): return lax.ppermute(block, AXES, pairs)]
    reshape x8 -> x0, local copies, waits for them, and re-layouts: 18.3 us -> none  [the longest x2 7.97 us: shards(): queries = heads[:, :HQ * HD].reshape(batch, length, KV, group_size, HD)]
    convert_element_type x30 -> x14, other arithmetic: 28.9 us -> 11.1 us  [low(): return value.astype(jnp.bfloat16)]
    reduce_sum x7 -> x2, other arithmetic: 11.8 us -> 0.05 us  [the longest x1 0.02 us: shards(): jnp.sum(head_sums[:HQ], 0)]
    dot_general x4 -> x0, matrix products: 10.6 us -> none  [the longest x1 3.53 us: shards(): jnp.einsum('bkrlm,blkrd->bmkd', attention, grad_mixed, preferred_element_...]
    slice x11 -> x4, local copies, waits for them, and re-layouts: 11.6 us -> 1.47 us  [the longest x2 0.75 us: shards(): head_sums[:HQ]]
  transfers between devices with their start and end apart: 36 -> 0, of which waited for: 13 -> 0; matrix products, arithmetic and copies ran while one was open for 27% -> 0% of each run, Pallas kernels for 0% -> 0%
where the time goes in v3:
time: 334 us; the launch traced here: 330 us
  Pallas kernels  242 us (72%)
  matrix products  35.8 us (11%)
  other arithmetic  26.4 us (8%)
  local copies, waits for them, and re-layouts  18 us (5%)
  between operations  7.62 us (2%)
    pallas_call x1, Pallas kernels, backward(): pl.pallas_call(functools.partial(backward_kernel, nd, nf, length), name='...  105 us
    pallas_call x1, Pallas kernels, attend(): pl.pallas_call(functools.partial(attend_kernel, nd, nf, length), name='at...  69 us
    pallas_call x1, Pallas kernels, gather_weights(): pl.pallas_call(functools.partial(weights_kernel, nd, nf), name='gather_we...  48.7 us
    pallas_call x1, Pallas kernels, all_totals(): pl.pallas_call(functools.partial(totals_kernel, nd, nf), name='all_totals...  19.8 us
    dot_general x6, matrix products, forward_product(): return jnp.dot(left, right, preferred_element_type=jnp.float32)  12.3 us
    dot_general x3, matrix products, weight_product(): lax.dot_general(left, right, (((0,), (0,)), ((), ())), preferred_element_...  12.2 us
    dot_general x6, matrix products, back_product(): lax.dot_general(left, right, (((1,), (1,)), ((), ())), preferred_element_...  11.3 us
    convert_element_type x14, other arithmetic, low(): return value.astype(jnp.bfloat16)  11.1 us

profile of v3, /device:TPU:0, one launch (start us, length us, event | category | flops | bytes accessed | tf_op | source)
XLA Modules:
  0.0 330.1 jit_solution(18351337118376898431)
XLA Ops:
  1.0 1.1 convert_element_type.110
  7.0 48.7 %gather_weights.1 = (bf16[2,2,2,4,40,1536]{5,4,3,2,1,0:T(8,128)(2,1)}, bf16[2,2,2,4,32,1280]{5,4,3,2,1,0:T(8,128)(2,1)}, bf16[2,4,4,40,768]{4,3,2,1,0:T(8,128)(2,1)}, bf16[4,40,768]{2,1,0:T(8,128)(2,1)}) custom-call(bf16[40,1536]{1,0:T(8,128)(2,1)} %pad_maximum_fusion.1.in_ref, bf16[32,1280]{1,0:T(8,128)(2,1)} %convert_element_type.109.out_ref, ...), custom_call_target="tpu_custom_call" | custom-call | bytes 104857600 | tf_op jit(solution)/shard_map/gather_weights/pallas_call | solution.py:370
  58.7 1.6 copy-done.5
  61.3 69.0 %attend.1 = (bf16[2,4,4,40,768]{4,3,2,1,0:T(8,128)(2,1)S(1)}, bf16[2,4,4,40,768]{4,3,2,1,0:T(8,128)(2,1)S(1)}, bf16[2,4,96,1280]{3,2,1,0:T(8,128)(2,1)S(1)}, bf1...) custom-call(bf16[320,1280]{1,0:T(8,128)(2,1)S(1)} %bitcast.58, ...), custom_call_target="tpu_custom_call", output_to_operand_aliasing={{0}: (10, {})} | custom-call | tf_op jit(solution)/shard_map/attend/pallas_call | solution.py:769
  130.3 5.1 %fusion.50 = (bf16[2,320,1280]{2,1,0:T(8,128)(2,1)S(1)}, bf16[2,320,1280]{2,1,0:T(8,128)(2,1)S(1)}, bf16[2,320,1280]{2,1,0:T(8,128)(2,1)S(1)}, bf16[2,320,1280]{2,1,0:T(8,128)(2,1)S(1)}) fusion(bf16[4,320,1280]{2,1,0:T(8,128)(2,1)} %get-tuple-element.68, bf16[4,320,1280]{2,1,0:T(8,128)(2,1)} %get-tuple-element.64), kind=kLoop, calls=%fused_computation.101 | loop fusion | bytes 13107200 | tf_op jit(solution)/shard_map/slice | solution.py:1530
  135.5 1.4 fusion.58
  136.9 1.5 fusion.57
  138.4 2.1 multiply_convert_fusion
  140.5 1.4 fusion.54
  142.0 1.5 fusion.55
  143.4 2.1 multiply_convert_fusion.3
  145.5 4.2 %convolution_convert_fusion = bf16[1280,768]{1,0:T(8,128)(2,1)} fusion(bf16[1280,1280]{1,0:T(8,128)(2,1)S(1)} %bitcast.78, bf16[640,768]{1,0:T(8,128)(2,1)S(1)} %get-tuple-element.114, bf16[640,768]{1,0:T(8,128)(2,1)S(1)} %get-tuple-element.117), kind=kOutput, calls=%fused_computation.2 | convolution fusion | flops 2521497600 | bytes 7208960 | tf_op jit(solution)/shard_map/dot_general | solution.py:70
  149.7 4.1 %convolution_convert_fusion.1 = bf16[1280,768]{1,0:T(8,128)(2,1)} fusion(bf16[1280,1280]{1,0:T(8,128)(2,1)S(1)} %bitcast.79, bf16[640,768]{1,0:T(8,128)(2,1)S(1)} %get-tuple-element.113, bf16[640,768]{1,0:T(8,128)(2,1)S(1)} %get-tuple-element.116), kind=kOutput, calls=%fused_computation.3 | convolution fusion | flops 2521497600 | bytes 7208960 | tf_op jit(solution)/shard_map/dot_general | solution.py:70
  153.8 4.0 %convolution_convert_fusion.2 = bf16[768,1280]{1,0:T(8,128)(2,1)} fusion(bf16[1280,1280]{1,0:T(8,128)(2,1)S(1)} %bitcast.77, bf16[640,768]{1,0:T(8,128)(2,1)S(1)} %get-tuple-element.112, bf16[640,768]{1,0:T(8,128)(2,1)S(1)} %get-tuple-element.115), kind=kOutput, calls=%fused_computation.4 | convolution fusion | flops 2521497600 | bytes 7208960 | tf_op jit(solution)/shard_map/dot_general | solution.py:70
  157.8 2.6 convolution_convert_fusion.3.out_far
  160.4 2.7 convolution_convert_fusion.4.out_near
  163.0 1.5 fusion.59
  164.5 2.7 fusion.1.ffn_far
  167.2 1.5 fusion.56
  168.7 2.7 fusion.ffn_near
  171.4 104.7 %backward.1 = (bf16[320,1280]{1,0:T(8,128)(2,1)}, bf16[320,1280]{1,0:T(8,128)(2,1)}, bf16[4,40,768]{2,1,0:T(8,128)(2,1)}, bf16[4,40,768]{2,1,0:T(8,128)(2,1)}, b...) custom-call(bf16[640,1280]{1,0:T(8,128)(2,1)} %fusion.ffn_near, ...), custom_call_target="tpu_custom_call" | custom-call | tf_op jit(solution)/shard_map/backward/pallas_call | solution.py:1376
  276.1 1.7 multiply_reduce_fusion.1
  277.9 1.6 multiply_reduce_fusion.2
  280.7 1.7 fusion.19
  283.1 1.7 fusion.20
  285.4 1.8 multiply_reduce_fusion
  292.2 19.8 %all_totals.1 = f32[32,8,128]{2,1,0:T(8,128)} custom-call(f32[32,8,128]{2,1,0:T(8,128)} %pad.9.part_ref, f32[7,128]{1,0:T(8,128)} %broadcast_in_dim.26.square_ref), custom_call_target="tpu_custom_call" | custom-call | tf_op jit(solution)/shard_map/all_totals/pallas_call | solution.py:457
  313.6 1.5 slice_reduce_fusion
  317.3 1.3 fusion.35
  319.7 1.4 fusion.37
  322.6 1.4 fusion.39
  326.5 1.2 add_convert_fusion
  (170 shorter events, 21.4 us)
Async XLA Ops:
  1.0 57.7 %copy-start.8 = (f32[160,128]{1,0:T(8,128)}, f32[160,128]{1,0:T(8,128)S(1)}, u32[]{:S(2)}) copy-start(f32[160,128]{1,0:T(8,128)S(1)} %copy.69.sine) | copy-start | bytes 245764
  2.7 3.7 %copy-start.32 = (f32[32,1280]{1,0:T(8,128)S(1)}, f32[32,1280]{1,0:T(8,128)}, u32[]{:S(2)}) copy-start(f32[32,1280]{1,0:T(8,128)} %param.33) | copy-start | bytes 491524
  3.1 55.5 %copy-start.23 = (f32[96,1280]{1,0:T(8,128)S(1)}, f32[96,1280]{1,0:T(8,128)}, u32[]{:S(2)}) copy-start(f32[96,1280]{1,0:T(8,128)} %param.36) | copy-start | bytes 1474564
  3.3 55.4 %copy-start.2 = (bf16[2,160,1280]{2,1,0:T(8,128)(2,1)S(1)}, bf16[2,160,1280]{2,1,0:T(8,128)(2,1)}, u32[]{:S(2)}) copy-start(bf16[2,160,1280]{2,1,0:T(8,128)(2,1)} %param.27) | copy-start | bytes 2457604
  3.3 55.4 %copy-start.3 = (bf16[2,160,1280]{2,1,0:T(8,128)(2,1)S(1)}, bf16[2,160,1280]{2,1,0:T(8,128)(2,1)}, u32[]{:S(2)}) copy-start(bf16[2,160,1280]{2,1,0:T(8,128)(2,1)} %param.28) | copy-start | bytes 2457604
  55.9 74.4 %copy-start.9 = (f32[160,128]{1,0:T(8,128)}, f32[160,128]{1,0:T(8,128)S(1)}, u32[]{:S(2)}) copy-start(f32[160,128]{1,0:T(8,128)S(1)} %copy.68.cosine) | copy-start | bytes 245764
  56.9 73.3 %copy-start.13 = (f32[1,1280]{1,0:T(1,128)}, f32[1,1280]{1,0:T(1,128)S(1)}, u32[]{:S(2)}) copy-start(f32[1,1280]{1,0:T(1,128)S(1)} %broadcast_in_dim.24.gain_heads) | copy-start | bytes 15364
  57.7 72.6 %copy-start.14 = (f32[1,1280]{1,0:T(1,128)}, f32[1,1280]{1,0:T(1,128)S(1)}, u32[]{:S(2)}) copy-start(f32[1,1280]{1,0:T(1,128)S(1)} %broadcast_in_dim.10.gain_attn) | copy-start | bytes 15364
  57.7 72.6 %copy-start.15 = (f32[1,1280]{1,0:T(1,128)}, f32[1,1280]{1,0:T(1,128)S(1)}, u32[]{:S(2)}) copy-start(f32[1,1280]{1,0:T(1,128)S(1)} %broadcast_in_dim.11.gain_ffn) | copy-start | bytes 15364
  58.6 71.6 %copy-start.4 = (f32[2,160,160]{2,1,0:T(8,128)}, f32[2,160,160]{2,1,0:T(8,128)S(1)}, u32[]{:S(2)}) copy-start(f32[2,160,160]{2,1,0:T(8,128)S(1)} %and_convert_fusion.mask) | copy-start | bytes 614404
  130.3 5.1 %copy-start = (f32[320,1280]{1,0:T(8,128)}, f32[320,1280]{1,0:T(8,128)S(1)}, u32[]{:S(2)}) copy-start(f32[320,1280]{1,0:T(8,128)S(1)} %get-tuple-element.63.hidden_in) | copy-start | bytes 4915204
  130.3 5.1 %copy-start.6 = (f32[320,1280]{1,0:T(8,128)}, f32[320,1280]{1,0:T(8,128)S(1)}, u32[]{:S(2)}) copy-start(f32[320,1280]{1,0:T(8,128)S(1)} %get-tuple-element.69.raw) | copy-start | bytes 4915204
  130.3 5.1 %copy-start.7 = (bf16[320,1280]{1,0:T(8,128)(2,1)}, bf16[320,1280]{1,0:T(8,128)(2,1)S(1)}, u32[]{:S(2)}) copy-start(bf16[320,1280]{1,0:T(8,128)(2,1)S(1)} %get-tuple-element.70.heads) | copy-start | bytes 2457604
  130.3 5.1 %copy-start.10 = (bf16[320,1024]{1,0:T(8,128)(2,1)}, bf16[320,1024]{1,0:T(8,128)(2,1)S(1)}, u32[]{:S(2)}) copy-start(bf16[320,1024]{1,0:T(8,128)(2,1)S(1)} %get-tuple-element.72.mixed) | copy-start | bytes 1966084
  130.3 5.1 %copy-start.12 = (bf16[320,256]{1,0:T(8,128)(2,1)}, bf16[320,256]{1,0:T(8,128)(2,1)S(1)}, u32[]{:S(2)}) copy-start(bf16[320,256]{1,0:T(8,128)(2,1)S(1)} %get-tuple-element.71.values) | copy-start | bytes 491524
  149.7 4.1 %copy-start.17 = (bf16[4,320,1280]{2,1,0:T(8,128)(2,1)S(1)}, bf16[4,320,1280]{2,1,0:T(8,128)(2,1)}, u32[]{:S(2)}) copy-start(bf16[4,320,1280]{2,1,0:T(8,128)(2,1)} %get-tuple-element.68) | copy-start | bytes 9830404
  276.1 40.5 %copy-start.46 = (f32[2688]{0:T(1024)S(1)}, f32[2688]{0:T(1024)}, u32[]{:S(2)}) copy-start(f32[2688]{0:T(1024)} %param.51) | copy-start | bytes 32260
  276.1 40.5 %copy-start.52 = (f32[2688]{0:T(1024)S(1)}, f32[2688]{0:T(1024)}, u32[]{:S(2)}) copy-start(f32[2688]{0:T(1024)} %param.52) | copy-start | bytes 32260
  276.1 40.5 %copy-start.53 = (f32[2688]{0:T(1024)S(1)}, f32[2688]{0:T(1024)}, u32[]{:S(2)}) copy-start(f32[2688]{0:T(1024)} %param.53) | copy-start | bytes 32260
  276.1 41.2 %copy-start.24 = (f32[96,1280]{1,0:T(8,128)S(1)}, f32[96,1280]{1,0:T(8,128)}, u32[]{:S(2)}) copy-start(f32[96,1280]{1,0:T(8,128)} %get-tuple-element.83) | copy-start | bytes 1474564
  276.1 41.2 %copy-start.38 = (f32[96,1280]{1,0:T(8,128)S(1)}, f32[96,1280]{1,0:T(8,128)}, u32[]{:S(2)}) copy-start(f32[96,1280]{1,0:T(8,128)} %param.43) | copy-start | bytes 1474564
  276.1 41.1 %copy-start.39 = (f32[96,1280]{1,0:T(8,128)S(1)}, f32[96,1280]{1,0:T(8,128)}, u32[]{:S(2)}) copy-start(f32[96,1280]{1,0:T(8,128)} %param.50) | copy-start | bytes 1474564
  312.0 6.6 %copy-start.27 = (bf16[4,40,768]{2,1,0:T(8,128)(2,1)S(1)}, bf16[4,40,768]{2,1,0:T(8,128)(2,1)}, u32[]{:S(2)}) copy-start(bf16[4,40,768]{2,1,0:T(8,128)(2,1)} %get-tuple-element.82) | copy-start | bytes 737284
  322.5 2.4 copy-start.22
  322.5 2.4 copy-start.40
  322.5 2.4 copy-start.41
  322.6 3.1 copy-start.44
  322.6 3.1 copy-start.45
  322.6 3.9 %copy-start.16 = (bf16[640,1280]{1,0:T(8,128)(2,1)S(1)}, bf16[640,1280]{1,0:T(8,128)(2,1)}, u32[]{:S(2)}) copy-start(bf16[640,1280]{1,0:T(8,128)(2,1)} %convolution_convert_fusion.4.out_near) | copy-start | bytes 4915204
  322.6 3.9 %copy-start.29 = (bf16[320,1280]{1,0:T(8,128)(2,1)S(1)}, bf16[320,1280]{1,0:T(8,128)(2,1)}, u32[]{:S(2)}) copy-start(bf16[320,1280]{1,0:T(8,128)(2,1)} %get-tuple-element.74) | copy-start | bytes 2457604
  324.0 2.5 copy-start.1
  324.0 2.5 copy-start.28
  (22 other events, 38.7 us)

commit v4 on v3

--- a/solution.py
+++ b/solution.py
@@ -3,6 +3,7 @@
 
 import jax
 import jax.numpy as jnp
+import numpy as np
 from jax import lax
 from jax.experimental import pallas as pl
 from jax.experimental.pallas import tpu as pltpu
@@ -30,32 +31,21 @@
 MESH = pl.DeviceIdType.MESH
 ANYWHERE = pl.BlockSpec(memory_space=pl.ANY)
 ON_CHIP = pl.BlockSpec(memory_space=pltpu.VMEM)
+VMEM_MOST = 58 * 2**20
 
 
 def rms_scale(values, gain):
     return values * lax.rsqrt(jnp.mean(values * values, -1, keepdims=True) + norm_eps) * gain
 
 
-def rotary_tables(length, size):
-    half = size // 2
-    frequency = rope_base ** (-jnp.arange(half, dtype=jnp.float32) * 2.0 / size)
-    angles = jnp.arange(length, dtype=jnp.float32)[:, None] * frequency[None, :]
-    return (jnp.cos(angles), jnp.sin(angles))
-
-
-def rotate(vectors, cosine, sine):
-    half = vectors.shape[-1] // 2
-    first = vectors[..., :half]
-    second = vectors[..., half:]
-    cosine = cosine[:, None, :]
-    sine = sine[:, None, :]
-    return jnp.concatenate([first * cosine - second * sine, second * cosine + first * sine], -1)
-
-
-def head_norm(raw, gain, cosine, sine):
-    size = gain.shape[0]
-    shaped = raw.reshape(raw.shape[:-1] + (raw.shape[-1] // size, size))
-    return rotate(rms_scale(shaped, gain), cosine, sine)
+def rotary_tables(length):
+    half = HD // 2
+    frequency = rope_base ** (-np.arange(half, dtype=np.float64) * 2.0 / HD)
+    angles = np.arange(length, dtype=np.float64)[:, None] * frequency[None, :]
+    cosine, sine = np.cos(angles), np.sin(angles)
+    cosine = np.tile(cosine, (1, LANES // half))
+    sine = np.tile(np.concatenate([-sine, sine], 1), (1, LANES // HD))
+    return jnp.asarray(cosine, jnp.float32), jnp.asarray(sine, jnp.float32)
 
 
 def swiglu(gate, upper):
@@ -141,13 +131,25 @@
 def weights_kernel(
     nd,
     nf,
+    query_full,
+    key_full,
+    value_full,
+    out_full,
+    gate_full,
+    up_full,
+    in_w,
+    out_w,
+    gate_w,
+    upper_w,
+    w_query,
+    w_key,
+    w_value,
+    w_out,
+    w_gate,
+    w_up,
     in_ref,
     out_ref,
     inner_ref,
-    in_w,
-    out_w,
-    gate_w,
-    upper_x,
     z_send,
     z_recv,
     y_send,
@@ -164,7 +166,10 @@
     gate_recv,
     over_send,
     over_recv,
+    up_send,
+    up_recv,
     local_sem,
+    load_sem,
 ):
     outer = nd // MEMBERS
     dp = lax.axis_index("dp")
@@ -196,6 +201,29 @@
     peers += [x_peer, core_peer, in_group(MEMBERS - 1 - member)]
     for peer in peers:
         pl.semaphore_signal(barrier, inc=1, device_id=peer, device_id_type=MESH)
+    fulls = (query_full, key_full, value_full, out_full, gate_full, up_full)
+    loads = [
+        pltpu.make_async_copy(full, here, load_sem.at[index])
+        for index, (full, here) in enumerate(
+            zip(fulls, (w_query, w_key, w_value, w_out, w_gate, w_up))
+        )
+    ]
+    start_all(loads)
+    for copy in loads:
+        copy.wait()
+    column = 0
+    for weight in (w_query, w_key, w_value):
+        in_ref[:, column : column + weight.shape[1]] = weight[...].astype(jnp.bfloat16)
+        column += weight.shape[1]
+    out_ref[...] = w_out[...].astype(jnp.bfloat16)
+    span = inner_ref.shape[3] // outer
+    for half, weight in enumerate((w_gate, w_up)):
+        for k in range(MEMBERS):
+            for part in range(outer):
+                column = (part * MEMBERS + k) * span
+                inner_ref[half, k, :, part * span : (part + 1) * span] = weight[
+                    :, column : column + span
+                ].astype(jnp.bfloat16)
     pl.semaphore_wait(barrier, len(peers))
 
     def remote(source, target, send, recv, device):
@@ -236,7 +264,7 @@
             )
     masks = (2, 1, 3)
     trades = {}
-    for half, target in ((0, gate_w.at[y, :, z]), (1, upper_x)):
+    for half, target in ((0, gate_w.at[y, :, z]), (1, upper_w.at[y, :, z])):
         for mask in masks:
             other = member ^ mask
             trades[half, mask] = send(
@@ -284,39 +312,46 @@
     local[2].wait()
     gates = {}
     gate_own = gate_w.at[y, :, z]
+
+    def gate_to_y(step):
+        piece = gate_w.at[y, :, from_z(step)]
+        for hop in range(1, outer):
+            gates[hop, step] = send(
+                remote(
+                    piece, piece, over_send.at[hop, step], over_recv.at[hop, step], y_peer(hop)
+                )
+            )
+
     for step in range(1, nf):
-        gates[step] = send(
+        gates[0, step] = send(
             remote(gate_own, gate_own, gate_send.at[step], gate_recv.at[step], z_peer(step))
         )
-    for hop in range(1, outer):
-        gates[-hop] = send(
-            remote(gate_own, gate_own, over_send.at[hop], over_recv.at[hop], y_peer(hop))
-        )
+    gate_to_y(0)
+    for mask in masks:
+        trades[1, mask].wait_recv()
+    local[3].wait()
+    upper_own = upper_w.at[y, :, z]
+    uppers = [
+        send(remote(upper_own, upper_own, up_send.at[step], up_recv.at[step], z_peer(step)))
+        for step in early_steps(nf)
+    ]
     hops = {}
-    for step in range(nf):
-        x_copies[0, step].wait_recv()
-        for hop in range(1, outer):
-            hops[0, hop, step] = send(
-                remote(
-                    block(0, step, ox=1 - x),
-                    block(0, step, ox=1 - x),
-                    hop_send.at[0, hop, step],
-                    hop_recv.at[0, hop, step],
-                    y_peer(hop),
+    for a in range(2):
+        for step in range(nf):
+            for hop in range(1, outer):
+                y_copies[a, hop, step].wait_recv()
+                hops[a, hop, step] = send(
+                    remote(
+                        block(a, step, oy=from_y(hop)),
+                        block(a, step, oy=from_y(hop)),
+                        hop_send.at[a, hop, step],
+                        hop_recv.at[a, hop, step],
+                        x_peer,
+                    )
                 )
-            )
-    for step in range(nf):
-        for hop in range(1, outer):
-            y_copies[1, hop, step].wait_recv()
-            hops[1, hop, step] = send(
-                remote(
-                    block(1, step, oy=from_y(hop)),
-                    block(1, step, oy=from_y(hop)),
-                    hop_send.at[1, hop, step],
-                    hop_recv.at[1, hop, step],
-                    x_peer,
-                )
-            )
+    for step in range(1, nf):
+        gates[0, step].wait_recv()
+        gate_to_y(step)
     cores = {}
 
     def to_core(a, hop, far):
@@ -334,152 +369,78 @@
     local[0].wait()
     local[1].wait()
     for a in range(2):
-        to_core(a, 0, 0)
-    to_core(0, 0, 1)
-    for hop in range(1, outer):
+        for hop in range(outer):
+            to_core(a, hop, 0)
+    for a in range(2):
         for step in range(nf):
-            y_copies[0, hop, step].wait_recv()
-        to_core(0, hop, 0)
-        to_core(1, hop, 0)
-    for step in range(nf):
-        x_copies[1, step].wait_recv()
-    to_core(1, 0, 1)
+            x_copies[a, step].wait_recv()
+        to_core(a, 0, 1)
     for a in range(2):
         for hop in range(1, outer):
             for step in range(nf):
                 hops[a, hop, step].wait_recv()
             to_core(a, hop, 1)
-    for mask in masks:
-        trades[1, mask].wait_recv()
-    local[3].wait()
-    for key in gates:
-        gates[key].wait_recv()
+    for copy in uppers:
+        copy.wait_recv()
+    for hop in range(1, outer):
+        for step in range(nf):
+            gates[hop, step].wait_recv()
     for key in cores:
         cores[key].wait_recv()
     for copy in sent:
         copy.wait_send()
 
 
-def gather_weights(nd, nf, shard_in, shard_out, inner):
+def early_steps(nf):
+    return sorted({1, nf - 1})
+
+
+def gather_weights(nd, nf, shards_here):
     outer = nd // MEMBERS
     dma = pltpu.SemaphoreType.DMA
     lead = (outer, 2, 2, nf)
     low_type = jnp.bfloat16
-    pairs = [(2, nf), (2, outer, nf), (2, nf), (2, outer, nf), (2, outer, 2), (2, 4), (nf,), (outer,)]
-    moved = 2 * nd * nf * (shard_in.size + shard_out.size)
+    w_query, w_key, w_value, w_out, w_gate, w_up = shards_here
+    in_shape = (w_query.shape[0], w_query.shape[1] + w_key.shape[1] + w_value.shape[1])
+    inner = (w_gate.shape[0], w_gate.shape[1] // MEMBERS)
+    pairs = [(2, nf), (2, outer, nf), (2, nf), (2, outer, nf), (2, outer, 2), (2, MEMBERS)]
+    pairs += [(nf,), (outer, nf), (nf,)]
     return pl.pallas_call(
         functools.partial(weights_kernel, nd, nf),
         name="gather_weights",
         out_shape=(
-            jax.ShapeDtypeStruct(lead + shard_in.shape, low_type),
-            jax.ShapeDtypeStruct(lead + shard_out.shape, low_type),
-            jax.ShapeDtypeStruct((outer, MEMBERS, nf) + inner.shape[2:], low_type),
-            jax.ShapeDtypeStruct((MEMBERS,) + inner.shape[2:], low_type),
+            jax.ShapeDtypeStruct(lead + in_shape, low_type),
+            jax.ShapeDtypeStruct(lead + w_out.shape, low_type),
+            jax.ShapeDtypeStruct((outer, MEMBERS, nf) + inner, low_type),
+            jax.ShapeDtypeStruct((outer, MEMBERS, nf) + inner, low_type),
         ),
-        in_specs=[ANYWHERE] * 3,
+        in_specs=[ANYWHERE] * 6,
         out_specs=(ANYWHERE,) * 4,
-        scratch_shapes=[dma(shape) for shape in pairs for _ in range(2)] + [dma((4,))],
-        cost_estimate=pl.CostEstimate(flops=0, bytes_accessed=16 * moved, transcendentals=0),
-        compiler_params=pltpu.CompilerParams(collective_id=0, has_side_effects=True),
-    )(shard_in, shard_out, inner)
-
-
-def totals_kernel(nd, nf, part_ref, square_ref, all_ref, pieces, own, p_send, p_recv, q_send, q_recv):
-    total = nd * nf
-    dp = lax.axis_index("dp")
-    z = lax.axis_index("fsdp")
-    me = dp * nf + z
-
-    def device(step):
-        index = lax.rem(me + step, total)
-        return index, (index // nf, lax.rem(index, nf))
-
-    barrier = pltpu.get_barrier_semaphore()
-
-    def greet(step, carry):
-        pl.semaphore_signal(barrier, inc=1, device_id=device(step)[1], device_id_type=MESH)
-        return carry
-
-    lax.fori_loop(1, total, greet, 0)
-    pl.semaphore_wait(barrier, total - 1)
-
-    def part(step):
-        index, there = device(step)
-        return pltpu.make_async_remote_copy(
-            src_ref=part_ref.at[index],
-            dst_ref=pieces.at[me],
-            send_sem=p_send.at[step],
-            recv_sem=p_recv.at[step],
-            device_id=there,
-            device_id_type=MESH,
-        )
-
-    def share(step):
-        _, there = device(step)
-        return pltpu.make_async_remote_copy(
-            src_ref=own,
-            dst_ref=all_ref.at[me],
-            send_sem=q_send.at[step],
-            recv_sem=q_recv.at[step],
-            device_id=there,
-            device_id_type=MESH,
-        )
-
-    def begin(make):
-        def step_once(step, carry):
-            make(step).start()
-            return carry
-
-        lax.fori_loop(1, total, step_once, 0)
-
-    def finish(make):
-        def step_once(step, carry):
-            make(step).wait()
-            return carry
-
-        lax.fori_loop(1, total, step_once, 0)
-
-    begin(part)
-    pieces[me] = part_ref[me]
-    finish(part)
-    summed = jnp.sum(pieces[...], 0)
-    own[...] = jnp.concatenate([summed[:1], square_ref[...]], 0)
-    begin(share)
-    all_ref[me] = own[...]
-    finish(share)
-
-
-def all_totals(nd, nf, parts, square):
-    total = nd * nf
-    parts = jnp.pad(parts[:, None, :], ((0, 0), (0, 7), (0, 0)))
-    square = jnp.broadcast_to(square, (7, LANES))
-    dma = pltpu.SemaphoreType.DMA
-    result = pl.pallas_call(
-        functools.partial(totals_kernel, nd, nf),
-        name="all_totals",
-        out_shape=jax.ShapeDtypeStruct((total, 8, LANES), jnp.float32),
-        in_specs=[ON_CHIP] * 2,
-        out_specs=ON_CHIP,
-        scratch_shapes=[
-            pltpu.VMEM((total, 8, LANES), jnp.float32),
-            pltpu.VMEM((8, LANES), jnp.float32),
+        scratch_shapes=[pltpu.VMEM(weight.shape, weight.dtype) for weight in shards_here]
+        + [
+            pltpu.VMEM(in_shape, low_type),
+            pltpu.VMEM(w_out.shape, low_type),
+            pltpu.VMEM((2, MEMBERS) + inner, low_type),
         ]
-        + [dma((total,))] * 4,
-        compiler_params=pltpu.CompilerParams(collective_id=1, has_side_effects=True),
-    )(parts, square)
-    return result[:, 0], jnp.sum(result[:, 1, 0])
+        + [dma(shape) for shape in pairs for _ in range(2)]
+        + [dma((4,)), dma((6,))],
+        compiler_params=pltpu.CompilerParams(
+            collective_id=0, has_side_effects=True, vmem_limit_bytes=VMEM_MOST
+        ),
+    )(*shards_here)
 
 
 def block_mean():
     row = lax.broadcasted_iota(jnp.int32, (LANES, LANES), 0) // HD
     column = lax.broadcasted_iota(jnp.int32, (LANES, LANES), 1) // HD
-    return jnp.where(row == column, 1.0 / HD, 0.0)
+    return jnp.where(row == column, 1.0 / HD, 0.0).astype(jnp.bfloat16)
 
 
 def head_mean(values, averages):
-    return jnp.dot(
-        values, averages, preferred_element_type=jnp.float32, precision=lax.Precision.HIGHEST
-    )
+    high = values.astype(jnp.bfloat16)
+    rest = (values - high.astype(jnp.float32)).astype(jnp.bfloat16)
+    total = jnp.dot(high, averages, preferred_element_type=jnp.float32)
+    return total + jnp.dot(rest, averages, preferred_element_type=jnp.float32)
 
 
 def swap_halves(values):
@@ -497,6 +458,19 @@
     return jnp.where(lane == target, wide, 0.0).astype(values.dtype)
 
 
+def split_gains(gains):
+    width = (gains.shape[1] - 2 * HD) // 2
+    heads = gains[:, pl.ds(2 * width, 2 * HD)]
+    other = pltpu.roll(heads, HD, 1)
+    first = lax.broadcasted_iota(jnp.int32, heads.shape, 1) < HD
+    query, key = jnp.where(first, heads, other), jnp.where(first, other, heads)
+
+    def of_tile(index):
+        return jnp.where(index < HQ * HD // LANES, query, key)
+
+    return gains[:, pl.ds(0, width)], gains[:, pl.ds(width, width)], of_tile
+
+
 def tile_of(index, width=LANES):
     return pl.ds(pl.multiple_of(index * width, LANES), width)
 
@@ -522,20 +496,16 @@
     nd,
     nf,
     length,
-    tokens,
-    in_w,
-    out_w,
-    gain_attn,
-    gain_ffn,
-    gain_heads,
+    gains,
     cosine,
     sine,
     mask,
-    cot,
-    gate_in,
-    upper_x,
-    down_x,
-    gate_w,
+    tokens_full,
+    down_full,
+    in_full,
+    out_full,
+    cot_full,
+    upper_in,
     upper_w,
     down_w,
     back_all,
@@ -547,8 +517,12 @@
     hidden_in,
     normed,
     ffn_in,
-    gate_send,
-    gate_recv,
+    tokens,
+    w_down,
+    in_w,
+    out_w,
+    down_x,
+    cot,
     uz_send,
     uz_recv,
     uy_send,
@@ -585,6 +559,22 @@
     peers += [x_peer, core_peer]
     for peer in peers:
         pl.semaphore_signal(barrier, inc=1, device_id=peer, device_id_type=MESH)
+    gain_attn, gain_ffn, gain_heads = split_gains(gains)
+    weights_here = []
+    operands = (
+        (down_full, w_down),
+        (cot_full, cot),
+        (tokens_full, tokens),
+        (in_full, in_w),
+        (out_full, out_w),
+    )
+    for index, (source, target) in enumerate(operands):
+        copy = pltpu.make_async_copy(source, target, local_sem.at[4 + index])
+        copy.start()
+        weights_here.append(copy)
+    for _ in range(2):
+        weights_here.pop(0).wait()
+    down_x[...] = w_down[...].astype(jnp.bfloat16)
     pl.semaphore_wait(barrier, len(peers))
     sent = []
 
@@ -607,39 +597,65 @@
         return copy
 
     arrivals = []
-    for step in range(1, nf):
-        piece = gate_w.at[y, :, from_z(step)]
+    upper_own = upper_w.at[y, :, z]
+    down_own = down_w.at[y, z]
+    steps_left = [step for step in range(1, nf) if step not in early_steps(nf)]
+    upper_z = {
+        step: remote(upper_own, upper_own, uz_send.at[step], uz_recv.at[step], z_peer(step))
+        for step in steps_left
+    }
+
+    def upper_to_y(step):
+        if step in upper_z:
+            upper_z[step].wait_recv()
+        piece = upper_w.at[y, :, from_z(step)]
         for hop in range(1, outer):
             arrivals.append(
-                remote(piece, piece, gate_send.at[hop, step], gate_recv.at[hop, step], y_peer(hop))
+                remote(piece, piece, uy_send.at[hop, step], uy_recv.at[hop, step], y_peer(hop))
             )
-    upper_own = upper_w.at[y, :, z]
-    down_own = down_w.at[y, z]
-    upper_z = [
-        remote(upper_x, upper_own, uz_send.at[step], uz_recv.at[step], z_peer(step))
+
+    for step in [0] + early_steps(nf):
+        upper_to_y(step)
+    down_z = [
+        remote(down_x, down_own, dz_send.at[step], dz_recv.at[step], z_peer(step))
         for step in range(1, nf)
     ]
-    for hop in range(1, outer):
-        arrivals.append(
-            remote(upper_x, upper_own, uy_send.at[hop, 0], uy_recv.at[hop, 0], y_peer(hop))
-        )
-    kept = [keep(0, upper_x, upper_own), keep(1, down_x, down_own), keep(2, cot, back_all.at[0])]
-    cot_near = remote(cot, back_all.at[1], row_send.at[0], row_recv.at[0], core_peer)
-    cot_far = remote(cot, back_all.at[2], row_send.at[1], row_recv.at[1], x_peer)
+    kept = [keep(1, down_x, down_own), keep(2, cot, back_all.at[0])]
+    cot_near = remote(cot, back_all.at[1], row_send.at[0, 0], row_recv.at[0, 0], core_peer)
+    cot_far = remote(cot, back_all.at[2], row_send.at[0, 1], row_recv.at[0, 1], x_peer)
+
+    def down_to_y(step):
+        if step:
+            down_z[step - 1].wait_recv()
+        piece = down_w.at[y, from_z(step)] if step else down_x
+        for hop in range(1, outer):
+            arrivals.append(
+                remote(
+                    piece,
+                    down_w.at[y, from_z(step)],
+                    dy_send.at[hop, step],
+                    dy_recv.at[hop, step],
+                    y_peer(hop),
+                )
+            )
 
     count = tokens.shape[0]
     width = tokens.shape[1]
     chunk = 32
+
+    weights_here.pop(0).wait()
 
     def norm_rows(index, carry):
         rows = rows_of(index, chunk)
         part = tokens[rows, :].astype(jnp.float32)
         scale = lax.rsqrt(jnp.mean(part * part, -1, keepdims=True) + norm_eps)
-        normed[rows, :] = (part * scale * gain_attn[...]).astype(jnp.bfloat16)
+        normed[rows, :] = (part * scale * gain_attn).astype(jnp.bfloat16)
         return carry
 
     lax.fori_loop(0, count // chunk, norm_rows, 0)
     head_tiles = (HQ + KV) * HD // LANES
+    for copy in weights_here:
+        copy.wait()
 
     def project(index, carry):
         columns = tile_of(index, 2 * LANES)
@@ -660,7 +676,7 @@
             rows = pl.ds(row * length, length)
             part = raw[rows, columns]
             scale = lax.rsqrt(head_mean(part * part, averages) + norm_eps)
-            part = part * scale * gain_heads[:, columns]
+            part = part * scale * gain_heads(index)
             part = part * cosine[...] + swap_halves(part) * sine[...]
             heads[rows, columns] = part.astype(jnp.bfloat16)
         return carry
@@ -690,57 +706,70 @@
 
         lax.fori_loop(0, KV * HD // LANES, pair, 0)
 
-    for row in range(count // length):
+    down_steps = list(range(nf))
+    ffn_far, ffn_near = [], []
+
+    def finish(row):
+        rows = pl.ds(row * length, length)
+
+        def project_out(index, carry):
+            columns = tile_of(index, 2 * LANES)
+            hidden_in[rows, columns] = tokens[rows, columns].astype(jnp.float32) + jnp.dot(
+                mixed[rows, :], out_w[:, columns], preferred_element_type=jnp.float32
+            )
+            return carry
+
+        lax.fori_loop(0, width // (2 * LANES), project_out, 0)
+
+        def norm_hidden(index, carry):
+            part_rows = pl.ds(pl.multiple_of(row * length + index * chunk, 16), chunk)
+            part = hidden_in[part_rows, :]
+            scale = lax.rsqrt(jnp.mean(part * part, -1, keepdims=True) + norm_eps)
+            ffn_in[part_rows, :] = (part * scale * gain_ffn).astype(jnp.bfloat16)
+            return carry
+
+        lax.fori_loop(0, length // chunk, norm_hidden, 0)
+        for slot, peer, copies in ((2, x_peer, ffn_far), (1, core_peer, ffn_near)):
+            copies.append(
+                remote(
+                    ffn_in.at[rows],
+                    ffn_all.at[slot, rows],
+                    row_send.at[slot, row],
+                    row_recv.at[slot, row],
+                    peer,
+                )
+            )
+
+    batch = count // length
+    for row in range(batch):
         attend(row)
-
-    def project_out(index, carry):
-        columns = tile_of(index, 2 * LANES)
-        hidden_in[:, columns] = tokens[:, columns].astype(jnp.float32) + jnp.dot(
-            mixed[...], out_w[:, columns], preferred_element_type=jnp.float32
+        finish(row)
+        if row == 0:
+            for step in steps_left:
+                upper_to_y(step)
+            down_to_y(down_steps.pop(0))
+    kept.append(keep(3, ffn_in, ffn_all.at[0]))
+
+    cot_far.wait_recv()
+    cot_cross = remote(
+        back_all.at[2], back_all.at[3], row_send.at[0, 2], row_recv.at[0, 2], core_peer
+    )
+    while len(down_steps) > 1:
+        down_to_y(down_steps.pop(0))
+    for row in range(batch):
+        rows = pl.ds(row * length, length)
+        ffn_far[row].wait_recv()
+        ffn_near.append(
+            remote(
+                ffn_all.at[2, rows],
+                ffn_all.at[3, rows],
+                row_send.at[3, row],
+                row_recv.at[3, row],
+                core_peer,
+            )
         )
-        return carry
-
-    lax.fori_loop(0, width // (2 * LANES), project_out, 0)
-
-    def norm_hidden(index, carry):
-        rows = rows_of(index, chunk)
-        part = hidden_in[rows, :]
-        scale = lax.rsqrt(jnp.mean(part * part, -1, keepdims=True) + norm_eps)
-        ffn_in[rows, :] = (part * scale * gain_ffn[...]).astype(jnp.bfloat16)
-        return carry
-
-    lax.fori_loop(0, count // chunk, norm_hidden, 0)
-    ffn_far = remote(ffn_in, ffn_all.at[2], row_send.at[3], row_recv.at[3], x_peer)
-    ffn_near = remote(ffn_in, ffn_all.at[1], row_send.at[4], row_recv.at[4], core_peer)
-    kept.append(keep(3, ffn_in, ffn_all.at[0]))
-
-    cot_far.wait_recv()
-    cot_cross = remote(back_all.at[2], back_all.at[3], row_send.at[2], row_recv.at[2], core_peer)
-    for step in range(1, nf):
-        upper_z[step - 1].wait_recv()
-        piece = upper_w.at[y, :, from_z(step)]
-        for hop in range(1, outer):
-            arrivals.append(
-                remote(piece, piece, uy_send.at[hop, step], uy_recv.at[hop, step], y_peer(hop))
-            )
-    down_z = [
-        remote(down_x, down_own, dz_send.at[step], dz_recv.at[step], z_peer(step))
-        for step in range(1, nf)
-    ]
-    for hop in range(1, outer):
-        arrivals.append(
-            remote(down_x, down_own, dy_send.at[hop, 0], dy_recv.at[hop, 0], y_peer(hop))
-        )
-    ffn_far.wait_recv()
-    ffn_cross = remote(ffn_all.at[2], ffn_all.at[3], row_send.at[5], row_recv.at[5], core_peer)
-    for step in range(1, nf):
-        down_z[step - 1].wait_recv()
-        piece = down_w.at[y, from_z(step)]
-        for hop in range(1, outer):
-            arrivals.append(
-                remote(piece, piece, dy_send.at[hop, step], dy_recv.at[hop, step], y_peer(hop))
-            )
-    for copy in arrivals + [cot_near, cot_cross, ffn_near, ffn_cross]:
+    down_to_y(nf - 1)
+    for copy in arrivals + ffn_near + [cot_near, cot_cross]:
         copy.wait_recv()
     for copy in sent:
         copy.wait_send()
@@ -748,16 +777,15 @@
         copy.wait()
 
 
-def attend(nd, nf, length, tokens, in_w, out_w, small, cot, gate_w, upper_x, down_x):
+def attend(nd, nf, length, small, tokens, w_down, in_w, out_w, cot, upper_w):
     outer = nd // MEMBERS
     count, width = tokens.shape
     lo, hi = jnp.bfloat16, jnp.float32
     dma = pltpu.SemaphoreType.DMA
-    moves = [(outer, nf), (nf,), (outer, nf), (nf,), (outer, nf), (6,)]
+    moves = [(nf,), (outer, nf), (nf,), (outer, nf), (4, max(3, count // length))]
     shapes = [
-        (gate_w.shape, lo),
-        (gate_w.shape, lo),
-        ((outer, nf) + down_x.shape, lo),
+        (upper_w.shape, lo),
+        ((outer, nf) + w_down.shape, lo),
         ((MEMBERS, count, width), lo),
         ((MEMBERS, count, width), lo),
         ((count, (HQ + KV) * HD), hi),
@@ -766,48 +794,52 @@
         ((count, HQ * HD), lo),
         ((count, width), hi),
     ]
+    early = [(count, width), (count, width), (count, width)]
+    late = [in_w.shape, out_w.shape, w_down.shape, (count, width)]
     return pl.pallas_call(
         functools.partial(attend_kernel, nd, nf, length),
         name="attend",
         out_shape=tuple(jax.ShapeDtypeStruct(*item) for item in shapes),
-        in_specs=[ON_CHIP] * 9 + [ANYWHERE] * 4,
-        out_specs=(ANYWHERE,) * 5 + (ON_CHIP,) * 5,
-        input_output_aliases={10: 0},
-        scratch_shapes=[pltpu.VMEM((count, width), lo), pltpu.VMEM((count, width), lo)]
+        in_specs=[ON_CHIP] * 4 + [ANYWHERE] * 6,
+        out_specs=(ANYWHERE,) * 4 + (ON_CHIP,) * 5,
+        input_output_aliases={9: 0},
+        scratch_shapes=[pltpu.VMEM(shape, lo) for shape in early]
+        + [pltpu.VMEM(w_down.shape, hi)]
+        + [pltpu.VMEM(shape, lo) for shape in late]
         + [dma(shape) for shape in moves for _ in range(2)]
-        + [dma((4,))],
+        + [dma((10,))],
         compiler_params=pltpu.CompilerParams(
-            collective_id=2, has_side_effects=True, vmem_limit_bytes=40 * 2**20
+            collective_id=2, has_side_effects=True, vmem_limit_bytes=VMEM_MOST
         ),
-    )(tokens, in_w, out_w, *small, cot, gate_w, upper_x, down_x)
+    )(*small, tokens, w_down, in_w, out_w, cot, upper_w)
 
 
 def backward_kernel(
     nd,
     nf,
     length,
-    ffn_near,
-    ffn_far,
+    gains,
+    cosine,
+    sine,
+    mask,
     out_near,
     out_far,
+    down_got,
     down_terms,
     gate_terms,
     upper_terms,
-    tokens,
-    cot,
-    hidden_in,
-    raw,
-    heads,
-    values,
-    mixed,
-    in_w,
-    out_w,
-    gain_attn,
-    gain_ffn,
-    gain_heads,
-    cosine,
-    sine,
-    mask,
+    mine_full,
+    near_full,
+    far_full,
+    hidden_full,
+    cot_full,
+    out_w_full,
+    mixed_full,
+    heads_full,
+    values_full,
+    tokens_full,
+    raw_full,
+    in_w_full,
     out_core,
     out_x,
     gate_parts,
@@ -816,14 +848,31 @@
     in_sum,
     out_sum,
     down_sum,
+    gain_totals,
+    norm,
     sum_attn,
     sum_ffn,
     sum_heads,
+    gain_here,
+    gain_group,
+    gain_got,
+    gain_far,
+    square_here,
+    square_group,
+    square_got,
+    square_far,
     mine_ref,
-    pass_ref,
     core_near,
-    core_far,
     from_x,
+    hidden_in,
+    cot,
+    out_w,
+    mixed,
+    heads,
+    values,
+    tokens,
+    raw,
+    in_w,
     out_pass,
     out_core_far,
     normed,
@@ -871,7 +920,13 @@
     ay_recv,
     az_send,
     az_recv,
+    tg_send,
+    tg_recv,
+    tf_send,
+    tf_recv,
     load_sem,
+    got_sem,
+    operand_sem,
     local_sem,
 ):
     outer = nd // MEMBERS
@@ -903,6 +958,26 @@
     barrier = pltpu.get_barrier_semaphore()
     peers = [z_peer(step) for step in range(1, nf)] + [y_peer(step) for step in range(1, outer)]
     peers += [x_peer, core_peer, in_group(MEMBERS - 1 - member)]
+    crossed = [(hop, step) for hop in range(outer) for step in range(nf) if hop or step]
+
+    def cross_peer(hop, step):
+        return (y_to(hop) * MEMBERS + member, z_to(step))
+
+    peers += [cross_peer(hop, step) for hop, step in crossed if hop and step]
+    fulls = (mine_full, near_full, far_full, hidden_full, cot_full, out_w_full, mixed_full)
+    fulls += (heads_full, values_full, tokens_full, raw_full, in_w_full)
+    places = (mine_ref, core_near, from_x, hidden_in, cot, out_w, mixed)
+    places += (heads, values, tokens, raw, in_w)
+    operands = [
+        pltpu.make_async_copy(source, target, operand_sem.at[index])
+        for index, (source, target) in enumerate(zip(fulls, places))
+    ]
+    start_all(operands)
+
+    def ready(number):
+        for _ in range(number):
+            operands.pop(0).wait()
+
     for peer in peers:
         pl.semaphore_signal(barrier, inc=1, device_id=peer, device_id_type=MESH)
     pl.semaphore_wait(barrier, len(peers))
@@ -926,16 +1001,13 @@
         copy.start()
         return copy
 
+    gain_attn, gain_ffn, gain_heads = split_gains(gains)
     count, width = tokens.shape
     here, there = pl.ds(0, count), pl.ds(count, count)
 
-    far_copy = remote(ffn_far.at[there], core_far, row_send.at[0], row_recv.at[0], core_peer)
-    pass_copy = keep(local_sem.at[0], ffn_far.at[here], pass_ref)
-    near_copy = remote(ffn_near.at[there], core_near, row_send.at[1], row_recv.at[1], core_peer)
-    mine_copy = keep(local_sem.at[1], ffn_near.at[here], mine_ref)
-    out_far_copy = remote(out_far.at[there], out_core_far, row_send.at[2], row_recv.at[2], core_peer)
-    out_pass_copy = keep(local_sem.at[2], out_far.at[here], out_pass)
-    out_near_copy = remote(out_near.at[there], out_core, row_send.at[3], row_recv.at[3], core_peer)
+    out_far_copy = remote(out_far.at[there], out_core_far, row_send.at[0], row_recv.at[0], core_peer)
+    out_pass_copy = keep(local_sem.at[0], out_far.at[here], out_pass)
+    out_near_copy = remote(out_near.at[there], out_core, row_send.at[1], row_recv.at[1], core_peer)
 
     terms = (down_terms, gate_terms, upper_terms)
     owns = (down_own, gate_own, upper_own)
@@ -954,6 +1026,11 @@
             load_sem.at[matrix, step], piece_of(matrix, y, step), owns[matrix].at[step]
         )
         for hop in range(1, outer):
+            if matrix == 0:
+                y_copies[0, step, hop] = keep(
+                    got_sem.at[hop, step], down_got.at[hop - 1, z_to(step)], down_y.at[hop - 1, step]
+                )
+                continue
             y_copies[matrix, step, hop] = remote(
                 piece_of(matrix, y_to(hop), step),
                 over_y[matrix].at[hop - 1, step],
@@ -970,7 +1047,10 @@
             loads[matrix, step].wait()
             total = owns[matrix][step].astype(hi)
             for hop in range(1, outer):
-                y_copies[matrix, step, hop].wait_recv()
+                if matrix:
+                    y_copies[matrix, step, hop].wait_recv()
+                else:
+                    y_copies[0, step, hop].wait()
                 total = total + over_y[matrix][hop - 1, step].astype(hi)
             owns[matrix][step] = total.astype(lo)
             if step:
@@ -991,8 +1071,13 @@
 
     swaps = []
 
+    squares = []
+
     def trade(matrix, parts):
-        owns[matrix][0] = piece_total(matrix).astype(lo)
+        total = piece_total(matrix).astype(lo)
+        owns[matrix][0] = total
+        total = total.astype(hi)
+        squares.append(jnp.sum(total * total))
         for mask_bits in range(1, MEMBERS):
             other = member ^ mask_bits
             swaps.append(
@@ -1011,8 +1096,38 @@
     swaps_local = []
     chunk = 32
 
-    far_copy.wait_recv()
-    pass_copy.wait()
+    def to_group(index, source, target):
+        target[member] = source[...]
+        return [
+            remote(
+                source,
+                target.at[member],
+                tg_send.at[index, mask_bits],
+                tg_recv.at[index, mask_bits],
+                in_group(member ^ mask_bits),
+            )
+            for mask_bits in range(1, MEMBERS)
+        ]
+
+    def to_crossed(index, source, target):
+        target[y * nf + z] = source[...]
+        return [
+            remote(
+                source,
+                target.at[y * nf + z],
+                tf_send.at[index, place],
+                tf_recv.at[index, place],
+                cross_peer(hop, step),
+            )
+            for place, (hop, step) in enumerate(crossed)
+        ]
+
+    def summed(got, copies):
+        for copy in copies:
+            copy.wait_recv()
+        return jnp.sum(got[...], 0)
+
+    pieces(nf)
 
     def add_rows(target, other):
         def step_once(index, carry):
@@ -1022,28 +1137,17 @@
 
         lax.fori_loop(0, count // chunk, step_once, 0)
 
-    add_rows(pass_ref, core_far)
-    x_copy = remote(pass_ref, from_x, row_send.at[4], row_recv.at[4], x_peer)
-    out_far_copy.wait_recv()
-    out_pass_copy.wait()
-    add_rows(out_pass, out_core_far)
-    out_x_copy = remote(out_pass, out_x, row_send.at[5], row_recv.at[5], x_peer)
-
     def norm_rows(index, carry):
         rows = rows_of(index, chunk)
         part = tokens[rows, :].astype(hi)
         scale = lax.rsqrt(jnp.mean(part * part, -1, keepdims=True) + norm_eps)
-        normed[rows, :] = (part * scale * gain_attn[...]).astype(lo)
+        normed[rows, :] = (part * scale * gain_attn).astype(lo)
         return carry
 
-    lax.fori_loop(0, count // chunk, norm_rows, 0)
     sum_attn[...] = jnp.zeros_like(sum_attn)
     sum_ffn[...] = jnp.zeros_like(sum_ffn)
     sum_heads[...] = jnp.zeros_like(sum_heads)
-    pieces(3)
-    near_copy.wait_recv()
-    mine_copy.wait()
-    x_copy.wait_recv()
+    ready(5)
 
     def norm_back(part, gain, grad):
         scale = lax.rsqrt(jnp.mean(part * part, -1, keepdims=True) + norm_eps)
@@ -1056,7 +1160,7 @@
         rows = rows_of(index, chunk)
         grad = mine_ref[rows, :].astype(hi) + core_near[rows, :].astype(hi)
         grad = grad + from_x[rows, :].astype(hi)
-        back, gain_term = norm_back(hidden_in[rows, :], gain_ffn[...], grad)
+        back, gain_term = norm_back(hidden_in[rows, :], gain_ffn, grad)
         sum_ffn[...] += gain_term
         back = back + cot[rows, :].astype(hi)
         grad_hidden[rows, :] = back
@@ -1065,6 +1169,7 @@
 
     lax.fori_loop(0, count // chunk, ffn_norm_back, 0)
     pair = 2 * LANES
+    ready(2)
 
     def mixed_back(index, carry):
         columns = tile_of(index, pair)
@@ -1202,6 +1307,7 @@
     outer_product(mixed, branch, out_terms)
     core_out(1)
     pieces(2)
+    ready(len(operands))
     query_tiles = HQ * HD // LANES
     head_tiles = (HQ + KV) * HD // LANES
     key_tiles = KV * HD // LANES
@@ -1253,14 +1359,14 @@
     batch = count // length
     for row in range(batch):
         attend_back(row)
-        pieces(2)
         if row == 0:
             core_in(1)
+        pieces(1)
     averages = block_mean()
 
     def turn_back(index, carry):
         columns = tile_of(index)
-        gain = gain_heads[:, columns]
+        gain = gain_heads(index)
         for row in range(batch):
             rows = pl.ds(row * length, length)
             grad = wide[rows, columns]
@@ -1275,6 +1381,7 @@
         return carry
 
     lax.fori_loop(0, head_tiles, turn_back, 0)
+    lax.fori_loop(0, count // chunk, norm_rows, 0)
     outer_product(normed, grad_raw, in_terms)
     core_out(0)
     pieces(1)
@@ -1286,26 +1393,55 @@
         return carry
 
     core_in(0)
+    out_far_copy.wait_recv()
+    out_pass_copy.wait()
+    add_rows(out_pass, out_core_far)
+    out_x_copy = remote(out_pass, out_x, row_send.at[2], row_recv.at[2], x_peer)
     lax.fori_loop(0, width // pair, normed_back, 0)
 
     def attn_norm_back(index, carry):
         rows = rows_of(index, chunk)
-        back, gain_term = norm_back(tokens[rows, :].astype(hi), gain_attn[...], wide[rows, :])
+        back, gain_term = norm_back(tokens[rows, :].astype(hi), gain_attn, wide[rows, :])
         sum_attn[...] += gain_term
         input_grad[rows, :] = (back + grad_hidden[rows, :]).astype(lo)
         return carry
 
     lax.fori_loop(0, count // chunk, attn_norm_back, 0)
+    gain_here[...] = jnp.zeros_like(gain_here)
+    place = 0
+    for source in (sum_attn, sum_ffn, sum_heads):
+        for tile in range(source.shape[1] // LANES):
+            gain_here[pl.ds(place, 1), :] = source[:, tile * LANES : (tile + 1) * LANES]
+            place += 1
+    gain_copies = to_group(0, gain_here, gain_got)
+    pieces(1)
+    x_in(0)
     down_sum[...] = piece_total(0)
-    pieces(2)
-    x_in(0)
     y_in(1)
     pieces(2 * nf)
     trade(1, gate_parts)
     y_in(0)
+    gain_group[...] = summed(gain_got, gain_copies)
+    gain_copies = to_crossed(0, gain_group, gain_far)
     z_in(1, out_sum)
     trade(2, upper_parts)
     z_in(0, in_sum)
+    for target in (down_sum, out_sum, in_sum):
+        squares.append(jnp.sum(target[...] * target[...]))
+    square_here[...] = jnp.full(square_here.shape, sum(squares))
+    square_copies = to_group(1, square_here, square_got)
+    square_group[...] = summed(square_got, square_copies)
+    square_copies = to_crossed(1, square_group, square_far)
+    gain_totals[...] = summed(gain_far, gain_copies)
+    gain_place = 2 * width // LANES
+    gain_squares = gain_totals[:gain_place, :]
+    gain_squares = jnp.sum(gain_squares * gain_squares)
+    for first, last in ((0, query_tiles), (query_tiles, head_tiles)):
+        total = jnp.sum(gain_totals[gain_place + first : gain_place + last, :], 0, keepdims=True)
+        total = jnp.broadcast_to(total, (8, LANES))
+        total = total + pltpu.roll(total, HD, 1)
+        gain_squares += jnp.sum(total * total) / (8 * LANES // HD)
+    norm[...] = jnp.sqrt(summed(square_far, square_copies) + gain_squares)
     for copy in swaps + [out_near_copy, out_x_copy]:
         copy.wait_recv()
     for copy in sent:
@@ -1314,17 +1450,20 @@
         copy.wait()
 
 
-def backward(nd, nf, length, halves, terms, rows, weights, small):
+def backward(nd, nf, length, small, halves, terms, operands):
     outer = nd // MEMBERS
-    count, width = rows[0].shape
-    in_w, out_w = weights
-    down_terms, gate_terms, _ = terms
+    count, width = operands[0].shape
+    out_w, in_w = operands[5], operands[-1]
+    _, down_terms, gate_terms, _ = terms
     lo, hi = jnp.bfloat16, jnp.float32
     dma = pltpu.SemaphoreType.DMA
     in_rows, in_cols = in_w.shape[0] // (nd * nf), in_w.shape[1]
     out_rows, out_cols = out_w.shape[0] // (nd * nf), out_w.shape[1]
     inner = (MEMBERS,) + gate_terms.shape[3:]
     down = down_terms.shape[2:]
+    tiles = (2 * width + (HQ + KV) * HD) // LANES
+    gain_tile = (-(-tiles // 8) * 8, LANES)
+    far = outer * nf - 1
     shapes = [
         ((count, width), lo),
         ((count, width), lo),
@@ -1334,12 +1473,15 @@
         ((in_rows, in_cols), hi),
         ((out_rows, out_cols), hi),
         (down, hi),
-        ((1, width), hi),
-        ((1, width), hi),
-        ((1, (HQ + KV) * HD), hi),
+        (gain_tile, hi),
+        ((8, LANES), hi),
     ]
     in_block, out_block = (nf * in_rows, in_cols), (nf * out_rows, out_cols)
-    scratch = [((count, width), lo)] * 7
+    scratch = [((1, width), hi), ((1, width), hi), ((1, (HQ + KV) * HD), hi)]
+    for tile in (gain_tile, (8, LANES)):
+        scratch += [(tile, hi), (tile, hi), ((MEMBERS,) + tile, hi), ((outer * nf,) + tile, hi)]
+    scratch += [(operand.shape, operand.dtype) for operand in operands]
+    scratch += [((count, width), lo)] * 2
     scratch += [
         ((count, width), lo),
         ((count, width), lo),
@@ -1371,21 +1513,177 @@
         ((nf - 1,) + inner, lo),
         ((nf - 1,) + inner, lo),
     ]
-    moves = [(6,), (3, outer, nf), (3, nf), (2, MEMBERS), (2, outer, 2), (2, outer), (2, outer)]
-    moves += [(2, nf)]
+    moves = [(3,), (3, outer, nf), (3, nf), (2, MEMBERS), (2, outer, 2), (2, outer), (2, outer)]
+    moves += [(2, nf), (2, MEMBERS), (2, far)]
     return pl.pallas_call(
         functools.partial(backward_kernel, nd, nf, length),
         name="backward",
         out_shape=tuple(jax.ShapeDtypeStruct(*item) for item in shapes),
-        in_specs=[ANYWHERE] * 7 + [ON_CHIP] * 15,
-        out_specs=(ANYWHERE,) * 4 + (ON_CHIP,) * 7,
+        in_specs=[ON_CHIP] * 4 + [ANYWHERE] * (6 + len(operands)),
+        out_specs=(ANYWHERE,) * 4 + (ON_CHIP,) * 6,
         scratch_shapes=[pltpu.VMEM(*item) for item in scratch]
         + [dma(shape) for shape in moves for _ in range(2)]
-        + [dma((3, nf)), dma((5,))],
+        + [dma((3, nf)), dma((outer, nf)), dma((len(operands),)), dma((5,))],
         compiler_params=pltpu.CompilerParams(
-            collective_id=3, has_side_effects=True, vmem_limit_bytes=58 * 2**20
+            collective_id=3, has_side_effects=True, vmem_limit_bytes=VMEM_MOST
         ),
-    )(*halves, *terms, *rows, *weights, *small)
+    )(*small, *halves, *terms, *operands)
+
+
+def adam_kernel(
+    span, norm, gain_totals, in_sum, out_sum, gate_parts, upper_parts, down_sum, *rest
+):
+    count = 8
+    row_terms, rest = rest[:4], rest[4:]
+    masters, firsts, seconds = rest[:count], rest[count : 2 * count], rest[2 * count : 3 * count]
+    rest = rest[3 * count :]
+    outs = [rest[index * count : (index + 1) * count] for index in range(3)]
+    copies = rest[3 * count : 4 * count - 1]
+    output = rest[4 * count - 1]
+    rest = rest[4 * count :]
+    ins_here = [rest[index * count : (index + 1) * count] for index in range(3)]
+    rest = rest[3 * count :]
+    outs_here = [rest[index * count : (index + 1) * count] for index in range(3)]
+    copies_here = rest[3 * count : 4 * count - 1]
+    sums_here = rest[4 * count - 1 : 4 * count + 4]
+    terms_here = rest[4 * count + 4 : 4 * count + 8]
+    output_here, sum_sem, in_sem, out_sem, term_sem = rest[4 * count + 8 :]
+    sums = (in_sum, out_sum, gate_parts, upper_parts, down_sum)
+    loads = {}
+    for index in (6, 4, 5, 3, 0, 1, 2, 7):
+        source = {6: 4, 4: 2, 5: 3, 3: 1, 0: 0}.get(index)
+        if source is not None:
+            loads[source] = pltpu.make_async_copy(
+                sums[source], sums_here[source], sum_sem.at[source]
+            )
+            loads[source].start()
+        for kind, arrays in enumerate((masters, firsts, seconds)):
+            loads[index, kind] = pltpu.make_async_copy(
+                arrays[index], ins_here[kind][index], in_sem.at[kind, index]
+            )
+            loads[index, kind].start()
+    rows_count = output.shape[0]
+    term_loads = []
+    for index, (source, target) in enumerate(zip(row_terms, terms_here)):
+        copy = pltpu.make_async_copy(
+            source.at[pl.ds(0, rows_count)], target, term_sem.at[index]
+        )
+        copy.start()
+        term_loads.append(copy)
+    stores = []
+
+    def store(index):
+        pairs = [(outs_here[kind][index], outs[kind][index]) for kind in range(3)]
+        if index < count - 1:
+            pairs.append((copies_here[index], copies[index]))
+        for kind, (source, target) in enumerate(pairs):
+            copy = pltpu.make_async_copy(source, target, out_sem.at[kind, index])
+            copy.start()
+            stores.append(copy)
+
+    factor = jnp.minimum(1.0, clip_limit / (norm[0:1, 0:1] + 1e-06))
+    weight_rate = 2.0 * D ** (-0.5)
+
+    def update(index, columns, grad, rate, decay):
+        grad = grad * factor
+        master, first, second = (ins_here[kind][index][:, columns] for kind in range(3))
+        new, second_new = adam_update(master, first, second, grad, rate, decay)
+        outs_here[0][index][:, columns] = grad
+        outs_here[1][index][:, columns] = new
+        outs_here[2][index][:, columns] = second_new
+        if index < count - 1:
+            copies_here[index][:, columns] = new.astype(jnp.bfloat16)
+
+    def arrived(index):
+        for kind in range(3):
+            loads[index, kind].wait()
+
+    step = 2 * LANES
+    loads[4].wait()
+    arrived(6)
+    for start in range(0, down_sum.shape[1], step):
+        columns = slice(start, start + step)
+        update(6, columns, sums_here[4][:, columns], weight_rate, decay_rate)
+    store(6)
+    members, _, mine = gate_parts.shape
+    for index in (4, 5):
+        loads[index - 2].wait()
+        arrived(index)
+        place = 0
+        for part in range(mine // span):
+            for member in range(members):
+                grad = sums_here[index - 2][member, :, part * span : (part + 1) * span]
+                columns = slice(place, place + span)
+                update(index, columns, grad.astype(jnp.float32), weight_rate, decay_rate)
+                place += span
+        store(index)
+    loads[1].wait()
+    arrived(3)
+    for start in range(0, out_sum.shape[1], step):
+        columns = slice(start, start + step)
+        update(3, columns, sums_here[1][:, columns], weight_rate, decay_rate)
+    store(3)
+    loads[0].wait()
+    place = 0
+    for index in range(3):
+        arrived(index)
+        for start in range(0, masters[index].shape[1], step):
+            grad = sums_here[0][:, place : place + step]
+            update(index, slice(start, start + step), grad, weight_rate, decay_rate)
+            place += step
+        store(index)
+    arrived(7)
+    norm_rows = 2 * D // LANES
+    head_rows = HQ * HD // LANES
+    key_rows = KV * HD // LANES
+    folded = []
+    for first, size in ((norm_rows, head_rows), (norm_rows + head_rows, key_rows)):
+        total = jnp.sum(gain_totals[first : first + size, :], 0, keepdims=True)
+        folded.append(total + pltpu.roll(jnp.broadcast_to(total, (8, LANES)), HD, 1)[:1])
+    lane = lax.broadcasted_iota(jnp.int32, (1, LANES), 1)
+    heads = jnp.where(lane < HD, folded[0], folded[1])
+    gain_grad = jnp.concatenate([gain_totals[:norm_rows, :], heads], 0)
+    update(7, slice(None), gain_grad, gain_rate, 0.0)
+    store(7)
+    for copy in term_loads:
+        copy.wait()
+
+    def add_rows(index, carry):
+        rows = rows_of(index, 32)
+        total = terms_here[0][rows, :]
+        for term in terms_here[1:]:
+            total = total + term[rows, :].astype(jnp.float32)
+        output_here[rows, :] = total.astype(jnp.bfloat16)
+        return carry
+
+    lax.fori_loop(0, rows_count // 32, add_rows, 0)
+    copy = pltpu.make_async_copy(output_here, output, term_sem.at[0])
+    copy.start()
+    stores.append(copy)
+    for copy in stores:
+        copy.wait()
+
+
+def adam(span, norm, gain_totals, sums, row_terms, masters, firsts, seconds):
+    lo, hi = jnp.bfloat16, jnp.float32
+    dma = pltpu.SemaphoreType.DMA
+    shapes = [(array.shape, hi) for _ in range(3) for array in masters]
+    shapes += [(array.shape, lo) for array in masters[:-1]]
+    rows_shape = row_terms[0].shape
+    inputs = [(array.shape, hi) for _ in range(3) for array in masters]
+    scratch = inputs + shapes + [(array.shape, array.dtype) for array in sums]
+    scratch += [(rows_shape, array.dtype) for array in row_terms] + [(rows_shape, lo)]
+    shapes += [(rows_shape, lo)]
+    return pl.pallas_call(
+        functools.partial(adam_kernel, span),
+        name="adam",
+        out_shape=tuple(jax.ShapeDtypeStruct(*item) for item in shapes),
+        in_specs=[ON_CHIP] * 2 + [ANYWHERE] * (9 + len(inputs)),
+        out_specs=(ANYWHERE,) * len(shapes),
+        scratch_shapes=[pltpu.VMEM(*item) for item in scratch]
+        + [dma((5,)), dma((3, len(masters))), dma((4, len(masters))), dma((4,))],
+        compiler_params=pltpu.CompilerParams(vmem_limit_bytes=VMEM_MOST),
+    )(norm, gain_totals, *sums, *row_terms, *masters, *firsts, *seconds)
 
 
 def after(value, *others):
@@ -1469,47 +1767,23 @@
     batch, length, width = tokens.shape
     count = batch * length
     hidden_rows = w_down.shape[0]
-    hidden_all = w_gate.shape[1]
     span = nf * hidden_rows
     mine = outer * span
     in_rows = w_query.shape[0]
     out_rows = w_out.shape[0]
     attn_cols = (HQ + 2 * KV) * HD
 
-    shard_in = jnp.concatenate([low(w_query), low(w_key), low(w_value)], 1)
-    shard_out = low(w_out)
-
-    def member_columns(weight):
-        cut = low(weight).reshape(in_rows, outer, MEMBERS, span).transpose(2, 0, 1, 3)
-        return cut.reshape(MEMBERS, in_rows, mine)
-
-    columns = jnp.stack([member_columns(w_gate), member_columns(w_up)])
-    in_w, out_w, gate_w, upper_x = gather_weights(nd, nf, shard_in, shard_out, columns)
+    in_w, out_w, gate_w, upper_w = gather_weights(nd, nf, masters[:6])
     in_w = in_w.reshape(D, attn_cols)
     out_w = out_w.reshape(HQ * HD, D)
 
-    gain_attn = gains[:D]
-    gain_ffn = gains[D : 2 * D]
-    gain_query = gains[2 * D : 2 * D + HD]
-    gain_key = gains[2 * D + HD :]
     positions = jnp.arange(length)
     causal = positions[None, :] <= positions[:, None]
     allowed = causal[None] & (segment_ids[:, :, None] == segment_ids[:, None, :])
-    cosine, sine = rotary_tables(length, HD)
-    scale = HD ** (-0.5)
-    group_size = HQ // KV
-    small = (
-        gain_attn[None],
-        gain_ffn[None],
-        jnp.concatenate([jnp.tile(gain_query, HQ), jnp.tile(gain_key, KV)])[None],
-        jnp.tile(cosine, (1, 2 * LANES // HD)),
-        jnp.tile(jnp.concatenate([-sine, sine], 1), (1, LANES // HD)),
-        allowed.astype(jnp.float32),
-    )
+    small = (gains[None], *rotary_tables(length), allowed.astype(jnp.float32))
     back_in = cotangent.reshape(count, width)
     token_rows = tokens.reshape(count, width)
     (
-        gate_w,
         upper_w,
         down_w,
         back_all,
@@ -1520,7 +1794,7 @@
         mixed,
         hidden_in,
     ) = attend(
-        nd, nf, length, token_rows, in_w, out_w, small, back_in, gate_w, upper_x, low(w_down)
+        nd, nf, length, small, token_rows, w_down, in_w, out_w, back_in, upper_w
     )
     gate_w = gate_w.reshape(D, mine)
     upper_w = upper_w.reshape(D, mine)
@@ -1529,24 +1803,37 @@
     ffn_all = ffn_all.reshape(MEMBERS * count, width)
     back_halves = (back_all[: 2 * count], back_all[2 * count :])
     ffn_halves = (ffn_all[: 2 * count], ffn_all[2 * count :])
-    gates = [forward_product(half, gate_w) for half in ffn_halves]
-    uppers = [forward_product(half, upper_w) for half in ffn_halves]
-    hiddens = [low(swiglu(gate, upper)) for gate, upper in zip(gates, uppers)]
-    down_terms = low(weight_product(jnp.concatenate(hiddens, 0), back_all))
-
-    def inner_grads(half):
-        grad_hidden = back_product(back_halves[half], down_w)
-        _, pull = jax.vjp(swiglu, gates[half], uppers[half])
+    def inner_grads(back_half, gate, upper):
+        grad_hidden = back_product(back_half, down_w)
+        _, pull = jax.vjp(swiglu, gate, upper)
         grad_gate, grad_upper = pull(grad_hidden)
         grad_gate, grad_upper = low(grad_gate), low(grad_upper)
         back = back_product(grad_gate, gate_w) + back_product(grad_upper, upper_w)
         return grad_gate, grad_upper, low(back)
 
-    far_gate, far_upper, far_ffn = inner_grads(1)
-    near_gate, near_upper, near_ffn = inner_grads(0)
+    near_half, far_half = ffn_halves
+    gate, upper = forward_product(far_half, gate_w), forward_product(far_half, upper_w)
+    far_hidden = low(swiglu(gate, upper))
+    far_gate, far_upper, far_ffn = inner_grads(back_halves[1], gate, upper)
+    far = far_ffn[:count].astype(jnp.float32) + ring_core.move(far_ffn[count:], 1)
+    far = low(far)
+    ffn_x = ring_x.move(far, 1)
+    gate = forward_product(after(near_half, far_ffn), gate_w)
+    upper = forward_product(after(near_half, far), upper_w)
+    near_hidden = low(swiglu(gate, upper))
+    down_terms = low(weight_product(jnp.concatenate([near_hidden, far_hidden], 0), back_all))
+    down_terms = down_terms.reshape(outer, nf, hidden_rows, width)
+    down_sent = [pick(down_terms, 0, ring_y.dest(hop)) for hop in range(1, outer)]
+    down_got = jnp.stack([ring_y.move(part, hop + 1) for hop, part in enumerate(down_sent)])
+    near_gate, near_upper, near_ffn = inner_grads(after(back_halves[0], *down_sent), gate, upper)
+    ffn_core = ring_core.move(near_ffn[count:], 1)
+    ffn_all = after(ffn_all, near_ffn)
     gate_terms = low(weight_product(ffn_all, jnp.concatenate([near_gate, far_gate], 0)))
     upper_terms = low(weight_product(ffn_all, jnp.concatenate([near_upper, far_upper], 0)))
-    near_out, far_out = [low(forward_product(half, down_w)) for half in hiddens]
+    near_out, far_out = [
+        low(forward_product(after(half, near_ffn, ffn_x, down_got), down_w))
+        for half in (near_hidden, far_hidden)
+    ]
     inner_shape = (outer, MEMBERS, nf, in_rows, mine)
     (
         out_core,
@@ -1557,81 +1844,50 @@
         in_sum,
         out_sum,
         down_sum,
-        grad_gain_attn,
-        grad_gain_ffn,
-        grad_gain_heads,
+        gain_totals,
+        norm,
     ) = backward(
         nd,
         nf,
         length,
-        (near_ffn, far_ffn, near_out, far_out),
+        small,
+        (near_out, far_out),
         (
-            down_terms.reshape(outer, nf, hidden_rows, width),
+            down_got,
+            down_terms,
             gate_terms.reshape(inner_shape),
             upper_terms.reshape(inner_shape),
         ),
-        (token_rows, back_in, hidden_in, raw, heads, values, mixed),
-        (in_w, out_w),
-        small,
+        (
+            near_ffn[:count],
+            ffn_core,
+            ffn_x,
+            hidden_in,
+            back_in,
+            out_w,
+            mixed,
+            heads,
+            values,
+            token_rows,
+            raw,
+            in_w,
+        ),
     )
-    output = hidden_in + near_out[:count].astype(jnp.float32)
-    output = low(output + out_core.astype(jnp.float32) + out_x.astype(jnp.float32))
-
-    def all_columns(parts):
-        parts = parts.astype(jnp.float32).reshape(MEMBERS, in_rows, outer, span)
-        return parts.transpose(1, 2, 0, 3).reshape(in_rows, hidden_all)
-
-    gate_sum = all_columns(gate_parts)
-    upper_sum = all_columns(upper_parts)
-    head_sums = grad_gain_heads.reshape(HQ + KV, HD)
-    gain_terms = jnp.concatenate(
-        [
-            grad_gain_attn[0],
-            grad_gain_ffn[0],
-            jnp.sum(head_sums[:HQ], 0),
-            jnp.sum(head_sums[HQ:], 0),
-        ]
+    tiled = [array.reshape(-1, LANES) for array in (gains, gain_first, gain_second)]
+    results = adam(
+        span,
+        norm,
+        gain_totals,
+        (in_sum, out_sum, gate_parts, upper_parts, down_sum),
+        (hidden_in, near_out, out_core, out_x),
+        masters + (tiled[0],),
+        firsts + (tiled[1],),
+        seconds + (tiled[2],),
     )
-
-    reduced = (
-        in_sum[:, : HQ * HD],
-        in_sum[:, HQ * HD : (HQ + KV) * HD],
-        in_sum[:, (HQ + KV) * HD :],
-        out_sum,
-        gate_sum,
-        upper_sum,
-        down_sum,
-    )
-    local_squares = (
-        jnp.sum(in_sum * in_sum)
-        + jnp.sum(out_sum * out_sum)
-        + jnp.sum(gate_sum * gate_sum)
-        + jnp.sum(upper_sum * upper_sum)
-        + jnp.sum(down_sum * down_sum)
-    )
-    gain_size = gains.shape[0]
-    share = -(-gain_size // (nd * nf))
-    gain_terms = jnp.pad(gain_terms, (0, share * nd * nf - gain_size)).reshape(nd * nf, share)
-    gain_terms = jnp.pad(gain_terms, ((0, 0), (0, LANES - share)))
-    gain_total, square_total = all_totals(nd, nf, gain_terms, local_squares)
-    gain_total = gain_total[:, :share].reshape(-1)[:gain_size]
-    total_norm = jnp.sqrt(square_total + jnp.sum(gain_total * gain_total))
-    factor = jnp.minimum(1.0, clip_limit / (total_norm + 1e-06))
-    clipped = tuple((share * factor for share in reduced))
-    gain_clipped = gain_total * factor
-    weight_rate = 2.0 * D ** (-0.5)
-    updates = [
-        adam_update(
-            masters[index], firsts[index], seconds[index], clipped[index], weight_rate, decay_rate
-        )
-        for index in range(7)
-    ]
-    new_masters = tuple((item[0] for item in updates))
-    new_seconds = tuple((item[1] for item in updates))
-    new_gains, gain_seconds = adam_update(
-        gains, gain_first, gain_second, gain_clipped, gain_rate, 0.0
-    )
-    copies = tuple((low(item) for item in new_masters))
+    clipped, new_masters, new_seconds = results[:7], results[8:15], results[16:23]
+    gain_clipped, new_gains, gain_seconds = (results[k].reshape(-1) for k in (7, 15, 23))
+    copies, output = tuple(results[24:31]), results[31]
+    total_norm = norm[0, 0]
     return (
         (output.reshape(tokens.shape), input_grad.reshape(tokens.shape))
         + clipped

time: 334 us -> 290 us (0.87)
  other arithmetic: 26.4 us -> 1.84 us
  Pallas kernels: 242 us -> 224 us
  waiting for transfers between devices: 0 us -> 6.74 us
  between operations: 7.62 us -> 1.42 us
    pallas_call x1, Pallas kernels: 19.8 us -> 7.53 us  [adam(): pl.pallas_call(functools.partial(adam_kernel, span), name='adam', out_sha...]
    convert_element_type x14 -> x1, other arithmetic: 11.1 us -> 0.22 us  [low(): return value.astype(jnp.bfloat16)]
    reduce_sum x9 -> x0, other arithmetic: 10.6 us -> none  [the longest x1 1.76 us: shards(): jnp.sum(down_sum * down_sum)]
    ppermute x0 -> x4, waiting for transfers between devices: none -> 6.74 us  [move(): return lax.ppermute(block, AXES, pairs)]
    pallas_call x1, Pallas kernels: 48.7 us -> 55.4 us  [gather_weights(): pl.pallas_call(functools.partial(weights_kernel, nd, nf), name='gather_we...]
    pallas_call x1, Pallas kernels: 69 us -> 62.4 us  [attend(): pl.pallas_call(functools.partial(attend_kernel, nd, nf, length), name='at...]
    pallas_call x1, Pallas kernels: 105 us -> 98.2 us  [backward(): pl.pallas_call(functools.partial(backward_kernel, nd, nf, length), name='...]
  transfers between devices with their start and end apart: 0 -> 4, of which waited for: 0 -> 1; matrix products, arithmetic and copies ran while one was open for 0% -> 10% of each run, Pallas kernels for 0% -> 0%
where the time goes in v4:
time: 290 us; the launch traced here: 286 us
  Pallas kernels  224 us (77%)
  matrix products  35.4 us (12%)
  local copies, waits for them, and re-layouts  15.9 us (5%)
  waiting for transfers between devices  6.74 us (2%)
    pallas_call x1, Pallas kernels, backward(): pl.pallas_call(functools.partial(backward_kernel, nd, nf, length), name='...  98.2 us
    pallas_call x1, Pallas kernels, attend(): pl.pallas_call(functools.partial(attend_kernel, nd, nf, length), name='at...  62.4 us
    pallas_call x1, Pallas kernels, gather_weights(): pl.pallas_call(functools.partial(weights_kernel, nd, nf), name='gather_we...  55.4 us
    dot_general x6, matrix products, forward_product(): return jnp.dot(left, right, preferred_element_type=jnp.float32)  14.9 us
    dot_general x3, matrix products, weight_product(): lax.dot_general(left, right, (((0,), (0,)), ((), ())), preferred_element_...  10.8 us
    dot_general x6, matrix products, back_product(): lax.dot_general(left, right, (((1,), (1,)), ((), ())), preferred_element_...  9.66 us
    pallas_call x1, Pallas kernels, adam(): pl.pallas_call(functools.partial(adam_kernel, span), name='adam', out_sha...  7.53 us
    ppermute x4, waiting for transfers between devices, move(): return lax.ppermute(block, AXES, pairs)  6.74 us
  transfers between devices with their start and end apart: 4, of which 1 were waited for; matrix products, arithmetic and copies ran while one was open for 10% of the time, Pallas kernels for 0%

profile of v4, /device:TPU:0, one launch (start us, length us, event | category | flops | bytes accessed | tf_op | source)
XLA Modules:
  0.0 286.2 jit_solution(13009276252917452331)
XLA Ops:
  0.7 1.3 broadcast_in_dim.2.gains
  2.0 1.6 and_convert_fusion.mask
  3.6 55.4 %gather_weights.1 = (bf16[2,2,2,4,40,1536]{5,4,3,2,1,0:T(8,128)(2,1)}, bf16[2,2,2,4,32,1280]{5,4,3,2,1,0:T(8,128)(2,1)}, bf16[2,4,4,40,768]{4,3,2,1,0:T(8,128)(2,1)}, bf16[2,4,4,40,768]{4,3,2,1,0:T(8,128)(2,1)}) custom-call(f32[40,1024]{1,0:T(8,128)} %rest_4_.1, f32[40,256]{1,0:T(8,128)} %rest_5_.1, f32[40,256]{1,0:T(8,128)} %rest_6_.1, f32[32,1280]{1,0:T(8,128)} %rest_7_.1, ...), custom_call_target="tpu_custom_call" | custom-call | tf_op jit(solution)/shard_map/gather_weights/pallas_call | solution.py:408
  59.0 62.4 %attend.1 = (bf16[2,4,4,40,768]{4,3,2,1,0:T(8,128)(2,1)}, bf16[2,4,96,1280]{3,2,1,0:T(8,128)(2,1)}, bf16[4,320,1280]{2,1,0:T(8,128)(2,1)}, bf16[4,320,1280]{2,1,...) custom-call(f32[1,2688]{1,0:T(1,128)} %broadcast_in_dim.2.gains, ...), custom_call_target="tpu_custom_call", output_to_operand_aliasing={{0}: (9, {})} | custom-call | tf_op jit(solution)/shard_map/attend/pallas_call | solution.py:799
  121.4 5.2 %fusion.22 = (bf16[2,320,1280]{2,1,0:T(8,128)(2,1)}, bf16[2,320,1280]{2,1,0:T(8,128)(2,1)S(1)}, bf16[2,320,1280]{2,1,0:T(8,128)(2,1)}, bf16[2,320,1280]{2,1,0:T(8,128)(2,1)S(1)}) fusion(bf16[4,320,1280]{2,1,0:T(8,128)(2,1)} %get-tuple-element.99, bf16[4,320,1280]{2,1,0:T(8,128)(2,1)} %get-tuple-element.98), kind=kLoop, calls=%fused_computation.41 | loop fusion | bytes 13107200 | tf_op jit(solution)/shard_map/slice | solution.py:1804
  126.6 1.4 fusion.26
  128.2 1.5 fusion.25
  129.7 3.1 %multiply_convert_fusion.1 = (bf16[640,768]{1,0:T(8,128)(2,1)}, bf16[640,768]{1,0:T(8,128)(2,1)S(1)}, bf16[640,768]{1,0:T(8,128)(2,1)S(1)}) fusion(f32[640,768]{1,0:T(8,128)S(1)} %fusion.26, f32[640,768]{1,0:T(8,128)S(1)} %fusion.25, bf16[640,1280]{1,0:T(8,128)(2,1)S(1)} %bitcast.78, bf16[1280,768]{1,0:T(8,128)(2,1)S(1)} %bitcast.68), kind=kOutput, calls=%fused_computation.27 | convolution fusion | flops 1266155520 | bytes 10485760 | tf_op jit(solution)/shard_map/dot_general | solution.py:56
  132.8 1.5 fusion.27
  134.3 1.5 fusion
  135.8 1.2 copy-done.6
  136.9 0.9 slice.53
  137.9 3.6 %fusion.28 = f32[640,768]{1,0:T(8,128)S(1)} fusion(bf16[640,1280]{1,0:T(8,128)(2,1)} %bitcast.75, bf16[1280,768]{1,0:T(8,128)(2,1)} %bitcast.89), kind=kOutput, calls=%fused_computation.47 | convolution fusion | flops 1258291200 | bytes 5570560 | tf_op jit(solution)/shard_map/dot_general | solution.py:56
  141.8 0.8 collective-permute-start.1
  142.9 1.6 multiply_convert_fusion.2
  144.6 2.8 convolution_convert_fusion.2
  147.6 2.0 copy-done.4
  149.5 2.2 multiply_convert_fusion
  151.8 1.5 fusion.29
  153.3 1.5 fusion.1
  155.5 4.0 %convolution_convert_fusion.1 = bf16[1280,768]{1,0:T(8,128)(2,1)} fusion(bf16[1280,1280]{1,0:T(8,128)(2,1)S(1)} %bitcast.61, bf16[640,768]{1,0:T(8,128)(2,1)S(1)} %copy-done.20, bf16[640,768]{1,0:T(8,128)(2,1)S(1)} %get-tuple-element.157), kind=kOutput, calls=%fused_computation.3 | convolution fusion | flops 2521497600 | bytes 7208960 | tf_op jit(solution)/shard_map/dot_general | solution.py:60
  159.5 1.0 fusion.24
  160.5 0.5 collective-permute-start.3
  161.0 4.0 %convolution_convert_fusion = bf16[1280,768]{1,0:T(8,128)(2,1)} fusion(bf16[1280,1280]{1,0:T(8,128)(2,1)S(1)} %bitcast.62, bf16[640,768]{1,0:T(8,128)(2,1)S(1)} %copy-done.17, bf16[640,768]{1,0:T(8,128)(2,1)S(1)} %get-tuple-element.156), kind=kOutput, calls=%fused_computation.2 | convolution fusion | flops 2521497600 | bytes 7208960 | tf_op jit(solution)/shard_map/dot_general | solution.py:60
  165.0 6.7 %collective-permute-done.2 = bf16[4,96,1280]{2,1,0:T(8,128)(2,1)S(1)} collective-permute-done((bf16[4,96,1280]{2,1,0:T(8,128)(2,1)S(1)}, bf16[4,96,1280]{2,1,0:T(8,128)(2,1)S(1)}, u32[]{:S(2)}, u32[]{:S(2)}) %collective-permute-start.2) | collective-permute-done | bytes 983072 | tf_op jit(solution)/shard_map/ppermute | solution.py:102
  171.7 2.6 convolution_convert_fusion.4.out_near.rest_1_
  174.3 2.6 convolution_convert_fusion.3.out_far
  177.0 0.9 copy-done.11
  177.9 98.2 %backward.1 = (bf16[320,1280]{1,0:T(8,128)(2,1)}, bf16[320,1280]{1,0:T(8,128)(2,1)}, bf16[4,40,768]{2,1,0:T(8,128)(2,1)}, bf16[4,40,768]{2,1,0:T(8,128)(2,1)}, b...) custom-call(f32[1,2688]{1,0:T(1,128)} %broadcast_in_dim.2.gains, ...), custom_call_target="tpu_custom_call" | custom-call | tf_op jit(solution)/shard_map/backward/pallas_call | solution.py:1518
  276.1 1.2 slice.51
  277.3 7.5 %adam.1 = (f32[40,1024]{1,0:T(8,128)}, f32[40,256]{1,0:T(8,128)}, f32[40,256]{1,0:T(8,128)}, f32[32,1280]{1,0:T(8,128)}, f32[40,3072]{1,0:T(8,128)}, /*index=5*/...) custom-call(f32[8,128]{1,0:T(8,128)} %get-tuple-element.114.norm, ...), custom_call_target="tpu_custom_call" | custom-call | tf_op jit(solution)/shard_map/adam/pallas_call | solution.py:1677
  284.9 0.9 copy.66
  (47 shorter events, 1.7 us)
Async XLA Ops:
  121.4 5.2 %copy-start.14 = (bf16[2,4,4,40,768]{4,3,2,1,0:T(8,128)(2,1)S(1)}, bf16[2,4,4,40,768]{4,3,2,1,0:T(8,128)(2,1)}, u32[]{:S(2)}) copy-start(bf16[2,4,4,40,768]{4,3,2,1,0:T(8,128)(2,1)} %get-tuple-element.102) | copy-start | bytes 5898244
  126.6 1.5 copy-start.12
  128.2 1.5 copy-start.3
  132.8 1.5 copy-start.19
  132.8 1.5 copy-start.16
  135.8 1.2 copy-start.6
  137.9 3.6 %collective-permute-start = (bf16[320,1280]{1,0:T(8,128)(2,1)}, bf16[320,1280]{1,0:T(8,128)(2,1)S(1)}, u32[]{:S(2)}, u32[]{:S(2)}) collective-permute-start(bf16[320,1280]{1,0:T(8,128)(2,1)} %slice.53), channel_id=1, source_target_pairs={{0,4},{1,5},{2,6},{3,7},{4,0},{5,1},{6,2},{7,3},{8,12},{9,13},{10,... | collective-permute-start | bytes 2457608 | tf_op jit(solution)/shard_map/ppermute | solution.py:102
  137.9 3.6 %copy-start.7 = (bf16[640,1280]{1,0:T(8,128)(2,1)S(1)}, bf16[640,1280]{1,0:T(8,128)(2,1)}, u32[]{:S(2)}) copy-start(bf16[640,1280]{1,0:T(8,128)(2,1)} %copy-done.6) | copy-start | bytes 4915204
  141.5 1.4 copy-start.5
  141.8 2.8 copy-start.2
  141.8 2.8 copy-start.18
  141.8 23.2 %collective-permute-start.1 = (bf16[320,1280]{1,0:T(8,128)(2,1)S(1)}, bf16[320,1280]{1,0:T(8,128)(2,1)S(1)}, u32[]{:S(2)}, u32[]{:S(2)}) collective-permute-start(bf16[320,1280]{1,0:T(8,128)(2,1)S(1)} %add_convert_fusion), channel_id=1, source_target_pairs={{0,8},{1,9},{2,10},{3,11},{4,12},{5,13},{6,14},{7,15},{8,0},{9,1},... | collective-permute-start | bytes 2457608 | tf_op jit(solution)/shard_map/ppermute | solution.py:102
  144.5 3.0 %copy-start.13 = (bf16[2,4,96,1280]{3,2,1,0:T(8,128)(2,1)S(1)}, bf16[2,4,96,1280]{3,2,1,0:T(8,128)(2,1)}, u32[]{:S(2)}) copy-start(bf16[2,4,96,1280]{3,2,1,0:T(8,128)(2,1)} %get-tuple-element.100) | copy-start | bytes 5898244
  147.4 4.4 %copy-start = (bf16[768,1280]{1,0:T(8,128)(2,1)}, bf16[768,1280]{1,0:T(8,128)(2,1)S(1)}, u32[]{:S(2)}) copy-start(bf16[768,1280]{1,0:T(8,128)(2,1)S(1)} %convolution_convert_fusion.2) | copy-start | bytes 5898244
  147.4 2.1 copy-start.4
  147.5 24.2 %collective-permute-start.2 = (bf16[4,96,1280]{2,1,0:T(8,128)(2,1)S(1)}, bf16[4,96,1280]{2,1,0:T(8,128)(2,1)S(1)}, u32[]{:S(2)}, u32[]{:S(2)}) collective-permute-start(bf16[4,96,1280]{2,1,0:T(8,128)(2,1)S(1)} %dynamic-slice_bitcast_fusion), channel_id=1, source_target_pairs={{0,16},{1,17},{2,18},{3,19},{4,20},{5,21},{6,22},{7,23},{8,24},{9,... | collective-permute-start | bytes 2949128 | tf_op jit(solution)/shard_map/ppermute | solution.py:102
  149.5 2.3 copy-start.15
  153.3 1.9 copy-start.1
  153.3 2.2 copy-start.20
  159.5 1.5 copy-start.17
  160.5 16.5 %collective-permute-start.3 = (bf16[320,1280]{1,0:T(8,128)(2,1)S(1)}, bf16[320,1280]{1,0:T(8,128)(2,1)S(1)}, u32[]{:S(2)}, u32[]{:S(2)}) collective-permute-start(bf16[320,1280]{1,0:T(8,128)(2,1)S(1)} %get-tuple-element.165), channel_id=1, source_target_pairs={{0,4},{1,5},{2,6},{3,7},{4,0},{5,1},{6,2},{7,3},{8,12},{9,13},{10,... | collective-permute-start | bytes 2457608 | tf_op jit(solution)/shard_map/ppermute | solution.py:102
  165.0 9.3 %copy-start.10 = (bf16[320,1280]{1,0:T(8,128)(2,1)}, bf16[320,1280]{1,0:T(8,128)(2,1)S(1)}, u32[]{:S(2)}) copy-start(bf16[320,1280]{1,0:T(8,128)(2,1)S(1)} %collective-permute-done.1.far_full) | copy-start | bytes 2457604
  171.7 2.6 copy-start.8
  177.0 0.9 copy-start.11
  277.3 7.5 %copy-start.9 = (bf16[320,1280]{1,0:T(8,128)(2,1)S(1)}, bf16[320,1280]{1,0:T(8,128)(2,1)}, u32[]{:S(2)}) copy-start(bf16[320,1280]{1,0:T(8,128)(2,1)} %get-tuple-element.124) | copy-start | bytes 2457604

commit v5 on v4

--- a/solution.py
+++ b/solution.py
@@ -492,6 +492,36 @@
     return weights / jnp.sum(weights, -1, keepdims=True)
 
 
+def outer_product(left, right, target):
+    pair, wide = 2 * LANES, 4 * LANES
+
+    def step_once(index, carry):
+        columns = tile_of(index, pair)
+        turned = left[:, columns].T
+        for start in range(0, right.shape[1], wide):
+            across = pl.ds(start, min(wide, right.shape[1] - start))
+            target[columns, across] = jnp.dot(
+                turned, right[:, across], preferred_element_type=jnp.float32
+            ).astype(jnp.bfloat16)
+        return carry
+
+    lax.fori_loop(0, left.shape[1] // pair, step_once, 0)
+
+
+def flatten_blocks(blocks, rows, target):
+    outer, members, nf, size, _ = blocks.shape
+
+    def step_once(index, carry):
+        for place in range(nf):
+            rows[place * size : (place + 1) * size, :] = blocks[
+                index // members, lax.rem(index, members), place
+            ].astype(jnp.float32)
+        target[rows_of(index, nf * size), :] = rows[...].astype(jnp.bfloat16)
+        return carry
+
+    lax.fori_loop(0, outer * members, step_once, 0)
+
+
 def attend_kernel(
     nd,
     nf,
@@ -506,23 +536,36 @@
     out_full,
     cot_full,
     upper_in,
+    gate_w,
     upper_w,
     down_w,
     back_all,
     ffn_all,
+    gate_out,
+    upper_out,
+    hidden_out,
+    down_terms,
     raw,
     heads,
     values,
     mixed,
     hidden_in,
     normed,
-    ffn_in,
+    ffn_here,
     tokens,
     w_down,
     in_w,
     out_w,
     down_x,
     cot,
+    gate_blocks,
+    upper_blocks,
+    block_rows,
+    gate_flat,
+    upper_flat,
+    gate_here,
+    upper_here,
+    hidden_here,
     uz_send,
     uz_recv,
     uy_send,
@@ -560,13 +603,20 @@
     for peer in peers:
         pl.semaphore_signal(barrier, inc=1, device_id=peer, device_id_type=MESH)
     gain_attn, gain_ffn, gain_heads = split_gains(gains)
+    count = tokens.shape[0]
+    width = tokens.shape[1]
+
+    def member_rows(slot):
+        return pl.ds(slot * count, count)
+
     weights_here = []
     operands = (
         (down_full, w_down),
-        (cot_full, cot),
+        (cot_full, cot.at[member_rows(0)]),
         (tokens_full, tokens),
         (in_full, in_w),
         (out_full, out_w),
+        (gate_w, gate_blocks),
     )
     for index, (source, target) in enumerate(operands):
         copy = pltpu.make_async_copy(source, target, local_sem.at[4 + index])
@@ -620,9 +670,14 @@
         remote(down_x, down_own, dz_send.at[step], dz_recv.at[step], z_peer(step))
         for step in range(1, nf)
     ]
-    kept = [keep(1, down_x, down_own), keep(2, cot, back_all.at[0])]
-    cot_near = remote(cot, back_all.at[1], row_send.at[0, 0], row_recv.at[0, 0], core_peer)
-    cot_far = remote(cot, back_all.at[2], row_send.at[0, 1], row_recv.at[0, 1], x_peer)
+    kept = [keep(1, down_x, down_own)]
+    cot_own = cot.at[member_rows(0)]
+    cot_near = remote(
+        cot_own, cot.at[member_rows(1)], row_send.at[0, 0], row_recv.at[0, 0], core_peer
+    )
+    cot_far = remote(
+        cot_own, cot.at[member_rows(2)], row_send.at[0, 1], row_recv.at[0, 1], x_peer
+    )
 
     def down_to_y(step):
         if step:
@@ -639,8 +694,6 @@
                 )
             )
 
-    count = tokens.shape[0]
-    width = tokens.shape[1]
     chunk = 32
 
     weights_here.pop(0).wait()
@@ -654,8 +707,8 @@
 
     lax.fori_loop(0, count // chunk, norm_rows, 0)
     head_tiles = (HQ + KV) * HD // LANES
-    for copy in weights_here:
-        copy.wait()
+    for _ in range(2):
+        weights_here.pop(0).wait()
 
     def project(index, carry):
         columns = tile_of(index, 2 * LANES)
@@ -725,15 +778,15 @@
             part_rows = pl.ds(pl.multiple_of(row * length + index * chunk, 16), chunk)
             part = hidden_in[part_rows, :]
             scale = lax.rsqrt(jnp.mean(part * part, -1, keepdims=True) + norm_eps)
-            ffn_in[part_rows, :] = (part * scale * gain_ffn).astype(jnp.bfloat16)
+            ffn_here[part_rows, :] = (part * scale * gain_ffn).astype(jnp.bfloat16)
             return carry
 
         lax.fori_loop(0, length // chunk, norm_hidden, 0)
         for slot, peer, copies in ((2, x_peer, ffn_far), (1, core_peer, ffn_near)):
             copies.append(
                 remote(
-                    ffn_in.at[rows],
-                    ffn_all.at[slot, rows],
+                    ffn_here.at[rows],
+                    ffn_here.at[pl.ds(slot * count + row * length, length)],
                     row_send.at[slot, row],
                     row_recv.at[slot, row],
                     peer,
@@ -747,29 +800,80 @@
         if row == 0:
             for step in steps_left:
                 upper_to_y(step)
+            uppers = list(arrivals)
+            arrivals.clear()
             down_to_y(down_steps.pop(0))
-    kept.append(keep(3, ffn_in, ffn_all.at[0]))
 
     cot_far.wait_recv()
     cot_cross = remote(
-        back_all.at[2], back_all.at[3], row_send.at[0, 2], row_recv.at[0, 2], core_peer
+        cot.at[member_rows(2)],
+        cot.at[member_rows(3)],
+        row_send.at[0, 2],
+        row_recv.at[0, 2],
+        core_peer,
     )
+    down_to_y(down_steps.pop(0))
+    weights_here.pop(0).wait()
+    flatten_blocks(gate_blocks, block_rows, gate_flat)
+    for copy in uppers:
+        copy.wait_recv()
+    kept.pop(0).wait()
+    upper_load = keep(0, upper_w, upper_blocks)
     while len(down_steps) > 1:
         down_to_y(down_steps.pop(0))
+    upper_load.wait()
+    flatten_blocks(upper_blocks, block_rows, upper_flat)
+
+    def ffn_rows(slot):
+        rows = member_rows(slot)
+
+        def tile_once(index, carry):
+            columns = tile_of(index, 2 * LANES)
+            gate = jnp.dot(
+                ffn_here[rows, :], gate_flat[:, columns], preferred_element_type=jnp.float32
+            )
+            upper = jnp.dot(
+                ffn_here[rows, :], upper_flat[:, columns], preferred_element_type=jnp.float32
+            )
+            gate_here[rows, columns] = gate
+            upper_here[rows, columns] = upper
+            hidden_here[rows, columns] = (gate / (1.0 + jnp.exp(-gate)) * upper).astype(
+                jnp.bfloat16
+            )
+            return carry
+
+        lax.fori_loop(0, gate_flat.shape[1] // (2 * LANES), tile_once, 0)
+
+    ffn_rows(0)
+    for copy in ffn_near:
+        copy.wait_recv()
+    ffn_rows(1)
+    crosses = []
     for row in range(batch):
-        rows = pl.ds(row * length, length)
         ffn_far[row].wait_recv()
-        ffn_near.append(
+        crosses.append(
             remote(
-                ffn_all.at[2, rows],
-                ffn_all.at[3, rows],
+                ffn_here.at[pl.ds(2 * count + row * length, length)],
+                ffn_here.at[pl.ds(3 * count + row * length, length)],
                 row_send.at[3, row],
                 row_recv.at[3, row],
                 core_peer,
             )
         )
     down_to_y(nf - 1)
-    for copy in arrivals + ffn_near + [cot_near, cot_cross]:
+    ffn_rows(2)
+    for copy in crosses:
+        copy.wait_recv()
+    kept.append(keep(2, ffn_here, ffn_all))
+    ffn_rows(3)
+    kept.append(keep(3, gate_here, gate_out))
+    kept.append(keep(9, upper_here, upper_out))
+    kept.append(keep(10, hidden_here, hidden_out))
+    cot_near.wait_recv()
+    cot_cross.wait_recv()
+    kept.append(keep(11, cot, back_all))
+    outer_product(hidden_here, cot, down_terms)
+    for copy in arrivals:
         copy.wait_recv()
     for copy in sent:
         copy.wait_send()
@@ -777,41 +881,50 @@
         copy.wait()
 
 
-def attend(nd, nf, length, small, tokens, w_down, in_w, out_w, cot, upper_w):
+def attend(nd, nf, length, small, tokens, w_down, in_w, out_w, cot, upper_w, gate_w):
     outer = nd // MEMBERS
     count, width = tokens.shape
+    nf_rows, mine = gate_w.shape[2] * gate_w.shape[3], gate_w.shape[4]
     lo, hi = jnp.bfloat16, jnp.float32
     dma = pltpu.SemaphoreType.DMA
     moves = [(nf,), (outer, nf), (nf,), (outer, nf), (4, max(3, count // length))]
     shapes = [
         (upper_w.shape, lo),
         ((outer, nf) + w_down.shape, lo),
-        ((MEMBERS, count, width), lo),
-        ((MEMBERS, count, width), lo),
+        ((MEMBERS * count, width), lo),
+        ((MEMBERS * count, width), lo),
+        ((MEMBERS * count, mine), hi),
+        ((MEMBERS * count, mine), hi),
+        ((MEMBERS * count, mine), lo),
+        ((mine, width), lo),
         ((count, (HQ + KV) * HD), hi),
         ((count, (HQ + KV) * HD), lo),
         ((count, KV * HD), lo),
         ((count, HQ * HD), lo),
         ((count, width), hi),
     ]
-    early = [(count, width), (count, width), (count, width)]
-    late = [in_w.shape, out_w.shape, w_down.shape, (count, width)]
+    early = [(count, width), (MEMBERS * count, width), (count, width)]
+    late = [in_w.shape, out_w.shape, w_down.shape, (MEMBERS * count, width)]
+    late += [gate_w.shape, gate_w.shape]
+    flat = (width, mine)
     return pl.pallas_call(
         functools.partial(attend_kernel, nd, nf, length),
         name="attend",
         out_shape=tuple(jax.ShapeDtypeStruct(*item) for item in shapes),
-        in_specs=[ON_CHIP] * 4 + [ANYWHERE] * 6,
-        out_specs=(ANYWHERE,) * 4 + (ON_CHIP,) * 5,
+        in_specs=[ON_CHIP] * 4 + [ANYWHERE] * 7,
+        out_specs=(ANYWHERE,) * 7 + (ON_CHIP,) * 6,
         input_output_aliases={9: 0},
         scratch_shapes=[pltpu.VMEM(shape, lo) for shape in early]
         + [pltpu.VMEM(w_down.shape, hi)]
         + [pltpu.VMEM(shape, lo) for shape in late]
+        + [pltpu.VMEM((nf_rows, mine), hi), pltpu.VMEM(flat, lo), pltpu.VMEM(flat, lo)]
+        + [pltpu.VMEM((MEMBERS * count, mine), kind) for kind in (hi, hi, lo)]
         + [dma(shape) for shape in moves for _ in range(2)]
-        + [dma((10,))],
+        + [dma((12,))],
         compiler_params=pltpu.CompilerParams(
             collective_id=2, has_side_effects=True, vmem_limit_bytes=VMEM_MOST
         ),
-    )(*small, tokens, w_down, in_w, out_w, cot, upper_w)
+    )(*small, tokens, w_down, in_w, out_w, cot, upper_w, gate_w)
 
 
 def backward_kernel(
@@ -1178,25 +1291,6 @@
 
     lax.fori_loop(0, HQ * HD // pair, mixed_back, 0)
 
-    def outer_product(left, right, target):
-        def step_once(index, carry):
-            columns = tile_of(index, pair)
-            turned = left[:, columns].T
-            for part in range(right.shape[1] // (2 * pair)):
-                across = pl.ds(part * 2 * pair, 2 * pair)
-                target[columns, across] = jnp.dot(
-                    turned, right[:, across], preferred_element_type=hi
-                ).astype(lo)
-            rest = right.shape[1] % (2 * pair)
-            if rest:
-                across = pl.ds(right.shape[1] - rest, rest)
-                target[columns, across] = jnp.dot(
-                    turned, right[:, across], preferred_element_type=hi
-                ).astype(lo)
-            return carry
-
-        lax.fori_loop(0, left.shape[1] // pair, step_once, 0)
-
     all_terms = (in_terms, out_terms)
     sizes = (in_terms.shape[0] // (nd), out_terms.shape[0] // (nd))
     core_terms = (in_core, out_core_terms)
@@ -1788,21 +1882,21 @@
         down_w,
         back_all,
         ffn_all,
+        gate,
+        upper,
+        hidden,
+        down_terms,
         raw,
         heads,
         values,
         mixed,
         hidden_in,
     ) = attend(
-        nd, nf, length, small, token_rows, w_down, in_w, out_w, back_in, upper_w
+        nd, nf, length, small, token_rows, w_down, in_w, out_w, back_in, upper_w, gate_w
     )
     gate_w = gate_w.reshape(D, mine)
     upper_w = upper_w.reshape(D, mine)
     down_w = down_w.reshape(mine, D)
-    back_all = back_all.reshape(MEMBERS * count, width)
-    ffn_all = ffn_all.reshape(MEMBERS * count, width)
-    back_halves = (back_all[: 2 * count], back_all[2 * count :])
-    ffn_halves = (ffn_all[: 2 * count], ffn_all[2 * count :])
     def inner_grads(back_half, gate, upper):
         grad_hidden = back_product(back_half, down_w)
         _, pull = jax.vjp(swiglu, gate, upper)
@@ -1811,28 +1905,24 @@
         back = back_product(grad_gate, gate_w) + back_product(grad_upper, upper_w)
         return grad_gate, grad_upper, low(back)
 
-    near_half, far_half = ffn_halves
-    gate, upper = forward_product(far_half, gate_w), forward_product(far_half, upper_w)
-    far_hidden = low(swiglu(gate, upper))
-    far_gate, far_upper, far_ffn = inner_grads(back_halves[1], gate, upper)
+    down_terms = down_terms.reshape(outer, nf, hidden_rows, width)
+    down_sent = [pick(down_terms, 0, ring_y.dest(hop)) for hop in range(1, outer)]
+    down_got = jnp.stack([ring_y.move(part, hop + 1) for hop, part in enumerate(down_sent)])
+    half = 2 * count
+    far_gate, far_upper, far_ffn = inner_grads(back_all[half:], gate[half:], upper[half:])
     far = far_ffn[:count].astype(jnp.float32) + ring_core.move(far_ffn[count:], 1)
     far = low(far)
     ffn_x = ring_x.move(far, 1)
-    gate = forward_product(after(near_half, far_ffn), gate_w)
-    upper = forward_product(after(near_half, far), upper_w)
-    near_hidden = low(swiglu(gate, upper))
-    down_terms = low(weight_product(jnp.concatenate([near_hidden, far_hidden], 0), back_all))
-    down_terms = down_terms.reshape(outer, nf, hidden_rows, width)
-    down_sent = [pick(down_terms, 0, ring_y.dest(hop)) for hop in range(1, outer)]
-    down_got = jnp.stack([ring_y.move(part, hop + 1) for hop, part in enumerate(down_sent)])
-    near_gate, near_upper, near_ffn = inner_grads(after(back_halves[0], *down_sent), gate, upper)
+    near_gate, near_upper, near_ffn = inner_grads(
+        after(back_all[:half], far), gate[:half], upper[:half]
+    )
     ffn_core = ring_core.move(near_ffn[count:], 1)
     ffn_all = after(ffn_all, near_ffn)
     gate_terms = low(weight_product(ffn_all, jnp.concatenate([near_gate, far_gate], 0)))
     upper_terms = low(weight_product(ffn_all, jnp.concatenate([near_upper, far_upper], 0)))
     near_out, far_out = [
-        low(forward_product(after(half, near_ffn, ffn_x, down_got), down_w))
-        for half in (near_hidden, far_hidden)
+        low(forward_product(after(rows, near_ffn), down_w))
+        for rows in (hidden[:half], hidden[half:])
     ]
     inner_shape = (outer, MEMBERS, nf, in_rows, mine)
     (

time: 290 us -> 270 us (0.931); the launches traced: 286 us -> 270 us
  matrix products: 35.4 us -> 28 us
  waiting for transfers between devices: 6.74 us -> 0.3 us
  local copies, waits for them, and re-layouts: 15.9 us -> 12.3 us
    dot_general x6 -> x2, matrix products: 14.9 us -> 5.26 us  [forward_product(): return jnp.dot(left, right, preferred_element_type=jnp.float32)]
    ppermute x4, waiting for transfers between devices: 6.74 us -> 0.3 us  [move(): return lax.ppermute(block, AXES, pairs)]
    dot_general x6, matrix products: 9.66 us -> 14.7 us  [back_product(): lax.dot_general(left, right, (((1,), (1,)), ((), ())), preferred_element_...]
    slice x1 -> x2, local copies, waits for them, and re-layouts: 5.21 us -> 1.81 us  [the longest x1 1.69 us: shards(): back_all[:half]]
    dot_general x3 -> x2, matrix products: 10.8 us -> 8.01 us  [weight_product(): lax.dot_general(left, right, (((0,), (0,)), ((), ())), preferred_element_...]
    unnamed x43 -> x39, local copies, waits for them, and re-layouts: 6.2 us -> 5.98 us
  transfers between devices with their start and end apart: 4 -> 4, of which waited for: 1 -> 1; matrix products, arithmetic and copies ran while one was open for 10% -> 8% of each run, Pallas kernels for 0% -> 0%
where the time goes in v5:
time: 270 us
  Pallas kernels  225 us (83%)
  matrix products  28 us (10%)
  local copies, waits for them, and re-layouts  12.3 us (5%)
    pallas_call x1, Pallas kernels, backward(): pl.pallas_call(functools.partial(backward_kernel, nd, nf, length), name='...  99.1 us
    pallas_call x1, Pallas kernels, attend(): pl.pallas_call(functools.partial(attend_kernel, nd, nf, length), name='at...  63 us
    pallas_call x1, Pallas kernels, gather_weights(): pl.pallas_call(functools.partial(weights_kernel, nd, nf), name='gather_we...  55.4 us
    dot_general x6, matrix products, back_product(): lax.dot_general(left, right, (((1,), (1,)), ((), ())), preferred_element_...  14.7 us
    dot_general x2, matrix products, weight_product(): lax.dot_general(left, right, (((0,), (0,)), ((), ())), preferred_element_...  8.01 us
    pallas_call x1, Pallas kernels, adam(): pl.pallas_call(functools.partial(adam_kernel, span), name='adam', out_sha...  7.53 us
    unnamed x39, local copies, waits for them, and re-layouts  5.98 us
  transfers between devices with their start and end apart: 4, of which 1 were waited for; matrix products, arithmetic and copies ran while one was open for 8% of the time, Pallas kernels for 0%

profile of v5, /device:TPU:0, one launch (start us, length us, event | category | flops | bytes accessed | tf_op | source)
XLA Modules:
  0.0 269.7 jit_solution(3452997400411539764)
XLA Ops:
  0.7 1.3 broadcast_in_dim.2.gains
  2.0 1.6 and_convert_fusion.mask
  3.6 55.4 %gather_weights.1 = (bf16[2,2,2,4,40,1536]{5,4,3,2,1,0:T(8,128)(2,1)}, bf16[2,2,2,4,32,1280]{5,4,3,2,1,0:T(8,128)(2,1)}, bf16[2,4,4,40,768]{4,3,2,1,0:T(8,128)(2,1)}, bf16[2,4,4,40,768]{4,3,2,1,0:T(8,128)(2,1)}) custom-call(f32[40,1024]{1,0:T(8,128)} %rest_4_.1, f32[40,256]{1,0:T(8,128)} %rest_5_.1, f32[40,256]{1,0:T(8,128)} %rest_6_.1, f32[32,1280]{1,0:T(8,128)} %rest_7_.1, ...), custom_call_target="tpu_custom_call" | custom-call | tf_op jit(solution)/shard_map/gather_weights/pallas_call | solution.py:408
  59.0 63.0 %attend.1 = (bf16[2,4,4,40,768]{4,3,2,1,0:T(8,128)(2,1)}, bf16[2,4,96,1280]{3,2,1,0:T(8,128)(2,1)}, bf16[1280,1280]{1,0:T(8,128)(2,1)}, bf16[1280,1280]{1,0:T(8,...) custom-call(f32[1,2688]{1,0:T(1,128)} %broadcast_in_dim.2.gains, ...), custom_call_target="tpu_custom_call", output_to_operand_aliasing={{0}: (9, {})} | custom-call | tf_op jit(solution)/shard_map/attend/pallas_call | solution.py:910
  122.0 5.3 %multiply_convert_fusion.1 = (bf16[640,768]{1,0:T(8,128)(2,1)S(1)}, bf16[640,768]{1,0:T(8,128)(2,1)S(1)}) fusion(f32[1280,768]{1,0:T(8,128)} %get-tuple-element.105, f32[1280,768]{1,0:T(8,128)} %get-tuple-element.104, bf16[768,1280]{1,0:T(8,128)(2,1)} %bitcast.60, bf16[1280,1280]{1,0:T(8,128)(2,1)} %get-tuple-element.102), kind=kOutput, calls=%fused_computation.24 | convolution fusion | flops 1265172480 | bytes 9502720 | tf_op jit(solution)/shard_map/dot_general | solution.py:66
  127.3 1.5 fusion.20
  128.8 0.7 copy-done.3
  129.6 1.5 fusion
  131.1 1.1 copy-done.6
  132.2 0.9 slice.53
  133.3 1.7 slice.40
  135.0 0.2 copy-done.5
  135.4 0.3 collective-permute-done
  135.7 1.0 copy-done.7
  136.7 0.2 add_convert_fusion
  136.9 0.8 collective-permute-start.3
  137.7 0.3 copy-done.12
  138.0 3.6 %multiply_convert_fusion = (bf16[640,768]{1,0:T(8,128)(2,1)S(1)}, bf16[640,768]{1,0:T(8,128)(2,1)S(1)}) fusion(f32[1280,768]{1,0:T(8,128)S(1)} %copy-done.12, f32[1280,768]{1,0:T(8,128)} %get-tuple-element.104, bf16[640,1280]{1,0:T(8,128)(2,1)S(1)} %slice.40, bf16[768,1280]{1,0:T(8,128)(2,1)S(1)} %bitcast.61), kind=kOutput, calls=%fused_computation.22 | convolution fusion | flops 1265172480 | bytes 9502720 | tf_op jit(solution)/shard_map/dot_general | solution.py:66
  141.6 1.5 fusion.21
  143.2 1.5 fusion.1
  144.7 1.0 fusion.19
  145.7 2.6 convolution_convert_fusion.3.out_near.rest_1_
  148.3 4.0 %convolution_convert_fusion.1 = bf16[1280,768]{1,0:T(8,128)(2,1)} fusion(bf16[1280,1280]{1,0:T(8,128)(2,1)S(1)} %copy-done.13, bf16[640,768]{1,0:T(8,128)(2,1)S(1)} %copy-done.18, bf16[640,768]{1,0:T(8,128)(2,1)S(1)} %get-tuple-element.161), kind=kOutput, calls=%fused_computation.3 | convolution fusion | flops 2521497600 | bytes 7208960 | tf_op jit(solution)/shard_map/dot_general | solution.py:60
  152.3 0.5 collective-permute-start.2
  152.8 2.7 convolution_convert_fusion.2.out_far
  155.5 4.0 %convolution_convert_fusion = bf16[1280,768]{1,0:T(8,128)(2,1)} fusion(bf16[1280,1280]{1,0:T(8,128)(2,1)S(1)} %copy-done.13, bf16[640,768]{1,0:T(8,128)(2,1)S(1)} %copy-done.16, bf16[640,768]{1,0:T(8,128)(2,1)S(1)} %get-tuple-element.160), kind=kOutput, calls=%fused_computation.2 | convolution fusion | flops 2521497600 | bytes 7208960 | tf_op jit(solution)/shard_map/dot_general | solution.py:60
  159.5 1.0 copy-done.8
  160.7 0.3 copy-done.10
  161.0 99.1 %backward.1 = (bf16[320,1280]{1,0:T(8,128)(2,1)}, bf16[320,1280]{1,0:T(8,128)(2,1)}, bf16[4,40,768]{2,1,0:T(8,128)(2,1)}, bf16[4,40,768]{2,1,0:T(8,128)(2,1)}, b...) custom-call(f32[1,2688]{1,0:T(1,128)} %broadcast_in_dim.2.gains, ...), custom_call_target="tpu_custom_call" | custom-call | tf_op jit(solution)/shard_map/backward/pallas_call | solution.py:1612
  260.1 1.2 slice.51
  261.3 7.5 %adam.1 = (f32[40,1024]{1,0:T(8,128)}, f32[40,256]{1,0:T(8,128)}, f32[40,256]{1,0:T(8,128)}, f32[32,1280]{1,0:T(8,128)}, f32[40,3072]{1,0:T(8,128)}, /*index=5*/...) custom-call(f32[8,128]{1,0:T(8,128)} %get-tuple-element.118.norm, ...), custom_call_target="tpu_custom_call" | custom-call | tf_op jit(solution)/shard_map/adam/pallas_call | solution.py:1771
  268.8 0.9 copy.66
  (39 shorter events, 0.6 us)
Async XLA Ops:
  122.0 5.3 %copy-start.1 = (bf16[2,4,4,40,768]{4,3,2,1,0:T(8,128)(2,1)S(1)}, bf16[2,4,4,40,768]{4,3,2,1,0:T(8,128)(2,1)}, u32[]{:S(2)}) copy-start(bf16[2,4,4,40,768]{4,3,2,1,0:T(8,128)(2,1)} %get-tuple-element.100.gate_w) | copy-start | bytes 5898244
  127.3 1.5 copy-start.17
  127.3 1.5 copy-start.15
  127.3 2.2 copy-start.3
  129.6 3.6 %copy-start = (bf16[768,1280]{1,0:T(8,128)(2,1)S(1)}, bf16[768,1280]{1,0:T(8,128)(2,1)}, u32[]{:S(2)}) copy-start(bf16[768,1280]{1,0:T(8,128)(2,1)} %get-tuple-element.110) | copy-start | bytes 5898244
  131.0 1.2 copy-start.6
  133.1 2.5 collective-permute-start
  133.2 2.0 copy-start.5
  133.2 26.2 %collective-permute-start.1 = (bf16[4,96,1280]{2,1,0:T(8,128)(2,1)S(1)}, bf16[4,96,1280]{2,1,0:T(8,128)(2,1)S(1)}, u32[]{:S(2)}, u32[]{:S(2)}) collective-permute-start(bf16[4,96,1280]{2,1,0:T(8,128)(2,1)S(1)} %dynamic-slice_bitcast_fusion), channel_id=1, source_target_pairs={{0,16},{1,17},{2,18},{3,19},{4,20},{5,21},{6,22},{7,23},{8,24},{9,... | collective-permute-start | bytes 2949128 | tf_op jit(solution)/shard_map/ppermute | solution.py:102
  133.3 4.4 %copy-start.14 = (bf16[2,4,96,1280]{3,2,1,0:T(8,128)(2,1)S(1)}, bf16[2,4,96,1280]{3,2,1,0:T(8,128)(2,1)}, u32[]{:S(2)}) copy-start(bf16[2,4,96,1280]{3,2,1,0:T(8,128)(2,1)} %get-tuple-element.103) | copy-start | bytes 5898244
  135.3 1.4 copy-start.7
  135.3 2.8 %copy-start.12 = (f32[1280,768]{1,0:T(8,128)S(1)}, f32[1280,768]{1,0:T(8,128)}, u32[]{:S(2)}) copy-start(f32[1280,768]{1,0:T(8,128)} %get-tuple-element.105) | copy-start | bytes 11796484
  136.9 4.7 %copy-start.2 = (bf16[2,4,4,40,768]{4,3,2,1,0:T(8,128)(2,1)S(1)}, bf16[2,4,4,40,768]{4,3,2,1,0:T(8,128)(2,1)}, u32[]{:S(2)}) copy-start(bf16[2,4,4,40,768]{4,3,2,1,0:T(8,128)(2,1)} %get-tuple-element.100.gate_w) | copy-start | bytes 5898244
  136.9 22.6 %collective-permute-start.3 = (bf16[320,1280]{1,0:T(8,128)(2,1)S(1)}, bf16[320,1280]{1,0:T(8,128)(2,1)S(1)}, u32[]{:S(2)}, u32[]{:S(2)}) collective-permute-start(bf16[320,1280]{1,0:T(8,128)(2,1)S(1)} %add_convert_fusion), channel_id=1, source_target_pairs={{0,8},{1,9},{2,10},{3,11},{4,12},{5,13},{6,14},{7,15},{8,0},{9,1},... | collective-permute-start | bytes 2457608 | tf_op jit(solution)/shard_map/ppermute | solution.py:102
  141.6 1.5 copy-start.4
  145.7 2.6 copy-start.13
  145.7 2.6 copy-start.18
  152.3 3.2 %copy-start.16 = (bf16[640,768]{1,0:T(8,128)(2,1)S(1)}, bf16[640,768]{1,0:T(8,128)(2,1)}, u32[]{:S(2)}) copy-start(bf16[640,768]{1,0:T(8,128)(2,1)} %copy-done.15) | copy-start | bytes 2949124
  152.3 7.2 %collective-permute-start.2 = (bf16[320,1280]{1,0:T(8,128)(2,1)S(1)}, bf16[320,1280]{1,0:T(8,128)(2,1)S(1)}, u32[]{:S(2)}, u32[]{:S(2)}) collective-permute-start(bf16[320,1280]{1,0:T(8,128)(2,1)S(1)} %get-tuple-element.166), channel_id=1, source_target_pairs={{0,4},{1,5},{2,6},{3,7},{4,0},{5,1},{6,2},{7,3},{8,12},{9,13},{10,... | collective-permute-start | bytes 2457608 | tf_op jit(solution)/shard_map/ppermute | solution.py:102
  159.5 1.0 copy-start.8
  159.5 1.2 copy-start.11
  159.5 1.5 copy-start.10
  261.3 7.5 %copy-start.9 = (bf16[320,1280]{1,0:T(8,128)(2,1)S(1)}, bf16[320,1280]{1,0:T(8,128)(2,1)}, u32[]{:S(2)}) copy-start(bf16[320,1280]{1,0:T(8,128)(2,1)} %get-tuple-element.128) | copy-start | bytes 2457604

commit v6 on v5

--- a/solution.py
+++ b/solution.py
@@ -459,16 +459,29 @@
 
 
 def split_gains(gains):
-    width = (gains.shape[1] - 2 * HD) // 2
-    heads = gains[:, pl.ds(2 * width, 2 * HD)]
-    other = pltpu.roll(heads, HD, 1)
+    rows = (gains.shape[0] - 1) // 2
+
+    def joined(first):
+        return jnp.concatenate([gains[first + row : first + row + 1, :] for row in range(rows)], 1)
+
+    heads = gains[2 * rows : 2 * rows + 1, :]
+    other = pltpu.roll(jnp.broadcast_to(heads, (8, LANES)), HD, 1)[:1]
     first = lax.broadcasted_iota(jnp.int32, heads.shape, 1) < HD
     query, key = jnp.where(first, heads, other), jnp.where(first, other, heads)
 
     def of_tile(index):
         return jnp.where(index < HQ * HD // LANES, query, key)
 
-    return gains[:, pl.ds(0, width)], gains[:, pl.ds(width, width)], of_tile
+    return joined(0), joined(rows), of_tile
+
+
+def may_attend(ids, row):
+    length = ids.shape[1]
+    across = ids[row : row + 1, :].astype(jnp.float32)
+    place = lax.broadcasted_iota(jnp.int32, (length, length), 0)
+    other = lax.broadcasted_iota(jnp.int32, (length, length), 1)
+    down = jnp.sum(jnp.where(place == other, across, 0.0), 1, keepdims=True)
+    return (other <= place) & (down == across)
 
 
 def tile_of(index, width=LANES):
@@ -529,7 +542,7 @@
     gains,
     cosine,
     sine,
-    mask,
+    segments,
     tokens_full,
     down_full,
     in_full,
@@ -541,9 +554,12 @@
     down_w,
     back_all,
     ffn_all,
-    gate_out,
-    upper_out,
-    hidden_out,
+    gate_near,
+    upper_near,
+    hidden_near,
+    gate_far,
+    upper_far,
+    hidden_far,
     down_terms,
     raw,
     heads,
@@ -738,7 +754,7 @@
 
     def attend(row):
         rows = pl.ds(row * length, length)
-        allowed = mask[row] > 0.5
+        allowed = may_attend(segments, row)
 
         def pair(tile, carry):
             key_tile = heads[rows, tile_of(HQ * HD // LANES + tile)]
@@ -866,12 +882,17 @@
         copy.wait_recv()
     kept.append(keep(2, ffn_here, ffn_all))
     ffn_rows(3)
-    kept.append(keep(3, gate_here, gate_out))
-    kept.append(keep(9, upper_here, upper_out))
-    kept.append(keep(10, hidden_here, hidden_out))
+    halves = (
+        (gate_near, upper_near, hidden_near),
+        (gate_far, upper_far, hidden_far),
+    )
+    for far, targets in enumerate(halves):
+        rows = pl.ds(far * 2 * count, 2 * count)
+        for index, source in enumerate((gate_here, upper_here, hidden_here)):
+            kept.append(keep(9 + 3 * far + index, source.at[rows], targets[index]))
     cot_near.wait_recv()
     cot_cross.wait_recv()
-    kept.append(keep(11, cot, back_all))
+    kept.append(keep(3, cot, back_all))
     outer_product(hidden_here, cot, down_terms)
     for copy in arrivals:
         copy.wait_recv()
@@ -893,9 +914,7 @@
         ((outer, nf) + w_down.shape, lo),
         ((MEMBERS * count, width), lo),
         ((MEMBERS * count, width), lo),
-        ((MEMBERS * count, mine), hi),
-        ((MEMBERS * count, mine), hi),
-        ((MEMBERS * count, mine), lo),
+        *[((2 * count, mine), kind) for kind in (hi, hi, lo)] * 2,
         ((mine, width), lo),
         ((count, (HQ + KV) * HD), hi),
         ((count, (HQ + KV) * HD), lo),
@@ -912,7 +931,7 @@
         name="attend",
         out_shape=tuple(jax.ShapeDtypeStruct(*item) for item in shapes),
         in_specs=[ON_CHIP] * 4 + [ANYWHERE] * 7,
-        out_specs=(ANYWHERE,) * 7 + (ON_CHIP,) * 6,
+        out_specs=(ANYWHERE,) * 10 + (ON_CHIP,) * 6,
         input_output_aliases={9: 0},
         scratch_shapes=[pltpu.VMEM(shape, lo) for shape in early]
         + [pltpu.VMEM(w_down.shape, hi)]
@@ -920,7 +939,7 @@
         + [pltpu.VMEM((nf_rows, mine), hi), pltpu.VMEM(flat, lo), pltpu.VMEM(flat, lo)]
         + [pltpu.VMEM((MEMBERS * count, mine), kind) for kind in (hi, hi, lo)]
         + [dma(shape) for shape in moves for _ in range(2)]
-        + [dma((12,))],
+        + [dma((15,))],
         compiler_params=pltpu.CompilerParams(
             collective_id=2, has_side_effects=True, vmem_limit_bytes=VMEM_MOST
         ),
@@ -934,13 +953,14 @@
     gains,
     cosine,
     sine,
-    mask,
-    out_near,
-    out_far,
+    segments,
+    hidden_near,
+    hidden_far,
     down_got,
     down_terms,
     gate_terms,
     upper_terms,
+    tokens_full,
     mine_full,
     near_full,
     far_full,
@@ -950,9 +970,10 @@
     mixed_full,
     heads_full,
     values_full,
-    tokens_full,
     raw_full,
     in_w_full,
+    down_full,
+    out_mine,
     out_core,
     out_x,
     gate_parts,
@@ -974,6 +995,7 @@
     square_group,
     square_got,
     square_far,
+    tokens,
     mine_ref,
     core_near,
     from_x,
@@ -983,10 +1005,13 @@
     mixed,
     heads,
     values,
-    tokens,
     raw,
     in_w,
-    out_pass,
+    down_w,
+    near_here,
+    far_here,
+    out_near,
+    out_far,
     out_core_far,
     normed,
     branch,
@@ -1077,10 +1102,11 @@
         return (y_to(hop) * MEMBERS + member, z_to(step))
 
     peers += [cross_peer(hop, step) for hop, step in crossed if hop and step]
-    fulls = (mine_full, near_full, far_full, hidden_full, cot_full, out_w_full, mixed_full)
-    fulls += (heads_full, values_full, tokens_full, raw_full, in_w_full)
-    places = (mine_ref, core_near, from_x, hidden_in, cot, out_w, mixed)
-    places += (heads, values, tokens, raw, in_w)
+    fulls = (tokens_full, mine_full, near_full, far_full, hidden_full, cot_full, out_w_full, mixed_full)
+    fulls += (heads_full, values_full, raw_full, in_w_full)
+    fulls += (down_full, hidden_near, hidden_far)
+    places = (tokens, mine_ref, core_near, from_x, hidden_in, cot, out_w, mixed)
+    places += (heads, values, raw, in_w, down_w, near_here, far_here)
     operands = [
         pltpu.make_async_copy(source, target, operand_sem.at[index])
         for index, (source, target) in enumerate(zip(fulls, places))
@@ -1117,10 +1143,6 @@
     gain_attn, gain_ffn, gain_heads = split_gains(gains)
     count, width = tokens.shape
     here, there = pl.ds(0, count), pl.ds(count, count)
-
-    out_far_copy = remote(out_far.at[there], out_core_far, row_send.at[0], row_recv.at[0], core_peer)
-    out_pass_copy = keep(local_sem.at[0], out_far.at[here], out_pass)
-    out_near_copy = remote(out_near.at[there], out_core, row_send.at[1], row_recv.at[1], core_peer)
 
     terms = (down_terms, gate_terms, upper_terms)
     owns = (down_own, gate_own, upper_own)
@@ -1240,8 +1262,7 @@
             copy.wait_recv()
         return jnp.sum(got[...], 0)
 
-    pieces(nf)
-
+    ready(1)
     def add_rows(target, other):
         def step_once(index, carry):
             rows = rows_of(index, chunk)
@@ -1257,9 +1278,11 @@
         normed[rows, :] = (part * scale * gain_attn).astype(lo)
         return carry
 
+    lax.fori_loop(0, count // chunk, norm_rows, 0)
     sum_attn[...] = jnp.zeros_like(sum_attn)
     sum_ffn[...] = jnp.zeros_like(sum_ffn)
     sum_heads[...] = jnp.zeros_like(sum_heads)
+    pieces(nf)
     ready(5)
 
     def norm_back(part, gain, grad):
@@ -1411,7 +1434,7 @@
 
     def attend_back(row):
         rows = pl.ds(row * length, length)
-        allowed = mask[row] > 0.5
+        allowed = may_attend(segments, row)
 
         def pair_back(tile, carry):
             key_tile = heads[rows, tile_of(query_tiles + tile)]
@@ -1475,7 +1498,6 @@
         return carry
 
     lax.fori_loop(0, head_tiles, turn_back, 0)
-    lax.fori_loop(0, count // chunk, norm_rows, 0)
     outer_product(normed, grad_raw, in_terms)
     core_out(0)
     pieces(1)
@@ -1487,10 +1509,25 @@
         return carry
 
     core_in(0)
+
+    def down_product(left, target):
+        def step_once(index, carry):
+            columns = tile_of(index, pair)
+            target[:, columns] = jnp.dot(
+                left[...], down_w[:, columns], preferred_element_type=hi
+            ).astype(lo)
+            return carry
+
+        lax.fori_loop(0, width // pair, step_once, 0)
+
+    down_product(far_here, out_far)
+    out_far_copy = remote(out_far.at[there], out_core_far, row_send.at[0], row_recv.at[0], core_peer)
+    down_product(near_here, out_near)
+    out_near_copy = remote(out_near.at[there], out_core, row_send.at[1], row_recv.at[1], core_peer)
+    mine_copy = keep(local_sem.at[0], out_near.at[here], out_mine)
     out_far_copy.wait_recv()
-    out_pass_copy.wait()
-    add_rows(out_pass, out_core_far)
-    out_x_copy = remote(out_pass, out_x, row_send.at[2], row_recv.at[2], x_peer)
+    add_rows(out_far, out_core_far)
+    out_x_copy = remote(out_far.at[here], out_x, row_send.at[2], row_recv.at[2], x_peer)
     lax.fori_loop(0, width // pair, normed_back, 0)
 
     def attn_norm_back(index, carry):
@@ -1540,14 +1577,14 @@
         copy.wait_recv()
     for copy in sent:
         copy.wait_send()
-    for copy in swaps_local:
+    for copy in swaps_local + [mine_copy]:
         copy.wait()
 
 
 def backward(nd, nf, length, small, halves, terms, operands):
     outer = nd // MEMBERS
     count, width = operands[0].shape
-    out_w, in_w = operands[5], operands[-1]
+    out_w, in_w = operands[6], operands[-2]
     _, down_terms, gate_terms, _ = terms
     lo, hi = jnp.bfloat16, jnp.float32
     dma = pltpu.SemaphoreType.DMA
@@ -1559,6 +1596,7 @@
     gain_tile = (-(-tiles // 8) * 8, LANES)
     far = outer * nf - 1
     shapes = [
+        ((count, width), lo),
         ((count, width), lo),
         ((count, width), lo),
         (inner, lo),
@@ -1575,7 +1613,8 @@
     for tile in (gain_tile, (8, LANES)):
         scratch += [(tile, hi), (tile, hi), ((MEMBERS,) + tile, hi), ((outer * nf,) + tile, hi)]
     scratch += [(operand.shape, operand.dtype) for operand in operands]
-    scratch += [((count, width), lo)] * 2
+    scratch += [(array.shape, lo) for array in halves]
+    scratch += [((2 * count, width), lo)] * 2 + [((count, width), lo)]
     scratch += [
         ((count, width), lo),
         ((count, width), lo),
@@ -1614,10 +1653,10 @@
         name="backward",
         out_shape=tuple(jax.ShapeDtypeStruct(*item) for item in shapes),
         in_specs=[ON_CHIP] * 4 + [ANYWHERE] * (6 + len(operands)),
-        out_specs=(ANYWHERE,) * 4 + (ON_CHIP,) * 6,
+        out_specs=(ANYWHERE,) * 5 + (ON_CHIP,) * 6,
         scratch_shapes=[pltpu.VMEM(*item) for item in scratch]
         + [dma(shape) for shape in moves for _ in range(2)]
-        + [dma((3, nf)), dma((outer, nf)), dma((len(operands),)), dma((5,))],
+        + [dma((3, nf)), dma((outer, nf)), dma((len(operands) + 2,)), dma((5,))],
         compiler_params=pltpu.CompilerParams(
             collective_id=3, has_side_effects=True, vmem_limit_bytes=VMEM_MOST
         ),
@@ -1628,20 +1667,21 @@
     span, norm, gain_totals, in_sum, out_sum, gate_parts, upper_parts, down_sum, *rest
 ):
     count = 8
-    row_terms, rest = rest[:4], rest[4:]
+    row_terms, rest = rest[:5], rest[5:]
     masters, firsts, seconds = rest[:count], rest[count : 2 * count], rest[2 * count : 3 * count]
     rest = rest[3 * count :]
     outs = [rest[index * count : (index + 1) * count] for index in range(3)]
     copies = rest[3 * count : 4 * count - 1]
-    output = rest[4 * count - 1]
-    rest = rest[4 * count :]
+    output, rows_out, norm_out = rest[4 * count - 1 : 4 * count + 2]
+    rest = rest[4 * count + 2 :]
+    norm_out[...] = norm[0:1, 0:1]
     ins_here = [rest[index * count : (index + 1) * count] for index in range(3)]
     rest = rest[3 * count :]
     outs_here = [rest[index * count : (index + 1) * count] for index in range(3)]
     copies_here = rest[3 * count : 4 * count - 1]
     sums_here = rest[4 * count - 1 : 4 * count + 4]
-    terms_here = rest[4 * count + 4 : 4 * count + 8]
-    output_here, sum_sem, in_sem, out_sem, term_sem = rest[4 * count + 8 :]
+    terms_here = rest[4 * count + 4 : 4 * count + 9]
+    output_here, sum_sem, in_sem, out_sem, term_sem = rest[4 * count + 9 :]
     sums = (in_sum, out_sum, gate_parts, upper_parts, down_sum)
     loads = {}
     for index in (6, 4, 5, 3, 0, 1, 2, 7):
@@ -1745,11 +1785,14 @@
     def add_rows(index, carry):
         rows = rows_of(index, 32)
         total = terms_here[0][rows, :]
-        for term in terms_here[1:]:
+        for term in terms_here[1:4]:
             total = total + term[rows, :].astype(jnp.float32)
         output_here[rows, :] = total.astype(jnp.bfloat16)
         return carry
 
+    copy = pltpu.make_async_copy(terms_here[4], rows_out, term_sem.at[4])
+    copy.start()
+    stores.append(copy)
     lax.fori_loop(0, rows_count // 32, add_rows, 0)
     copy = pltpu.make_async_copy(output_here, output, term_sem.at[0])
     copy.start()
@@ -1767,15 +1810,15 @@
     inputs = [(array.shape, hi) for _ in range(3) for array in masters]
     scratch = inputs + shapes + [(array.shape, array.dtype) for array in sums]
     scratch += [(rows_shape, array.dtype) for array in row_terms] + [(rows_shape, lo)]
-    shapes += [(rows_shape, lo)]
+    shapes += [(rows_shape, lo), (rows_shape, lo), ((1, 1), hi)]
     return pl.pallas_call(
         functools.partial(adam_kernel, span),
         name="adam",
         out_shape=tuple(jax.ShapeDtypeStruct(*item) for item in shapes),
-        in_specs=[ON_CHIP] * 2 + [ANYWHERE] * (9 + len(inputs)),
-        out_specs=(ANYWHERE,) * len(shapes),
+        in_specs=[ON_CHIP] * 2 + [ANYWHERE] * (10 + len(inputs)),
+        out_specs=(ANYWHERE,) * (len(shapes) - 1) + (ON_CHIP,),
         scratch_shapes=[pltpu.VMEM(*item) for item in scratch]
-        + [dma((5,)), dma((3, len(masters))), dma((4, len(masters))), dma((4,))],
+        + [dma((5,)), dma((3, len(masters))), dma((4, len(masters))), dma((5,))],
         compiler_params=pltpu.CompilerParams(vmem_limit_bytes=VMEM_MOST),
     )(norm, gain_totals, *sums, *row_terms, *masters, *firsts, *seconds)
 
@@ -1871,10 +1914,8 @@
     in_w = in_w.reshape(D, attn_cols)
     out_w = out_w.reshape(HQ * HD, D)
 
-    positions = jnp.arange(length)
-    causal = positions[None, :] <= positions[:, None]
-    allowed = causal[None] & (segment_ids[:, :, None] == segment_ids[:, None, :])
-    small = (gains[None], *rotary_tables(length), allowed.astype(jnp.float32))
+    tiled = [array.reshape(-1, LANES) for array in (gains, gain_first, gain_second)]
+    small = (tiled[0], *rotary_tables(length), segment_ids)
     back_in = cotangent.reshape(count, width)
     token_rows = tokens.reshape(count, width)
     (
@@ -1882,9 +1923,12 @@
         down_w,
         back_all,
         ffn_all,
-        gate,
-        upper,
-        hidden,
+        gate_near,
+        upper_near,
+        hidden_near,
+        gate_far,
+        upper_far,
+        hidden_far,
         down_terms,
         raw,
         heads,
@@ -1909,23 +1953,20 @@
     down_sent = [pick(down_terms, 0, ring_y.dest(hop)) for hop in range(1, outer)]
     down_got = jnp.stack([ring_y.move(part, hop + 1) for hop, part in enumerate(down_sent)])
     half = 2 * count
-    far_gate, far_upper, far_ffn = inner_grads(back_all[half:], gate[half:], upper[half:])
+    far_gate, far_upper, far_ffn = inner_grads(back_all[half:], gate_far, upper_far)
     far = far_ffn[:count].astype(jnp.float32) + ring_core.move(far_ffn[count:], 1)
     far = low(far)
     ffn_x = ring_x.move(far, 1)
     near_gate, near_upper, near_ffn = inner_grads(
-        after(back_all[:half], far), gate[:half], upper[:half]
+        after(back_all[:half], far), gate_near, upper_near
     )
     ffn_core = ring_core.move(near_ffn[count:], 1)
     ffn_all = after(ffn_all, near_ffn)
     gate_terms = low(weight_product(ffn_all, jnp.concatenate([near_gate, far_gate], 0)))
     upper_terms = low(weight_product(ffn_all, jnp.concatenate([near_upper, far_upper], 0)))
-    near_out, far_out = [
-        low(forward_product(after(rows, near_ffn), down_w))
-        for rows in (hidden[:half], hidden[half:])
-    ]
     inner_shape = (outer, MEMBERS, nf, in_rows, mine)
     (
+        out_mine,
         out_core,
         out_x,
         gate_parts,
@@ -1941,7 +1982,7 @@
         nf,
         length,
         small,
-        (near_out, far_out),
+        (hidden_near, hidden_far),
         (
             down_got,
             down_terms,
@@ -1949,6 +1990,7 @@
             upper_terms.reshape(inner_shape),
         ),
         (
+            token_rows,
             near_ffn[:count],
             ffn_core,
             ffn_x,
@@ -1958,26 +2000,25 @@
             mixed,
             heads,
             values,
-            token_rows,
             raw,
             in_w,
+            down_w,
         ),
     )
-    tiled = [array.reshape(-1, LANES) for array in (gains, gain_first, gain_second)]
     results = adam(
         span,
         norm,
         gain_totals,
         (in_sum, out_sum, gate_parts, upper_parts, down_sum),
-        (hidden_in, near_out, out_core, out_x),
+        (hidden_in, out_mine, out_core, out_x, input_grad),
         masters + (tiled[0],),
         firsts + (tiled[1],),
         seconds + (tiled[2],),
     )
     clipped, new_masters, new_seconds = results[:7], results[8:15], results[16:23]
     gain_clipped, new_gains, gain_seconds = (results[k].reshape(-1) for k in (7, 15, 23))
-    copies, output = tuple(results[24:31]), results[31]
-    total_norm = norm[0, 0]
+    copies, output, input_grad = tuple(results[24:31]), results[31], results[32]
+    total_norm = results[33].reshape(())
     return (
         (output.reshape(tokens.shape), input_grad.reshape(tokens.shape))
         + clipped

time: 270 us -> 264 us (0.978)
  matrix products: 28 us -> 21.2 us
  waiting for transfers between devices: 0.3 us -> 5.65 us
  local copies, waits for them, and re-layouts: 12.3 us -> 8.33 us
    ppermute x4, waiting for transfers between devices: 0.3 us -> 5.65 us  [move(): return lax.ppermute(block, AXES, pairs)]
    dot_general x2 -> x0, matrix products: 5.26 us -> none  [forward_product(): return jnp.dot(left, right, preferred_element_type=jnp.float32)]
    unnamed x39 -> x36, local copies, waits for them, and re-layouts: 5.98 us -> 4.6 us
  transfers between devices with their start and end apart: 4 -> 4, of which waited for: 1 -> 2; matrix products, arithmetic and copies ran while one was open for 8% -> 6% of each run, Pallas kernels for 0% -> 0%
where the time goes in v6:
time: 264 us
  Pallas kernels  226 us (86%)
  matrix products  21.2 us (8%)
  local copies, waits for them, and re-layouts  8.33 us (3%)
  waiting for transfers between devices  5.65 us (2%)
    pallas_call x1, Pallas kernels, backward(): pl.pallas_call(functools.partial(backward_kernel, nd, nf, length), name='...  98.6 us
    pallas_call x1, Pallas kernels, attend(): pl.pallas_call(functools.partial(attend_kernel, nd, nf, length), name='at...  63 us
    pallas_call x1, Pallas kernels, gather_weights(): pl.pallas_call(functools.partial(weights_kernel, nd, nf), name='gather_we...  55.4 us
    dot_general x6, matrix products, back_product(): lax.dot_general(left, right, (((1,), (1,)), ((), ())), preferred_element_...  13.2 us
    pallas_call x1, Pallas kernels, adam(): pl.pallas_call(functools.partial(adam_kernel, span), name='adam', out_sha...  8.6 us
    dot_general x2, matrix products, weight_product(): lax.dot_general(left, right, (((0,), (0,)), ((), ())), preferred_element_...  8.01 us
    ppermute x4, waiting for transfers between devices, move(): return lax.ppermute(block, AXES, pairs)  5.65 us
  transfers between devices with their start and end apart: 4, of which 2 were waited for; matrix products, arithmetic and copies ran while one was open for 6% of the time, Pallas kernels for 0%

profile of v6, /device:TPU:0, one launch (start us, length us, event | category | flops | bytes accessed | tf_op | source)
XLA Modules:
  0.0 263.6 jit_solution(18304333756535791982)
XLA Ops:
  0.7 55.4 %gather_weights.1 = (bf16[2,2,2,4,40,1536]{5,4,3,2,1,0:T(8,128)(2,1)}, bf16[2,2,2,4,32,1280]{5,4,3,2,1,0:T(8,128)(2,1)}, bf16[2,4,4,40,768]{4,3,2,1,0:T(8,128)(2,1)}, bf16[2,4,4,40,768]{4,3,2,1,0:T(8,128)(2,1)}) custom-call(f32[40,1024]{1,0:T(8,128)} %rest_5_.1, f32[40,256]{1,0:T(8,128)} %rest_6_.1, f32[40,256]{1,0:T(8,128)} %rest_7_.1, f32[32,1280]{1,0:T(8,128)} %rest_8_.1, ...), custom_call_target="tpu_custom_call" | custom-call | tf_op jit(solution)/shard_map/gather_weights/pallas_call | solution.py:408
  56.1 63.0 %attend.1 = (bf16[2,4,4,40,768]{4,3,2,1,0:T(8,128)(2,1)}, bf16[2,4,96,1280]{3,2,1,0:T(8,128)(2,1)}, bf16[1280,1280]{1,0:T(8,128)(2,1)}, bf16[1280,1280]{1,0:T(8,...) custom-call(f32[21,128]{1,0:T(8,128)} %bitcast.55, ...), custom_call_target="tpu_custom_call", output_to_operand_aliasing={{0}: (9, {})} | custom-call | tf_op jit(solution)/shard_map/attend/pallas_call | solution.py:929
  119.1 5.3 %multiply_convert_fusion.1 = (bf16[640,768]{1,0:T(8,128)(2,1)S(1)}, bf16[640,768]{1,0:T(8,128)(2,1)S(1)}) fusion(f32[640,768]{1,0:T(8,128)} %get-tuple-element.112, f32[640,768]{1,0:T(8,128)} %get-tuple-element.111, bf16[768,1280]{1,0:T(8,128)(2,1)} %bitcast.49, bf16[1280,1280]{1,0:T(8,128)(2,1)} %get-tuple-element.109), kind=kOutput, calls=%fused_computation.22 | convolution fusion | flops 1265172480 | bytes 9502720 | tf_op jit(solution)/shard_map/dot_general | solution.py:66
  124.4 1.5 fusion.19
  125.9 0.7 copy-done.3
  126.7 1.5 fusion
  128.2 1.2 copy-done.6
  129.4 0.9 slice.25
  130.3 0.0 collective-permute-start.1
  130.3 0.1 dynamic-slice_bitcast_fusion
  130.4 0.1 collective-permute-start
  130.5 1.7 slice.18
  132.2 0.6 collective-permute-done.1
  132.9 0.2 add_convert_fusion
  133.1 0.8 collective-permute-start.3
  133.9 0.3 copy-done.5
  134.3 2.1 multiply_convert_fusion
  136.4 1.5 fusion.20
  137.8 0.1 copy-done.4
  137.9 1.5 fusion.1
  139.4 1.0 fusion.18
  140.4 0.5 collective-permute-start.2
  140.9 0.7 copy-done.11
  141.6 4.0 %convolution_convert_fusion = bf16[1280,768]{1,0:T(8,128)(2,1)} fusion(bf16[1280,1280]{1,0:T(8,128)(2,1)S(1)} %copy-done.11, bf16[640,768]{1,0:T(8,128)(2,1)S(1)} %copy-done.15, bf16[640,768]{1,0:T(8,128)(2,1)S(1)} %get-tuple-element.168), kind=kOutput, calls=%fused_computation.2 | convolution fusion | flops 2521497600 | bytes 7208960 | tf_op jit(solution)/shard_map/dot_general | solution.py:60
  145.6 4.0 %convolution_convert_fusion.1 = bf16[1280,768]{1,0:T(8,128)(2,1)} fusion(bf16[1280,1280]{1,0:T(8,128)(2,1)S(1)} %copy-done.11, bf16[640,768]{1,0:T(8,128)(2,1)S(1)} %copy-done.17, bf16[640,768]{1,0:T(8,128)(2,1)S(1)} %get-tuple-element.169), kind=kOutput, calls=%fused_computation.3 | convolution fusion | flops 2521497600 | bytes 7208960 | tf_op jit(solution)/shard_map/dot_general | solution.py:60
  149.6 5.0 %collective-permute-done = bf16[4,96,1280]{2,1,0:T(8,128)(2,1)S(1)} collective-permute-done((bf16[4,96,1280]{2,1,0:T(8,128)(2,1)S(1)}, bf16[4,96,1280]{2,1,0:T(8,128)(2,1)S(1)}, u32[]{:S(2)}, u32[]{:S(2)}) %collective-permute-start) | collective-permute-done | bytes 983072 | tf_op jit(solution)/shard_map/ppermute | solution.py:102
  154.6 0.0 collective-permute-done.2.near_full
  154.7 1.0 copy-done.8
  155.7 0.2 copy-done.10
  155.9 0.3 copy-done.9
  156.2 98.6 %backward.1 = (bf16[320,1280]{1,0:T(8,128)(2,1)}, bf16[320,1280]{1,0:T(8,128)(2,1)}, bf16[320,1280]{1,0:T(8,128)(2,1)}, bf16[4,40,768]{2,1,0:T(8,128)(2,1)}, bf1...) custom-call(f32[21,128]{1,0:T(8,128)} %bitcast.56, ...), custom_call_target="tpu_custom_call" | custom-call | tf_op jit(solution)/shard_map/backward/pallas_call | solution.py:1651
  254.8 8.6 %adam.1 = (f32[40,1024]{1,0:T(8,128)}, f32[40,256]{1,0:T(8,128)}, f32[40,256]{1,0:T(8,128)}, f32[32,1280]{1,0:T(8,128)}, f32[40,3072]{1,0:T(8,128)}, /*index=5*/...) custom-call(f32[8,128]{1,0:T(8,128)} %get-tuple-element.123.norm, ...), custom_call_target="tpu_custom_call" | custom-call | tf_op jit(solution)/shard_map/adam/pallas_call | solution.py:1814
  (29 shorter events, 0.1 us)
Async XLA Ops:
  119.1 5.3 %copy-start.1 = (bf16[2,4,4,40,768]{4,3,2,1,0:T(8,128)(2,1)S(1)}, bf16[2,4,4,40,768]{4,3,2,1,0:T(8,128)(2,1)}, u32[]{:S(2)}) copy-start(bf16[2,4,4,40,768]{4,3,2,1,0:T(8,128)(2,1)} %get-tuple-element.104.gate_w) | copy-start | bytes 5898244
  124.4 1.5 copy-start.16
  124.4 1.5 copy-start.14
  124.4 2.2 copy-start.3
  126.7 3.6 %copy-start = (bf16[768,1280]{1,0:T(8,128)(2,1)S(1)}, bf16[768,1280]{1,0:T(8,128)(2,1)}, u32[]{:S(2)}) copy-start(bf16[768,1280]{1,0:T(8,128)(2,1)} %get-tuple-element.107) | copy-start | bytes 5898244
  128.2 1.2 copy-start.6
  130.3 2.5 collective-permute-start.1
  130.3 3.6 %copy-start.13 = (f32[640,768]{1,0:T(8,128)S(1)}, f32[640,768]{1,0:T(8,128)}, u32[]{:S(2)}) copy-start(f32[640,768]{1,0:T(8,128)} %get-tuple-element.115) | copy-start | bytes 5898244
  130.4 2.5 copy-start.7
  130.4 24.2 %collective-permute-start = (bf16[4,96,1280]{2,1,0:T(8,128)(2,1)S(1)}, bf16[4,96,1280]{2,1,0:T(8,128)(2,1)S(1)}, u32[]{:S(2)}, u32[]{:S(2)}) collective-permute-start(bf16[4,96,1280]{2,1,0:T(8,128)(2,1)S(1)} %dynamic-slice_bitcast_fusion), channel_id=1, source_target_pairs={{0,16},{1,17},{2,18},{3,19},{4,20},{5,21},{6,22},{7,23},{8,24},{9,... | collective-permute-start | bytes 2949128 | tf_op jit(solution)/shard_map/ppermute | solution.py:102
  130.5 3.4 %copy-start.12 = (f32[640,768]{1,0:T(8,128)S(1)}, f32[640,768]{1,0:T(8,128)}, u32[]{:S(2)}) copy-start(f32[640,768]{1,0:T(8,128)} %get-tuple-element.116) | copy-start | bytes 5898244
  132.2 2.0 copy-start.5
  133.1 21.6 %collective-permute-start.3 = (bf16[320,1280]{1,0:T(8,128)(2,1)S(1)}, bf16[320,1280]{1,0:T(8,128)(2,1)S(1)}, u32[]{:S(2)}, u32[]{:S(2)}) collective-permute-start(bf16[320,1280]{1,0:T(8,128)(2,1)S(1)} %add_convert_fusion), channel_id=1, source_target_pairs={{0,8},{1,9},{2,10},{3,11},{4,12},{5,13},{6,14},{7,15},{8,0},{9,1},... | collective-permute-start | bytes 2457608 | tf_op jit(solution)/shard_map/ppermute | solution.py:102
  134.3 2.1 copy-start.2
  136.4 1.5 copy-start.4
  137.9 3.0 %copy-start.15 = (bf16[640,768]{1,0:T(8,128)(2,1)S(1)}, bf16[640,768]{1,0:T(8,128)(2,1)}, u32[]{:S(2)}) copy-start(bf16[640,768]{1,0:T(8,128)(2,1)} %copy-done.14) | copy-start | bytes 2949124
  139.4 2.2 copy-start.11
  140.4 5.2 %copy-start.17 = (bf16[640,768]{1,0:T(8,128)(2,1)S(1)}, bf16[640,768]{1,0:T(8,128)(2,1)}, u32[]{:S(2)}) copy-start(bf16[640,768]{1,0:T(8,128)(2,1)} %copy-done.16) | copy-start | bytes 2949124
  140.4 14.3 %collective-permute-start.2 = (bf16[320,1280]{1,0:T(8,128)(2,1)S(1)}, bf16[320,1280]{1,0:T(8,128)(2,1)S(1)}, u32[]{:S(2)}, u32[]{:S(2)}) collective-permute-start(bf16[320,1280]{1,0:T(8,128)(2,1)S(1)} %get-tuple-element.172), channel_id=1, source_target_pairs={{0,4},{1,5},{2,6},{3,7},{4,0},{5,1},{6,2},{7,3},{8,12},{9,13},{10,... | collective-permute-start | bytes 2457608 | tf_op jit(solution)/shard_map/ppermute | solution.py:102
  154.6 1.0 copy-start.8
  154.6 1.2 copy-start.10
  154.7 1.5 copy-start.9

commit v7 on v6

--- a/solution.py
+++ b/solution.py
@@ -209,21 +209,11 @@
         )
     ]
     start_all(loads)
-    for copy in loads:
-        copy.wait()
     column = 0
-    for weight in (w_query, w_key, w_value):
+    for index, weight in enumerate((w_query, w_key, w_value)):
+        loads[index].wait()
         in_ref[:, column : column + weight.shape[1]] = weight[...].astype(jnp.bfloat16)
         column += weight.shape[1]
-    out_ref[...] = w_out[...].astype(jnp.bfloat16)
-    span = inner_ref.shape[3] // outer
-    for half, weight in enumerate((w_gate, w_up)):
-        for k in range(MEMBERS):
-            for part in range(outer):
-                column = (part * MEMBERS + k) * span
-                inner_ref[half, k, :, part * span : (part + 1) * span] = weight[
-                    :, column : column + span
-                ].astype(jnp.bfloat16)
     pl.semaphore_wait(barrier, len(peers))
 
     def remote(source, target, send, recv, device):
@@ -245,13 +235,13 @@
         sent.append(copy)
         return copy
 
-    local = [
-        pltpu.make_async_copy(shards_here[a], wholes[a].at[y, x, c, z], local_sem.at[a])
-        for a in range(2)
-    ]
-    start_all(local)
+    local = []
     z_copies = {}
-    for a in range(2):
+
+    def start_shard(a):
+        kept = pltpu.make_async_copy(shards_here[a], wholes[a].at[y, x, c, z], local_sem.at[a])
+        kept.start()
+        local.append(kept)
         for step in range(1, nf):
             z_copies[a, step] = send(
                 remote(
@@ -262,6 +252,44 @@
                     z_peer(step),
                 )
             )
+
+    def block(a, step, oy=None, ox=None):
+        return wholes[a].at[y if oy is None else oy, x if ox is None else ox, c, from_z(step)]
+
+    y_copies = {}
+    x_copies = {}
+
+    def to_plane(a, step):
+        source = shards_here[a] if step == 0 else block(a, step)
+        for hop in range(1, outer):
+            y_copies[a, hop, step] = send(
+                remote(
+                    source,
+                    block(a, step),
+                    y_send.at[a, hop, step],
+                    y_recv.at[a, hop, step],
+                    y_peer(hop),
+                )
+            )
+        x_copies[a, step] = send(
+            remote(source, block(a, step), x_send.at[a, step], x_recv.at[a, step], x_peer)
+        )
+
+    start_shard(0)
+    to_plane(0, 0)
+    loads[3].wait()
+    out_ref[...] = w_out[...].astype(jnp.bfloat16)
+    start_shard(1)
+    to_plane(1, 0)
+    span = inner_ref.shape[3] // outer
+    for half, weight in enumerate((w_gate, w_up)):
+        loads[4 + half].wait()
+        for k in range(MEMBERS):
+            for part in range(outer):
+                column = (part * MEMBERS + k) * span
+                inner_ref[half, k, :, part * span : (part + 1) * span] = weight[
+                    :, column : column + span
+                ].astype(jnp.bfloat16)
     masks = (2, 1, 3)
     trades = {}
     for half, target in ((0, gate_w.at[y, :, z]), (1, upper_w.at[y, :, z])):
@@ -282,31 +310,10 @@
         kept.start()
         local.append(kept)
 
-    def block(a, step, oy=None, ox=None):
-        return wholes[a].at[y if oy is None else oy, x if ox is None else ox, c, from_z(step)]
-
-    y_copies = {}
-    x_copies = {}
     for a in range(2):
-        for step in range(nf):
-            if step:
-                z_copies[a, step].wait_recv()
-            source = shards_here[a] if step == 0 else block(a, step)
-            for hop in range(1, outer):
-                y_copies[a, hop, step] = send(
-                    remote(
-                        source,
-                        block(a, step),
-                        y_send.at[a, hop, step],
-                        y_recv.at[a, hop, step],
-                        y_peer(hop),
-                    )
-                )
-            x_copies[a, step] = send(
-                remote(
-                    source, block(a, step), x_send.at[a, step], x_recv.at[a, step], x_peer
-                )
-            )
+        for step in range(1, nf):
+            z_copies[a, step].wait_recv()
+            to_plane(a, step)
     for mask in masks:
         trades[0, mask].wait_recv()
     local[2].wait()
@@ -552,7 +559,8 @@
     gate_w,
     upper_w,
     down_w,
-    back_all,
+    back_near,
+    back_far,
     ffn_all,
     gate_near,
     upper_near,
@@ -638,9 +646,6 @@
         copy = pltpu.make_async_copy(source, target, local_sem.at[4 + index])
         copy.start()
         weights_here.append(copy)
-    for _ in range(2):
-        weights_here.pop(0).wait()
-    down_x[...] = w_down[...].astype(jnp.bfloat16)
     pl.semaphore_wait(barrier, len(peers))
     sent = []
 
@@ -682,6 +687,9 @@
 
     for step in [0] + early_steps(nf):
         upper_to_y(step)
+    for _ in range(2):
+        weights_here.pop(0).wait()
+    down_x[...] = w_down[...].astype(jnp.bfloat16)
     down_z = [
         remote(down_x, down_own, dz_send.at[step], dz_recv.at[step], z_peer(step))
         for step in range(1, nf)
@@ -892,7 +900,9 @@
             kept.append(keep(9 + 3 * far + index, source.at[rows], targets[index]))
     cot_near.wait_recv()
     cot_cross.wait_recv()
-    kept.append(keep(3, cot, back_all))
+    for far, target in enumerate((back_near, back_far)):
+        rows = pl.ds(far * 2 * count, 2 * count)
+        kept.append(keep(15 if far else 3, cot.at[rows], target))
     outer_product(hidden_here, cot, down_terms)
     for copy in arrivals:
         copy.wait_recv()
@@ -912,7 +922,8 @@
     shapes = [
         (upper_w.shape, lo),
         ((outer, nf) + w_down.shape, lo),
-        ((MEMBERS * count, width), lo),
+        ((2 * count, width), lo),
+        ((2 * count, width), lo),
         ((MEMBERS * count, width), lo),
         *[((2 * count, mine), kind) for kind in (hi, hi, lo)] * 2,
         ((mine, width), lo),
@@ -931,7 +942,7 @@
         name="attend",
         out_shape=tuple(jax.ShapeDtypeStruct(*item) for item in shapes),
         in_specs=[ON_CHIP] * 4 + [ANYWHERE] * 7,
-        out_specs=(ANYWHERE,) * 10 + (ON_CHIP,) * 6,
+        out_specs=(ANYWHERE,) * 11 + (ON_CHIP,) * 6,
         input_output_aliases={9: 0},
         scratch_shapes=[pltpu.VMEM(shape, lo) for shape in early]
         + [pltpu.VMEM(w_down.shape, hi)]
@@ -939,11 +950,15 @@
         + [pltpu.VMEM((nf_rows, mine), hi), pltpu.VMEM(flat, lo), pltpu.VMEM(flat, lo)]
         + [pltpu.VMEM((MEMBERS * count, mine), kind) for kind in (hi, hi, lo)]
         + [dma(shape) for shape in moves for _ in range(2)]
-        + [dma((15,))],
+        + [dma((16,))],
         compiler_params=pltpu.CompilerParams(
             collective_id=2, has_side_effects=True, vmem_limit_bytes=VMEM_MOST
         ),
     )(*small, tokens, w_down, in_w, out_w, cot, upper_w, gate_w)
+
+
+def ahead_steps(nf):
+    return list(range(1, nf))
 
 
 def backward_kernel(
@@ -1154,16 +1169,21 @@
             return terms[0].at[place, z_to(step)]
         return terms[matrix].at[place, :, z_to(step)]
 
-    order = [(matrix, step) for matrix in range(3) for step in list(range(1, nf)) + [0]]
+    ahead = ahead_steps(nf)
+    steps = list(range(1, nf)) + [0]
+    order = [(0, step) for step in ahead] + [(1, step) for step in steps]
+    order += [(0, step) for step in steps if step not in ahead] + [(2, step) for step in steps]
     y_copies, loads = {}, {}
     for matrix, step in order:
         loads[matrix, step] = keep(
             load_sem.at[matrix, step], piece_of(matrix, y, step), owns[matrix].at[step]
         )
         for hop in range(1, outer):
-            if matrix == 0:
+            if matrix == 0 and step in ahead:
                 y_copies[0, step, hop] = keep(
-                    got_sem.at[hop, step], down_got.at[hop - 1, z_to(step)], down_y.at[hop - 1, step]
+                    got_sem.at[hop, step],
+                    down_got.at[hop - 1, ahead.index(step)],
+                    down_y.at[hop - 1, step],
                 )
                 continue
             y_copies[matrix, step, hop] = remote(
@@ -1182,10 +1202,10 @@
             loads[matrix, step].wait()
             total = owns[matrix][step].astype(hi)
             for hop in range(1, outer):
-                if matrix:
+                if matrix == 0 and step in ahead:
+                    y_copies[0, step, hop].wait()
+                else:
                     y_copies[matrix, step, hop].wait_recv()
-                else:
-                    y_copies[0, step, hop].wait()
                 total = total + over_y[matrix][hop - 1, step].astype(hi)
             owns[matrix][step] = total.astype(lo)
             if step:
@@ -1282,7 +1302,7 @@
     sum_attn[...] = jnp.zeros_like(sum_attn)
     sum_ffn[...] = jnp.zeros_like(sum_ffn)
     sum_heads[...] = jnp.zeros_like(sum_heads)
-    pieces(nf)
+    pieces(len(ahead))
     ready(5)
 
     def norm_back(part, gain, grad):
@@ -1478,7 +1498,7 @@
         attend_back(row)
         if row == 0:
             core_in(1)
-        pieces(1)
+        pieces(1 if row else 2)
     averages = block_mean()
 
     def turn_back(index, carry):
@@ -1528,6 +1548,7 @@
     out_far_copy.wait_recv()
     add_rows(out_far, out_core_far)
     out_x_copy = remote(out_far.at[here], out_x, row_send.at[2], row_recv.at[2], x_peer)
+    pieces(2)
     lax.fori_loop(0, width // pair, normed_back, 0)
 
     def attn_norm_back(index, carry):
@@ -1921,7 +1942,8 @@
     (
         upper_w,
         down_w,
-        back_all,
+        back_near,
+        back_far,
         ffn_all,
         gate_near,
         upper_near,
@@ -1950,15 +1972,18 @@
         return grad_gate, grad_upper, low(back)
 
     down_terms = down_terms.reshape(outer, nf, hidden_rows, width)
-    down_sent = [pick(down_terms, 0, ring_y.dest(hop)) for hop in range(1, outer)]
-    down_got = jnp.stack([ring_y.move(part, hop + 1) for hop, part in enumerate(down_sent)])
-    half = 2 * count
-    far_gate, far_upper, far_ffn = inner_grads(back_all[half:], gate_far, upper_far)
+    down_got = []
+    for hop in range(1, outer):
+        parts = pick(down_terms, 0, ring_y.dest(hop))
+        parts = jnp.stack([pick(parts, 0, ring_z.dest(step)) for step in ahead_steps(nf)])
+        down_got.append(ring_y.move(parts, hop))
+    down_got = jnp.stack(down_got)
+    far_gate, far_upper, far_ffn = inner_grads(back_far, gate_far, upper_far)
     far = far_ffn[:count].astype(jnp.float32) + ring_core.move(far_ffn[count:], 1)
     far = low(far)
     ffn_x = ring_x.move(far, 1)
     near_gate, near_upper, near_ffn = inner_grads(
-        after(back_all[:half], far), gate_near, upper_near
+        after(back_near, far), gate_near, upper_near
     )
     ffn_core = ring_core.move(near_ffn[count:], 1)
     ffn_all = after(ffn_all, near_ffn)

time: 264 us -> 261 us (0.989)
  transfers between devices with their start and end apart: 4 -> 4, of which waited for: 2 -> 2; matrix products, arithmetic and copies ran while one was open for 6% -> 7% of each run, Pallas kernels for 0% -> 0%
where the time goes in v7:
time: 261 us
  Pallas kernels  225 us (86%)
  matrix products  23.3 us (9%)
  local copies, waits for them, and re-layouts  6.97 us (3%)
  waiting for transfers between devices  3.14 us (1%)
    pallas_call x1, Pallas kernels, backward(): pl.pallas_call(functools.partial(backward_kernel, nd, nf, length), name='...  97.5 us
    pallas_call x1, Pallas kernels, attend(): pl.pallas_call(functools.partial(attend_kernel, nd, nf, length), name='at...  62.9 us
    pallas_call x1, Pallas kernels, gather_weights(): pl.pallas_call(functools.partial(weights_kernel, nd, nf), name='gather_we...  55.4 us
    dot_general x6, matrix products, back_product(): lax.dot_general(left, right, (((1,), (1,)), ((), ())), preferred_element_...  15.2 us
    pallas_call x1, Pallas kernels, adam(): pl.pallas_call(functools.partial(adam_kernel, span), name='adam', out_sha...  8.67 us
    dot_general x2, matrix products, weight_product(): lax.dot_general(left, right, (((0,), (0,)), ((), ())), preferred_element_...  8.08 us
  transfers between devices with their start and end apart: 4, of which 2 were waited for; matrix products, arithmetic and copies ran while one was open for 7% of the time, Pallas kernels for 0%

profile of v7, /device:TPU:0, one launch (start us, length us, event | category | flops | bytes accessed | tf_op | source)
XLA Modules:
  0.0 260.7 jit_solution(17633704287932489271)
XLA Ops:
  0.7 55.4 %gather_weights.1 = (bf16[2,2,2,4,40,1536]{5,4,3,2,1,0:T(8,128)(2,1)}, bf16[2,2,2,4,32,1280]{5,4,3,2,1,0:T(8,128)(2,1)}, bf16[2,4,4,40,768]{4,3,2,1,0:T(8,128)(2,1)}, bf16[2,4,4,40,768]{4,3,2,1,0:T(8,128)(2,1)}) custom-call(f32[40,1024]{1,0:T(8,128)} %rest_5_.1, f32[40,256]{1,0:T(8,128)} %rest_6_.1, f32[40,256]{1,0:T(8,128)} %rest_7_.1, f32[32,1280]{1,0:T(8,128)} %rest_8_.1, ...), custom_call_target="tpu_custom_call" | custom-call | tf_op jit(solution)/shard_map/gather_weights/pallas_call | solution.py:415
  56.1 62.9 %attend.1 = (bf16[2,4,4,40,768]{4,3,2,1,0:T(8,128)(2,1)}, bf16[2,4,96,1280]{3,2,1,0:T(8,128)(2,1)}, bf16[640,1280]{1,0:T(8,128)(2,1)}, bf16[640,1280]{1,0:T(8,12...) custom-call(f32[21,128]{1,0:T(8,128)} %bitcast.60, ...), custom_call_target="tpu_custom_call", output_to_operand_aliasing={{0}: (9, {})} | custom-call | tf_op jit(solution)/shard_map/attend/pallas_call | solution.py:940
  119.1 5.3 %multiply_convert_fusion.1 = (bf16[640,768]{1,0:T(8,128)(2,1)S(1)}, bf16[640,768]{1,0:T(8,128)(2,1)S(1)}) fusion(f32[640,768]{1,0:T(8,128)} %get-tuple-element.114, f32[640,768]{1,0:T(8,128)} %get-tuple-element.113, bf16[640,1280]{1,0:T(8,128)(2,1)} %get-tuple-element.111, bf16[768,1280]{1,0:T(8,128)(2,1)} %bitcast.50), kind=kOutput, calls=%fused_computation.22 | convolution fusion | flops 1265172480 | bytes 9502720 | tf_op jit(solution)/shard_map/dot_general | solution.py:66
  124.4 0.0 copy-start.13
  124.4 1.5 fusion.17
  125.9 0.7 copy-done.2
  126.6 1.5 fusion
  128.1 1.2 copy-done.4
  129.3 0.9 slice.17
  130.2 0.0 collective-permute-start.1
  130.3 1.4 dynamic-slice_bitcast_fusion.2
  131.6 0.1 pad_maximum_fusion
  131.7 0.1 collective-permute-start
  131.8 1.0 collective-permute-done.1
  132.8 0.2 add_convert_fusion
  133.0 0.8 collective-permute-start.3
  133.8 4.1 %multiply_convert_fusion = (bf16[640,768]{1,0:T(8,128)(2,1)S(1)}, bf16[640,768]{1,0:T(8,128)(2,1)S(1)}) fusion(f32[640,768]{1,0:T(8,128)} %get-tuple-element.118, f32[640,768]{1,0:T(8,128)} %get-tuple-element.117, bf16[640,1280]{1,0:T(8,128)(2,1)S(1)} %copy-done.10, bf16[768,1280]{1,0:T(8,128)(2,1)S(1)} %bitcast.52), kind=kOutput, calls=%fused_computation.20 | convolution fusion | flops 1265172480 | bytes 9502720 | tf_op jit(solution)/shard_map/dot_general | solution.py:66
  137.9 1.5 fusion.18
  139.4 0.1 copy-done.3
  139.4 1.5 fusion.1
  140.9 1.0 fusion.16
  141.9 0.5 collective-permute-start.2
  142.4 0.7 copy-done.9
  143.1 4.0 %convolution_convert_fusion = bf16[1280,768]{1,0:T(8,128)(2,1)} fusion(bf16[1280,1280]{1,0:T(8,128)(2,1)S(1)} %copy-done.9, bf16[640,768]{1,0:T(8,128)(2,1)S(1)} %copy-done.12, bf16[640,768]{1,0:T(8,128)(2,1)S(1)} %get-tuple-element.170), kind=kOutput, calls=%fused_computation.2 | convolution fusion | flops 2521497600 | bytes 7208960 | tf_op jit(solution)/shard_map/dot_general | solution.py:60
  147.2 4.0 %convolution_convert_fusion.1 = bf16[1280,768]{1,0:T(8,128)(2,1)} fusion(bf16[1280,1280]{1,0:T(8,128)(2,1)S(1)} %copy-done.9, bf16[640,768]{1,0:T(8,128)(2,1)S(1)} %copy-done.14, bf16[640,768]{1,0:T(8,128)(2,1)S(1)} %get-tuple-element.171), kind=kOutput, calls=%fused_computation.3 | convolution fusion | flops 2521497600 | bytes 7208960 | tf_op jit(solution)/shard_map/dot_general | solution.py:60
  151.2 0.0 collective-permute-done
  151.2 0.0 collective-permute-done.2.near_full
  151.2 0.0 copy-start.7
  151.2 2.1 collective-permute-done.3.far_full
  153.4 0.9 copy-done.6
  154.3 97.5 %backward.1 = (bf16[320,1280]{1,0:T(8,128)(2,1)}, bf16[320,1280]{1,0:T(8,128)(2,1)}, bf16[320,1280]{1,0:T(8,128)(2,1)}, bf16[4,40,768]{2,1,0:T(8,128)(2,1)}, bf1...) custom-call(f32[21,128]{1,0:T(8,128)} %bitcast.61, ...), custom_call_target="tpu_custom_call" | custom-call | tf_op jit(solution)/shard_map/backward/pallas_call | solution.py:1672
  251.8 8.7 %adam.1 = (f32[40,1024]{1,0:T(8,128)}, f32[40,256]{1,0:T(8,128)}, f32[40,256]{1,0:T(8,128)}, f32[32,1280]{1,0:T(8,128)}, f32[40,3072]{1,0:T(8,128)}, /*index=5*/...) custom-call(f32[8,128]{1,0:T(8,128)} %get-tuple-element.125.norm, ...), custom_call_target="tpu_custom_call" | custom-call | tf_op jit(solution)/shard_map/adam/pallas_call | solution.py:1835
  (23 shorter events, 0.0 us)
Async XLA Ops:
  119.1 5.3 %copy-start.1 = (bf16[2,4,4,40,768]{4,3,2,1,0:T(8,128)(2,1)S(1)}, bf16[2,4,4,40,768]{4,3,2,1,0:T(8,128)(2,1)}, u32[]{:S(2)}) copy-start(bf16[2,4,4,40,768]{4,3,2,1,0:T(8,128)(2,1)} %get-tuple-element.105.gate_w) | copy-start | bytes 5898244
  124.4 1.5 copy-start.13
  124.4 1.5 copy-start.11
  124.4 2.2 copy-start.2
  128.1 1.2 copy-start.4
  130.2 2.5 collective-permute-start.1
  130.3 2.5 copy-start.5
  131.6 2.2 copy-start
  131.6 2.2 copy-start.10
  131.7 19.5 %collective-permute-start = (bf16[3,96,1280]{2,1,0:T(8,128)(2,1)S(1)}, bf16[3,96,1280]{2,1,0:T(8,128)(2,1)S(1)}, u32[]{:S(2)}, u32[]{:S(2)}) collective-permute-start(bf16[3,96,1280]{2,1,0:T(8,128)(2,1)S(1)} %pad_maximum_fusion), channel_id=1, source_target_pairs={{0,16},{1,17},{2,18},{3,19},{4,20},{5,21},{6,22},{7,23},{8,24},{9,... | collective-permute-start | bytes 2211848 | tf_op jit(solution)/shard_map/ppermute | solution.py:102
  133.0 20.4 %collective-permute-start.3 = (bf16[320,1280]{1,0:T(8,128)(2,1)S(1)}, bf16[320,1280]{1,0:T(8,128)(2,1)S(1)}, u32[]{:S(2)}, u32[]{:S(2)}) collective-permute-start(bf16[320,1280]{1,0:T(8,128)(2,1)S(1)} %add_convert_fusion), channel_id=1, source_target_pairs={{0,8},{1,9},{2,10},{3,11},{4,12},{5,13},{6,14},{7,15},{8,0},{9,1},... | collective-permute-start | bytes 2457608 | tf_op jit(solution)/shard_map/ppermute | solution.py:102
  137.9 1.5 copy-start.3
  139.4 3.0 %copy-start.12 = (bf16[640,768]{1,0:T(8,128)(2,1)S(1)}, bf16[640,768]{1,0:T(8,128)(2,1)}, u32[]{:S(2)}) copy-start(bf16[640,768]{1,0:T(8,128)(2,1)} %copy-done.11) | copy-start | bytes 2949124
  140.9 2.2 copy-start.9
  141.9 5.2 %copy-start.14 = (bf16[640,768]{1,0:T(8,128)(2,1)S(1)}, bf16[640,768]{1,0:T(8,128)(2,1)}, u32[]{:S(2)}) copy-start(bf16[640,768]{1,0:T(8,128)(2,1)} %copy-done.13) | copy-start | bytes 2949124
  141.9 9.3 %collective-permute-start.2 = (bf16[320,1280]{1,0:T(8,128)(2,1)S(1)}, bf16[320,1280]{1,0:T(8,128)(2,1)S(1)}, u32[]{:S(2)}, u32[]{:S(2)}) collective-permute-start(bf16[320,1280]{1,0:T(8,128)(2,1)S(1)} %get-tuple-element.177), channel_id=1, source_target_pairs={{0,4},{1,5},{2,6},{3,7},{4,0},{5,1},{6,2},{7,3},{8,12},{9,13},{10,... | collective-permute-start | bytes 2457608 | tf_op jit(solution)/shard_map/ppermute | solution.py:102
  151.2 2.2 copy-start.8
  151.2 2.2 copy-start.7
  153.4 0.9 copy-start.6
